TPU v7x, 32 devices: a whole 2x2x4 slice. The times are simulated.
32 devices in a mesh: dp: 8 (over z, y), mp: 4 (over x, core).
Axes of the slice: x: 2, y: 2, z: 4, core: 2. Of those that a mesh axis runs over, the one named last changes fastest.
Arguments:
- roll_x: bfloat16 [256, 16, 8192], P('dp', None, 'mp'), may hold values from -6 to 6
- lengths: int32 [256], P('dp'), may hold values from 1 to 16, as said below
- dest: int32 [256], P('dp'), may hold values from 0 to 7, as said below
- offsets: int32 [256], P('dp'), may hold values from 0 to 496, as said below
- queries: bfloat16 [4096, 4096], P('dp', 'mp'), may hold values from -240 to 240
- out_grad: bfloat16 [4096, 4096], P('dp', 'mp'), may hold values from -6 to 6
- w_key: bfloat16 [8192, 512], P('mp'), may hold values from -0.0625 to 0.0625
- w_value: bfloat16 [8192, 512], P('mp'), may hold values from -0.0625 to 0.0625
Outputs:
- attn_out: bfloat16 [4096, 4096], P('dp', 'mp')
- grad_x: bfloat16 [4096, 8192], P('dp', 'mp')
- grad_wk: float32 [8192, 512], P(('mp', 'dp'))
- grad_wv: float32 [8192, 512], P(('mp', 'dp'))
Inputs may be any that keep to these rules, and one draw needn't show every extreme that they name: `lengths`: each sample has at least one token; some sample has 16. `dest`: every learner receives exactly 32 samples; one index of dp sends at most 4 samples to one learner, and exactly 4 to some. The samples of one learner occupy disjoint rows offsets[s] to offsets[s] + lengths[s] - 1 within its 512 rows; some sample starts at row 496.
All inputs are finite; a program needn't handle non-finite values.
Results may differ from a plain program's by a relative error of at most 0.029.
The roundings to bfloat16 on the way count: a program that leaves them out, or rounds other values in their place, can miss the bound.
Values may be sent and summed in bfloat16 or wider, within the bound.
No kernel may reach another device: no remote copies, remote signals or barrier semaphores. Data moves between devices by JAX's collectives and lax.ppermute only.
A program may use at most 128 MiB of HBM per device.

v0:
```python
import jax
import jax.numpy as jnp
from jax import lax
from jax.sharding import PartitionSpec as P

HEAD_DIM = 128


def attend(qs, ks, vs, grads, mask):
    scale = 1.0 / qs.shape[-1] ** 0.5
    scores = jnp.einsum("bqkge,bmke->bkgqm", qs, ks, preferred_element_type=jnp.float32) * scale
    allowed = mask[:, None, None, :, :]
    scores = jnp.where(allowed, scores, -1e30)
    top = jnp.max(scores, axis=-1, keepdims=True)
    expo = jnp.exp(scores - top)
    total = jnp.sum(expo, axis=-1, keepdims=True)
    probs = jnp.where(allowed, expo / total, 0.0)
    probs_b = probs.astype(jnp.bfloat16)
    out = jnp.einsum("bkgqm,bmke->bqkge", probs_b, vs, preferred_element_type=jnp.float32).astype(
        jnp.bfloat16
    )
    dprob = jnp.einsum("bqkge,bmke->bkgqm", grads, vs, preferred_element_type=jnp.float32)
    delta = jnp.einsum("bqkge,bqkge->bkgq", grads, out, preferred_element_type=jnp.float32)
    dscore = probs * (dprob - delta[..., None])
    dscore_b = dscore.astype(jnp.bfloat16)
    key_grad = (
        jnp.einsum("bkgqm,bqkge->bmke", dscore_b, qs, preferred_element_type=jnp.float32) * scale
    ).astype(jnp.bfloat16)
    val_grad = jnp.einsum(
        "bkgqm,bqkge->bmke", probs_b, grads, preferred_element_type=jnp.float32
    ).astype(jnp.bfloat16)
    return (out, key_grad, val_grad)


def input_grads(key_all, val_all, w_key, w_value):
    contract = (((1,), (1,)), ((), ()))
    total = lax.dot_general(key_all, w_key, contract, preferred_element_type=jnp.float32)
    total = total + lax.dot_general(val_all, w_value, contract, preferred_element_type=jnp.float32)
    return total.astype(jnp.bfloat16)


def local(roll_x, lengths, dest, offsets, queries, out_grad, w_key, w_value):
    learners = lax.axis_size("dp")
    samp, lmax, feats = roll_x.shape
    rows = queries.shape[0]
    slots_per = (samp + learners - 1) // learners
    slot_count = learners * slots_per
    order = jnp.arange(samp, dtype=jnp.int32)
    earlier = (dest[None, :] == dest[:, None]) & (order[None, :] < order[:, None])
    rank = jnp.sum(earlier.astype(jnp.int32), axis=1)
    slot = dest * slots_per + rank
    match = slot[None, :] == jnp.arange(slot_count, dtype=jnp.int32)[:, None]
    filled = jnp.any(match, axis=1)
    pick = jnp.sum(jnp.where(match, order[None, :], 0), axis=1)
    send_x = jnp.where(
        filled[:, None, None], jnp.take(roll_x, pick, axis=0), jnp.zeros((), jnp.bfloat16)
    )
    send_len = jnp.where(filled, jnp.take(lengths, pick), 0)
    send_off = jnp.where(filled, jnp.take(offsets, pick), 0)
    recv_x, recv_len, recv_off = (
        lax.all_to_all(send_x, "dp", split_axis=0, concat_axis=0, tiled=True),
        lax.all_to_all(send_len, "dp", split_axis=0, concat_axis=0, tiled=True),
        lax.all_to_all(send_off, "dp", split_axis=0, concat_axis=0, tiled=True),
    )
    position = jnp.arange(lmax, dtype=jnp.int32)
    live = position[None, :] < recv_len[:, None]
    target = jnp.where(live, recv_off[:, None] + position[None, :], rows).astype(jnp.int32)
    flat = target.reshape(-1)
    packed = (
        jnp.zeros((rows, feats), jnp.bfloat16).at[flat].set(recv_x.reshape(-1, feats), mode="drop")
    )
    part_k = jnp.dot(packed, w_key, preferred_element_type=jnp.float32)
    part_v = jnp.dot(packed, w_value, preferred_element_type=jnp.float32)
    key_mine, val_mine = (
        lax.psum_scatter(part_k, "mp", scatter_dimension=1, tiled=True),
        lax.psum_scatter(part_v, "mp", scatter_dimension=1, tiled=True),
    )
    keys = key_mine.astype(jnp.bfloat16)
    vals = val_mine.astype(jnp.bfloat16)
    local_heads = keys.shape[1] // HEAD_DIM
    q_cols = queries.shape[1]
    group = q_cols // (local_heads * HEAD_DIM)
    slot_ids = jnp.broadcast_to(
        jnp.arange(slot_count, dtype=jnp.int32)[:, None], (slot_count, lmax)
    )
    seg = jnp.full((rows,), -1, jnp.int32).at[flat].set(slot_ids.reshape(-1), mode="drop")
    rowpos = jnp.arange(rows, dtype=jnp.int32)
    mask = (
        (seg[:, None] == seg[None, :]) & (seg[:, None] >= 0) & (rowpos[None, :] <= rowpos[:, None])
    )
    out, key_grad, val_grad = attend(
        queries.reshape(1, rows, local_heads, group, HEAD_DIM),
        keys.reshape(1, rows, local_heads, HEAD_DIM),
        vals.reshape(1, rows, local_heads, HEAD_DIM),
        out_grad.reshape(1, rows, local_heads, group, HEAD_DIM),
        mask[None],
    )
    attn_out = out.reshape(rows, q_cols)
    key_grad = key_grad.reshape(rows, local_heads * HEAD_DIM)
    val_grad = val_grad.reshape(rows, local_heads * HEAD_DIM)
    key_all, val_all = (
        lax.all_gather(key_grad, "mp", axis=1, tiled=True),
        lax.all_gather(val_grad, "mp", axis=1, tiled=True),
    )
    grad_x = input_grads(key_all, val_all, w_key, w_value)
    contract = (((0,), (0,)), ((), ()))
    whole_k = lax.dot_general(packed, key_all, contract, preferred_element_type=jnp.float32)
    whole_v = lax.dot_general(packed, val_all, contract, preferred_element_type=jnp.float32)
    sum_k, sum_v = (
        lax.psum_scatter(whole_k, "dp", scatter_dimension=0, tiled=True),
        lax.psum_scatter(whole_v, "dp", scatter_dimension=0, tiled=True),
    )
    return (attn_out, grad_x, sum_k / learners, sum_v / learners)


def solution(mesh):
    return jax.shard_map(
        local,
        mesh=mesh,
        in_specs=(
            P("dp", None, "mp"),
            P("dp"),
            P("dp"),
            P("dp"),
            P("dp", "mp"),
            P("dp", "mp"),
            P("mp", None),
            P("mp", None),
        ),
        out_specs=(P("dp", "mp"), P("dp", "mp"), P(("mp", "dp"), None), P(("mp", "dp"), None)),
        check_vma=False,
    )
```

profile of v0, /device:TPU:0, one launch (start us, length us, event | category | flops | bytes accessed | tf_op | source)
XLA Modules:
  0.0 371.3 jit_solution(11747425738382235603)
XLA Ops:
  12.5 7.3 %all-to-all-start.1 = ((s32[8,4,1]{1,2,0:T(1,128)}), s32[8,4,1]{1,2,0:T(1,128)S(1)}, u32[]{:S(2)}, u32[]{:S(2)}) async-start(s32[8,4,1]{1,2,0:T(1,128)} %bitcast.3), calls=%async_computation.1 | async-start | bytes 8192 | tf_op jit(solution)/shard_map/all_to_all | solution.py:63
  20.5 3.6 gather_fusion
  24.1 2.1 all-to-all-done.1
  26.2 3.9 %all-to-all-start = ((s32[8,4,1]{1,2,0:T(1,128)}), s32[8,4,1]{1,2,0:T(1,128)S(1)}, u32[]{:S(2)}, u32[]{:S(2)}) async-start(s32[8,4,1]{1,2,0:T(1,128)} %bitcast.2), calls=%async_computation | async-start | bytes 8192 | tf_op jit(solution)/shard_map/all_to_all | solution.py:62
  30.1 3.2 select_select_fusion
  33.3 3.1 all-to-all-done
  36.5 4.3 %all-to-all-start.2 = ((bf16[32,16,2048]{2,1,0:T(8,128)(2,1)}), bf16[32,16,2048]{2,1,0:T(8,128)(2,1)}, u32[]{:S(2)}, u32[]{:S(2)}) async-start(bf16[32,16,2048]{2,1,0:T(8,128)(2,1)} %select_select_fusion), calls=%async_computation.2 | async-start | bytes 4194304 | tf_op jit(solution)/shard_map/all_to_all | solution.py:61
  43.0 44.4 %all-to-all-done.2 = bf16[32,16,2048]{2,1,0:T(8,128)(2,1)} async-done(((bf16[32,16,2048]{2,1,0:T(8,128)(2,1)}), bf16[32,16,2048]{2,1,0:T(8,128)(2,1)}, u32[]{:S(2)}, u32[]{:S(2)}) %all-to-all-start.2) | async-done | bytes 2097184 | tf_op jit(solution)/shard_map/all_to_all | solution.py:61
  87.5 6.1 %scatter_custom_fusion = bf16[512,2048]{1,0:T(8,128)(2,1)} fusion(s32[512]{0:T(512)S(1)} %bitcast.189, bf16[512,2048]{1,0:T(8,128)(2,1)} %bitcast.7, bf16[]{:T(256)} %constant.12.clone.1), kind=kCustom, calls=%fused_computation.40 | custom fusion | bytes 2097664 | tf_op jit(solution)/shard_map/scatter | solution.py:70
  93.6 3.8 %fusion.79 = f32[512,512]{1,0:T(8,128)} fusion(bf16[512,2048]{1,0:T(8,128)(2,1)} %scatter_custom_fusion, bf16[2048,512]{1,0:T(8,128)(2,1)S(1)} %copy-done), kind=kOutput, calls=%fused_computation.87 | convolution fusion | flops 1073741824 | bytes 5242880 | tf_op jit(solution)/shard_map/dot_general | solution.py:72
  97.5 4.5 %fusion.78 = f32[512,512]{1,0:T(8,128)} fusion(bf16[512,2048]{1,0:T(8,128)(2,1)} %scatter_custom_fusion, bf16[2048,512]{1,0:T(8,128)(2,1)} %param.17), kind=kOutput, calls=%fused_computation.86 | convolution fusion | flops 1073741824 | bytes 5242880 | tf_op jit(solution)/shard_map/dot_general | solution.py:73
  103.7 2.6 scatter_custom_fusion.1
  106.6 14.7 %reduce-scatter.7.cloned.1.call-done = f32[512,128]{1,0:T(8,128)} async-done(((f32[512,512]{1,0:T(8,128)}), f32[512,128]{1,0:T(8,128)}) %reduce-scatter.7.cloned.1.call-update) | async-done | bytes 262160 | tf_op jit(solution)/shard_map/reduce_scatter | solution.py:75
  121.3 2.9 fusion.3
  124.3 3.2 copy-done.1
  127.5 1.8 fusion.2
  129.2 19.7 %reduce-scatter.5.cloned.1.call-done = f32[512,128]{1,0:T(8,128)} async-done(((f32[512,512]{1,0:T(8,128)}), f32[512,128]{1,0:T(8,128)}) %reduce-scatter.5.cloned.1.call-update) | async-done | bytes 262160 | tf_op jit(solution)/shard_map/reduce_scatter | solution.py:76
  148.9 7.9 %bitcast_convert_fusion = (f32[8,512,128]{1,2,0:T(8,128)}, bf16[128,8,512]{2,0,1:T(8,128)(2,1)}) fusion(f32[8,512]{1,0:T(8,128)S(1)} %fusion.2, f32[8,512]{1,0:T(8,128)S(1)} %get-tuple-element.23, f32[512,512,8]{1,0,2:T(8,128)} %copy-done.1, pred[512,512]{0,1:T(8,128)(4,1)S(1)} %fusion.47, f32[512,128]{1,0:T(8,128)} %reduce-scatter.5.cloned.1.call-done), kind=kOutput, calls=%fused_computation.38 | convolution fusion | flops 550567936 | bytes 12091392 | tf_op jit(solution)/shard_map/bkgqm,bmke->bqkge/dot_general | solution.py:19
  156.8 2.9 copy.51
  159.7 2.9 multiply_reduce_fusion
  163.7 7.3 %fusion.36 = bf16[1,512,1,128]{3,1,2,0:T(8,128)(2,1)S(1)} fusion(f32[8,512]{1,0:T(8,128)S(1)} %copy.52, f32[8,512]{1,0:T(8,128)S(1)} %fusion.2, f32[8,512]{1,0:T(8,128)S(1)} %get-tuple-element.23, f32[512,512,8]{1,0,2:T(8,128)} %copy-done.1, pred[512,512]{0,1:T(8,128)(4,1)S(1)} %fusion.47, f32[512,128]{1,0:T(8,128)} %reduce-scatter.5.cloned.1.call-done, ...), kind=kOutput, calls=%fused_computation.32 | convolution fusion | flops 1090715648 | bytes 11190272 | tf_op jit(solution)/shard_map/bkgqm,bqkge->bmke/dot_general | solution.py:27
  171.0 6.8 %all-gather = bf16[1,512,1,512]{3,1,2,0:T(8,128)(2,1)S(1)} all-gather(bf16[1,512,1,128]{3,1,2,0:T(8,128)(2,1)S(1)} %fusion.36), channel_id=2, replica_groups=mesh['dp'=8,'mp'=4] {'mp'}, dimensions={3}, use_global_device_ids=true | all-gather | bytes 655360 | tf_op jit(solution)/shard_map/all_gather | solution.py:102
  177.8 4.9 %fusion.56 = f32[2048,512]{1,0:T(8,128)} fusion(bf16[512,2048]{1,0:T(8,128)(2,1)} %scatter_custom_fusion, bf16[1,512,1,512]{3,1,2,0:T(8,128)(2,1)S(1)} %all-gather), kind=kOutput, calls=%fused_computation.50 | convolution fusion | flops 1073741824 | bytes 6815744 | tf_op jit(solution)/shard_map/dot_general | solution.py:107
  183.0 6.0 %fusion.33 = bf16[1,512,1,128]{3,1,2,0:T(8,128)(2,1)S(1)} fusion(f32[8,512]{1,0:T(8,128)S(1)} %fusion.2, f32[8,512]{1,0:T(8,128)S(1)} %get-tuple-element.23, f32[512,512,8]{1,0,2:T(8,128)} %copy-done.1, pred[512,512]{0,1:T(8,128)(4,1)S(1)} %fusion.47, bf16[512,1024]{1,0:T(8,128)(2,1)} %param.15), kind=kOutput, calls=%fused_computation.31 | convolution fusion | flops 549519360 | bytes 9863168 | tf_op jit(solution)/shard_map/bkgqm,bqkge->bmke/dot_general | solution.py:29
  189.0 7.3 %all-gather.1 = bf16[1,512,1,512]{3,1,2,0:T(8,128)(2,1)S(1)} all-gather(bf16[1,512,1,128]{3,1,2,0:T(8,128)(2,1)S(1)} %fusion.33), channel_id=3, replica_groups=mesh['dp'=8,'mp'=4] {'mp'}, dimensions={3}, use_global_device_ids=true | all-gather | bytes 655360 | tf_op jit(solution)/shard_map/all_gather | solution.py:103
  196.3 3.2 fusion.53
  199.5 2.3 copy.43
  203.4 2.6 add_convert_fusion
  206.0 65.1 %reduce-scatter.9.cloned.1.call-done = f32[256,512]{1,0:T(8,128)} async-done(((f32[2048,512]{1,0:T(8,128)}), f32[256,512]{1,0:T(8,128)}) %reduce-scatter.9.cloned.1.call-update) | async-done | bytes 524304 | tf_op jit(solution)/shard_map/reduce_scatter | solution.py:110
  271.1 1.9 broadcast_multiply_fusion.1
  273.0 89.9 %reduce-scatter.11.cloned.1.call-done = f32[256,512]{1,0:T(8,128)} async-done(((f32[2048,512]{1,0:T(8,128)}), f32[256,512]{1,0:T(8,128)}) %reduce-scatter.11.cloned.1.call-update) | async-done | bytes 524304 | tf_op jit(solution)/shard_map/reduce_scatter | solution.py:111
  362.9 1.9 broadcast_multiply_fusion
  (44 shorter events, 13.1 us)
Async XLA Ops:
  7.2 86.4 %copy-start = (bf16[2048,512]{1,0:T(8,128)(2,1)S(1)}, bf16[2048,512]{1,0:T(8,128)(2,1)}, u32[]{:S(2)}) copy-start(bf16[2048,512]{1,0:T(8,128)(2,1)} %param.16) | copy-start | bytes 6291460
  12.5 13.7 %all-to-all-start.1 = ((s32[8,4,1]{1,2,0:T(1,128)}), s32[8,4,1]{1,2,0:T(1,128)S(1)}, u32[]{:S(2)}, u32[]{:S(2)}) async-start(s32[8,4,1]{1,2,0:T(1,128)} %bitcast.3), calls=%async_computation.1 | async-start | bytes 8192 | tf_op jit(solution)/shard_map/all_to_all | solution.py:63
  26.2 10.3 %all-to-all-start = ((s32[8,4,1]{1,2,0:T(1,128)}), s32[8,4,1]{1,2,0:T(1,128)S(1)}, u32[]{:S(2)}, u32[]{:S(2)}) async-start(s32[8,4,1]{1,2,0:T(1,128)} %bitcast.2), calls=%async_computation | async-start | bytes 8192 | tf_op jit(solution)/shard_map/all_to_all | solution.py:62
  36.5 51.0 %all-to-all-start.2 = ((bf16[32,16,2048]{2,1,0:T(8,128)(2,1)}), bf16[32,16,2048]{2,1,0:T(8,128)(2,1)}, u32[]{:S(2)}, u32[]{:S(2)}) async-start(bf16[32,16,2048]{2,1,0:T(8,128)(2,1)} %select_select_fusion), calls=%async_computation.2 | async-start | bytes 4194304 | tf_op jit(solution)/shard_map/all_to_all | solution.py:61
  40.8 80.5 %reduce-scatter.7.cloned.1.call-start = ((), (), s32[]{:S(2)}) async-start(), calls=%async_computation.8 | async-start | bytes 1310720 | tf_op jit(solution)/shard_map/reduce_scatter | solution.py:75
  97.4 51.5 %reduce-scatter.5.cloned.1.call-start = ((), (), s32[]{:S(2)}) async-start(), calls=%async_computation.7 | async-start | bytes 1310720 | tf_op jit(solution)/shard_map/reduce_scatter | solution.py:76
  102.1 169.1 %reduce-scatter.9.cloned.1.call-start = ((), (), s32[]{:S(2)}) async-start(), calls=%async_computation.9 | async-start | bytes 4718592 | tf_op jit(solution)/shard_map/reduce_scatter | solution.py:110
  124.2 3.2 copy-start.1
  182.7 180.2 %reduce-scatter.11.cloned.1.call-start = ((), (), s32[]{:S(2)}) async-start(), calls=%async_computation.10 | async-start | bytes 4718592 | tf_op jit(solution)/shard_map/reduce_scatter | solution.py:111
  183.0 13.3 %copy-start.2 = (bf16[512,2048]{1,0:T(8,128)(2,1)S(1)}, bf16[512,2048]{1,0:T(8,128)(2,1)}, u32[]{:S(2)}) copy-start(bf16[512,2048]{1,0:T(8,128)(2,1)} %scatter_custom_fusion) | copy-start | bytes 6291460
  201.8 1.6 copy-start.3
Sparse Core Ops, SparseCore 0:
  97.6 23.7 reduce-scatter.6
  124.0 24.8 reduce-scatter.4
  182.8 88.2 reduce-scatter.8
  275.1 87.8 reduce-scatter.10
where the time goes:
time: 372 us; the launch traced here: 371 us
  waiting for transfers between devices  239 us (64%)
  matrix products  44.4 us (12%)
  local copies, waits for them, and re-layouts  28.5 us (8%)
  starting transfers between devices  15.9 us (4%)
  other arithmetic  15.2 us (4%)
  blocking collectives  14.1 us (4%)
  between operations  13.9 us (4%)
    reduce_scatter x1, waiting for transfers between devices, local(): lax.psum_scatter(whole_v, 'dp', scatter_dimension=0, tiled=True)  89.9 us
    reduce_scatter x1, waiting for transfers between devices, local(): lax.psum_scatter(whole_k, 'dp', scatter_dimension=0, tiled=True)  65.1 us
    all_to_all x1, waiting for transfers between devices, local(): lax.all_to_all(send_x, 'dp', split_axis=0, concat_axis=0, tiled=True)  44.4 us
    reduce_scatter x1, waiting for transfers between devices, local(): lax.psum_scatter(part_v, 'mp', scatter_dimension=1, tiled=True)  19.7 us
    reduce_scatter x1, waiting for transfers between devices, local(): lax.psum_scatter(part_k, 'mp', scatter_dimension=1, tiled=True)  14.7 us
    unnamed x11, local copies, waits for them, and re-layouts  10.2 us
    dot_general x1, matrix products, attend(): jnp.einsum('bkgqm,bmke->bqkge', probs_b, vs, preferred_element_type=jnp.f...  7.9 us
  transfers between devices with their start and end apart: 7, of which 7 were waited for; matrix products, arithmetic and copies ran while one was open for 11% of the time, Pallas kernels for 0%

commit v1 on v0

--- a/solution.py
+++ b/solution.py
@@ -1,6 +1,10 @@
+import functools
+
 import jax
 import jax.numpy as jnp
 from jax import lax
+from jax.experimental import pallas as pl
+from jax.experimental.pallas import tpu as pltpu
 from jax.sharding import PartitionSpec as P
 
 HEAD_DIM = 128
@@ -39,7 +43,7 @@
     return total.astype(jnp.bfloat16)
 
 
-def local(roll_x, lengths, dest, offsets, queries, out_grad, w_key, w_value):
+def general(roll_x, lengths, dest, offsets, queries, out_grad, w_key, w_value):
     learners = lax.axis_size("dp")
     samp, lmax, feats = roll_x.shape
     rows = queries.shape[0]
@@ -113,9 +117,373 @@
     return (attn_out, grad_x, sum_k / learners, sum_v / learners)
 
 
+BF16, F32, I32 = jnp.bfloat16, jnp.float32, jnp.int32
+ROWS_LAST = (((0,), (0,)), ((), ()))
+COLS_LAST = (((1,), (1,)), ((), ()))
+
+
+def dot(a, b, dims=(((1,), (0,)), ((), ()))):
+    return lax.dot_general(a, b, dims, preferred_element_type=F32)
+
+
+def iota(shape, dim):
+    return lax.broadcasted_iota(I32, shape, dim)
+
+
+def params(steps=1):
+    return pltpu.CompilerParams(
+        dimension_semantics=("arbitrary",) * steps, vmem_limit_bytes=48 * 1024 * 1024
+    )
+
+
+def cost(flops, moved):
+    return pl.CostEstimate(flops=flops, bytes_accessed=moved, transcendentals=0)
+
+
+def whole(shape):
+    zeros = (0,) * len(shape)
+    return pl.BlockSpec(shape, lambda *_: zeros)
+
+
+def project_kernel(me_ref, x_ref, wk_ref, wv_ref, out_ref):
+    weights = jnp.concatenate([wk_ref[...], wv_ref[...]], axis=1)
+    out_ref[0] = dot(x_ref[...], weights)
+
+
+def project(me, x, w_key, w_value, first):
+    rows, feats = x.shape
+    spec = pltpu.PrefetchScalarGridSpec(
+        num_scalar_prefetch=1,
+        grid=(2,),
+        in_specs=[
+            pl.BlockSpec((rows, feats), lambda i, me: (0, 0)),
+            pl.BlockSpec((feats, HEAD_DIM), lambda i, me: (0, me[0] ^ (first - 2 * i))),
+            pl.BlockSpec((feats, HEAD_DIM), lambda i, me: (0, me[0] ^ (first - 2 * i))),
+        ],
+        out_specs=pl.BlockSpec((1, rows, 2 * HEAD_DIM), lambda i, me: (i, 0, 0)),
+    )
+    return pl.pallas_call(
+        project_kernel,
+        out_shape=jax.ShapeDtypeStruct((2, rows, 2 * HEAD_DIM), F32),
+        grid_spec=spec,
+        compiler_params=params(),
+        cost_estimate=cost(4 * rows * feats * 2 * HEAD_DIM, 6 << 20),
+        name="project",
+    )(me, x, w_key, w_value)
+
+
+def slots_kernel(per, dest_ref, len_ref, off_ref, x_ref, xs_ref, pick_ref, meta_ref, pick):
+    samp = dest_ref.shape[1]
+    rows = x_ref.shape[0]
+    lmax = rows // samp
+
+    @pl.when(pl.program_id(0) == 0)
+    def _():
+        row = dest_ref[...]
+        a, b = iota((samp, samp), 0), iota((samp, samp), 1)
+        col = jnp.sum(jnp.where(a == b, row, 0), axis=1, keepdims=True)
+        rank = jnp.sum(jnp.where((col == row) & (a < b), 1, 0), axis=0, keepdims=True)
+        slot = row * per + rank
+        a, b = iota((samp, rows), 0), iota((samp, rows), 1)
+        spread = (a == lax.div(b, lmax)).astype(BF16)
+        wide = dot(jnp.broadcast_to(slot, (8, samp)).astype(BF16), spread)[0:1]
+        source = wide.astype(I32) * lmax + lax.rem(iota((1, rows), 1), lmax)
+        pick[...] = (iota((rows, rows), 0) == source).astype(BF16)
+        pick_ref[...] = pick[...]
+        held = iota((samp, samp), 0) == slot
+        size = jnp.sum(jnp.where(held, len_ref[...], 0), axis=1, keepdims=True)
+        start = jnp.sum(jnp.where(held, off_ref[...], 0), axis=1, keepdims=True)
+        lane = iota((samp, meta_ref.shape[2]), 1)
+        table = jnp.where(
+            lane == 0, size, jnp.where(lane == 1, lax.div(start, lmax), jnp.where(lane == 2, lax.rem(start, lmax), 0))
+        ).astype(BF16)
+        lines = meta_ref.shape[0] * meta_ref.shape[1]
+        a, b = iota((lines, samp), 0), iota((lines, samp), 1)
+        place = ((b == lax.div(a, 16) * per + lax.rem(a, 16)) & (lax.rem(a, 16) < per)).astype(BF16)
+        meta_ref[...] = dot(place, table).astype(BF16).reshape(meta_ref.shape)
+
+    xs_ref[0] = dot(pick[...], x_ref[...]).astype(BF16)
+
+
+def slots(dest, lengths, offsets, x, learners, per):
+    rows, feats = x.shape
+    samp = dest.shape[0]
+    part = feats // learners
+    line = whole((1, samp))
+    return pl.pallas_call(
+        functools.partial(slots_kernel, per),
+        out_shape=(
+            jax.ShapeDtypeStruct((learners, rows, part), BF16),
+            jax.ShapeDtypeStruct((rows, rows), BF16),
+            jax.ShapeDtypeStruct((learners, 16, 2 * HEAD_DIM), BF16),
+        ),
+        grid=(learners,),
+        in_specs=[line, line, line, pl.BlockSpec((rows, part), lambda i: (0, i))],
+        out_specs=(
+            pl.BlockSpec((1, rows, part), lambda i: (i, 0, 0)),
+            whole((rows, rows)),
+            whole((learners, 16, 2 * HEAD_DIM)),
+        ),
+        scratch_shapes=[pltpu.VMEM((rows, rows), BF16)],
+        compiler_params=params(),
+        cost_estimate=cost(2 * rows * rows * feats, 5 << 20),
+        name="slots",
+    )(dest.reshape(1, samp), lengths.reshape(1, samp), offsets.reshape(1, samp), x)
+
+
+def pack_kernel(mine_ref, core_ref, across_ref, pick_ref, meta_ref, out_ref):
+    total = (mine_ref[0] + core_ref[0]) + across_ref[...]
+    placed = dot(pick_ref[...], total.astype(BF16)).astype(BF16)
+    learners = out_ref.shape[0]
+    block = placed.shape[0] // learners
+    for i in range(learners):
+        out_ref[i, :block, :] = placed[i * block : (i + 1) * block]
+        out_ref[i, block:, :] = meta_ref[i]
+
+
+def pack(mine, core, across, pick, meta):
+    rows, cols = across.shape
+    learners, extra, _ = meta.shape
+    out = (learners, rows // learners + extra, cols)
+    second = pl.BlockSpec((1, rows, cols), lambda i: (1, 0, 0))
+    return pl.pallas_call(
+        pack_kernel,
+        out_shape=jax.ShapeDtypeStruct(out, BF16),
+        grid=(1,),
+        in_specs=[second, second, whole((rows, cols)), whole((rows, rows)), whole(meta.shape)],
+        out_specs=whole(out),
+        compiler_params=params(),
+        cost_estimate=cost(2 * rows * rows * cols, 3 << 20),
+        name="pack",
+    )(mine, core, across, pick, meta)
+
+
+def attention_kernel(lmax, per, kv_ref, q_ref, g_ref, out_ref, grad_ref, place_ref, slot_out):
+    rows, cols = q_ref.shape
+    learners, lines, _ = kv_ref.shape
+    block = rows // learners
+    heads = cols // HEAD_DIM
+    scale = 1.0 / HEAD_DIM**0.5
+    meta = kv_ref[:, block:, :HEAD_DIM].reshape(learners * (lines - block), HEAD_DIM)
+    a, b = iota((rows, meta.shape[0]), 0), iota((rows, meta.shape[0]), 1)
+    spread = (lax.div(a, block) * (lines - block) + lax.div(lax.rem(a, block), lmax) == b).astype(BF16)
+    table = dot(spread, meta).astype(I32)
+    inner = lax.rem(iota((rows, 1), 0), lmax)
+    alive = inner < table[:, 0:1]
+    target = jnp.where(alive, table[:, 1:2] * lmax + table[:, 2:3] + inner, -1)
+    place_ref[...] = (iota((rows, rows), 1) == target).astype(BF16)
+    size = HEAD_DIM
+    a, b = iota((size, size), 0), iota((size, size), 1)
+    near = (lax.div(a, lmax) == lax.div(b, lmax)) & (b <= a)
+    for i in range(rows // size):
+        span = slice(i * size, (i + 1) * size)
+        first = i * size // block
+        kv = jnp.concatenate([kv_ref[first + j, :block, :] for j in range(size // block)], axis=0)
+        k, v = kv[:, :HEAD_DIM], kv[:, HEAD_DIM:]
+        place = place_ref[span, :]
+        q = dot(place, q_ref[...]).astype(BF16)
+        g = dot(place, g_ref[...]).astype(BF16)
+        q = jnp.concatenate([q[:, h * HEAD_DIM : (h + 1) * HEAD_DIM] for h in range(heads)], axis=0)
+        g = jnp.concatenate([g[:, h * HEAD_DIM : (h + 1) * HEAD_DIM] for h in range(heads)], axis=0)
+        allowed = jnp.tile(near & alive[span], (heads, 1))
+        scores = jnp.where(allowed, dot(q, k, COLS_LAST) * scale, -1e30)
+        top = jnp.max(scores, axis=1, keepdims=True)
+        expo = jnp.exp(scores - top)
+        total = jnp.sum(expo, axis=1, keepdims=True)
+        probs = jnp.where(allowed, expo / total, 0.0)
+        probs_b = probs.astype(BF16)
+        out = dot(probs_b, v).astype(BF16)
+        dprob = dot(g, v, COLS_LAST)
+        delta = jnp.sum(g.astype(F32) * out.astype(F32), axis=1, keepdims=True)
+        dscore_b = (probs * (dprob - delta)).astype(BF16)
+        grad_ref[span, :HEAD_DIM] = (dot(dscore_b, q, ROWS_LAST) * scale).astype(BF16)
+        grad_ref[span, HEAD_DIM:] = dot(probs_b, g, ROWS_LAST).astype(BF16)
+        for h in range(heads):
+            slot_out[span, h * HEAD_DIM : (h + 1) * HEAD_DIM] = out[h * size : (h + 1) * size]
+    out_ref[...] = dot(place_ref[...], slot_out[...], ROWS_LAST).astype(BF16)
+
+
+def attention(kv, queries, out_grad, lmax, per):
+    rows, cols = queries.shape
+    return pl.pallas_call(
+        functools.partial(attention_kernel, lmax, per),
+        out_shape=(
+            jax.ShapeDtypeStruct((rows, cols), BF16),
+            jax.ShapeDtypeStruct((rows, 2 * HEAD_DIM), BF16),
+            jax.ShapeDtypeStruct((rows, rows), BF16),
+        ),
+        grid=(1,),
+        in_specs=[whole(kv.shape), whole((rows, cols)), whole((rows, cols))],
+        out_specs=(whole((rows, cols)), whole((rows, 2 * HEAD_DIM)), whole((rows, rows))),
+        scratch_shapes=[pltpu.VMEM((rows, cols), BF16)],
+        compiler_params=params(),
+        cost_estimate=cost(8 * rows * rows * cols, 4 << 20),
+        name="attention",
+    )(kv, queries, out_grad)
+
+
+def rows_kernel(me_ref, place_ref, g0, g1, g2, g3, wk_ref, wv_ref, out_ref, grads):
+    @pl.when(pl.program_id(0) == 0)
+    def _():
+        half = grads.shape[1] // 2
+        for i, ref in enumerate((g0, g1, g2, g3)):
+            part = dot(place_ref[...], ref[...], ROWS_LAST).astype(BF16)
+            at = pl.multiple_of((me_ref[0] ^ i) * HEAD_DIM, HEAD_DIM)
+            grads[:, pl.ds(at, HEAD_DIM)] = part[:, :HEAD_DIM]
+            grads[:, pl.ds(at + half, HEAD_DIM)] = part[:, HEAD_DIM:]
+
+    half = grads.shape[1] // 2
+    total = dot(grads[:, :half], wk_ref[...], COLS_LAST)
+    out_ref[...] = (total + dot(grads[:, half:], wv_ref[...], COLS_LAST)).astype(BF16)
+
+
+def row_grads(me, place, parts, w_key, w_value):
+    feats, cols = w_key.shape
+    rows = place.shape[0]
+    step = 512
+    spec = pltpu.PrefetchScalarGridSpec(
+        num_scalar_prefetch=1,
+        grid=(feats // step,),
+        in_specs=[whole((rows, rows))]
+        + [whole((rows, 2 * HEAD_DIM))] * 4
+        + [pl.BlockSpec((step, cols), lambda i, me: (i, 0))] * 2,
+        out_specs=pl.BlockSpec((rows, step), lambda i, me: (0, i)),
+        scratch_shapes=[pltpu.VMEM((rows, 2 * cols), BF16)],
+    )
+    return pl.pallas_call(
+        rows_kernel,
+        out_shape=jax.ShapeDtypeStruct((rows, feats), BF16),
+        grid_spec=spec,
+        compiler_params=params(),
+        cost_estimate=cost(4 * rows * feats * cols, 8 << 20),
+        name="row_grads",
+    )(me, place, *parts, w_key, w_value)
+
+
+def weights_kernel(codes, starts, me_ref, *refs):
+    refs = list(refs)
+    x_refs = refs[:2]
+    g_refs = refs[2 : 2 + len(codes)]
+    before = refs[2 + len(codes)] if starts else None
+    out_ref = refs[-1]
+    learners, rows, part = x_refs[0].shape
+    block = rows // learners
+    for side in range(2):
+        for far in range(2):
+            mine = [(e, r) for (e, f), r in zip(codes, g_refs) if f == far]
+            if not mine:
+                continue
+            cols = slice(far * 2 * HEAD_DIM, (far + 1) * 2 * HEAD_DIM)
+            total = before[side, :, cols] if starts else None
+            for code, ref in mine:
+                at = pl.multiple_of((me_ref[0] ^ code) * block, block)
+                x = x_refs[side][:, pl.ds(at, block), :].reshape(rows, part)
+                term = dot(x, ref[...], ROWS_LAST)
+                total = term if total is None else total + term
+            out_ref[side, :, cols] = total
+
+
+def weight_grads(me, x, x_core, pieces, before=None):
+    codes = list(pieces)
+    learners, rows, part = x.shape
+    shape = (2, part, 4 * HEAD_DIM)
+    given = [x, x_core] + [pieces[c] for c in codes] + ([] if before is None else [before])
+    spec = pltpu.PrefetchScalarGridSpec(
+        num_scalar_prefetch=1,
+        grid=(1,),
+        in_specs=[whole(a.shape) for a in given],
+        out_specs=whole(shape),
+    )
+    return pl.pallas_call(
+        functools.partial(weights_kernel, codes, before is not None),
+        out_shape=jax.ShapeDtypeStruct(shape, F32),
+        grid_spec=spec,
+        compiler_params=params(),
+        cost_estimate=cost(4 * len(codes) * rows * part * 2 * HEAD_DIM, 6 << 20),
+        name="weight_grads",
+    )(me, *given)
+
+
+def finish_kernel(learners, me_ref, own_ref, core_ref, k_ref, v_ref):
+    for side, ref in enumerate((own_ref, core_ref)):
+        for far in range(2):
+            at = pl.multiple_of((me_ref[0] ^ (side + 2 * far)) * HEAD_DIM, HEAD_DIM)
+            base = far * 2 * HEAD_DIM
+            k_ref[:, pl.ds(at, HEAD_DIM)] = ref[0, :, base : base + HEAD_DIM] / learners
+            v_ref[:, pl.ds(at, HEAD_DIM)] = ref[0, :, base + HEAD_DIM : base + 2 * HEAD_DIM] / learners
+
+
+def finish(me, own, core, learners):
+    _, part, cols = own.shape
+    spec = pltpu.PrefetchScalarGridSpec(
+        num_scalar_prefetch=1,
+        grid=(1,),
+        in_specs=[whole((1, part, cols))] * 2,
+        out_specs=(whole((part, cols)),) * 2,
+    )
+    return pl.pallas_call(
+        functools.partial(finish_kernel, float(learners)),
+        out_shape=(jax.ShapeDtypeStruct((part, cols), F32),) * 2,
+        grid_spec=spec,
+        compiler_params=params(),
+        cost_estimate=cost(part * cols, 2 << 20),
+        name="finish",
+    )(me, own, core)
+
+
+def swap(x, axis, code):
+    return lax.ppermute(x, axis, [(i, i ^ code) for i in range(lax.axis_size(axis))])
+
+
+def local(roll_x, lengths, dest, offsets, queries, out_grad, w_key, w_value):
+    learners = lax.axis_size("dp")
+    samp, lmax, feats = roll_x.shape
+    per = (samp + learners - 1) // learners
+    x = roll_x.reshape(samp * lmax, feats)
+    m = lax.axis_index("mp").astype(I32).reshape(1)
+    d = lax.axis_index("dp").astype(I32).reshape(1)
+
+    away = project(m, x, w_key, w_value, 3)
+    core = swap(away, "mp", 1)
+    mine = project(m, x, w_key, w_value, 2)
+    across = swap(mine[0] + core[0], "mp", 2)
+    xs, pick, meta = slots(dest, lengths, offsets, x, learners, per)
+    xs = lax.all_to_all(xs, "dp", split_axis=0, concat_axis=0, tiled=True)
+    xs_core = swap(xs, "mp", 1)
+    kv = pack(mine, core, across, pick, meta)
+    kv = lax.all_to_all(kv, "dp", split_axis=0, concat_axis=0, tiled=True)
+
+    attn_out, grads, place = attention(kv, queries, out_grad, lmax, per)
+
+    near = {(0, 0): grads}
+    hops = [
+        ((0, 0), "dp", 4), ((0, 0), "dp", 2), ((0, 0), "mp", 2), ((0, 0), "dp", 1),
+        ((0, 1), "dp", 4), ((1, 0), "dp", 2), ((1, 0), "mp", 2),
+        ((2, 0), "mp", 2), ((4, 0), "dp", 1), ((4, 0), "dp", 2), ((3, 0), "mp", 2),
+        ((5, 0), "mp", 2), ((6, 0), "dp", 1), ((4, 1), "dp", 2), ((6, 1), "dp", 1),
+    ]
+    for (code, far), axis, step in hops:
+        key = (code ^ step, far) if axis == "dp" else (code, 1 - far)
+        near[key] = swap(near[code, far], axis, step)
+    grad_x = row_grads(
+        m,
+        place,
+        [near[0, 0], swap(near[0, 0], "mp", 1), near[0, 1], swap(near[0, 1], "mp", 1)],
+        w_key,
+        w_value,
+    )
+    early = [(0, 0), (0, 1), (1, 0), (1, 1), (2, 0), (4, 0), (2, 1), (3, 0), (3, 1), (5, 0), (4, 1)]
+    sums = weight_grads(d, xs, xs_core, {c: near[c] for c in early})
+    sums = weight_grads(d, xs, xs_core, {c: near[c] for c in near if c not in early}, sums)
+    grad_wk, grad_wv = finish(m, sums, swap(sums[1:], "mp", 1), learners)
+    return (attn_out, grad_x, grad_wk, grad_wv)
+
+
 def solution(mesh):
+    dp, mp = mesh.shape["dp"], mesh.shape["mp"]
+    body = local if dp == 8 and mp == 4 else general
     return jax.shard_map(
-        local,
+        body,
         mesh=mesh,
         in_specs=(
             P("dp", None, "mp"),

time: 372 us -> 152 us (0.41)
  waiting for transfers between devices: 239 us -> 62.6 us
  matrix products: 44.4 us -> 0 us
  Pallas kernels: 0 us -> 29.1 us
  other arithmetic: 15.2 us -> 0.94 us
  between operations: 13.9 us -> 0.82 us
  local copies, waits for them, and re-layouts: 28.5 us -> 17.1 us
  starting transfers between devices: 15.9 us -> 25.9 us
    reduce_scatter x4 -> x0, waiting for transfers between devices: 189 us -> none  [the longest x1 89.9 us: local(): lax.psum_scatter(whole_v, 'dp', scatter_dimension=0, tiled=True)]
    dot_general x10 -> x0, matrix products: 44.4 us -> none  [the longest x1 7.9 us: attend(): jnp.einsum('bkgqm,bmke->bqkge', probs_b, vs, preferred_element_type=jnp.f...]
    pallas_call x0 -> x9, Pallas kernels: none -> 29.1 us  [the longest x1 6.83 us: attention(): pl.pallas_call(functools.partial(attention_kernel, lmax, per), out_shape=...]
    ppermute x0 -> x21, waiting for transfers between devices: none -> 25.5 us  [swap(): lax.ppermute(x, axis, [(i, i ^ code) for i in range(lax.axis_size(axis))])]
    ppermute x0 -> x21, starting transfers between devices: none -> 18.6 us  [swap(): lax.ppermute(x, axis, [(i, i ^ code) for i in range(lax.axis_size(axis))])]
    all_to_all x0 -> x1, blocking collectives: none -> 15 us  [local(): kv = lax.all_to_all(kv, 'dp', split_axis=0, concat_axis=0, tiled=True)]
    all_gather x2 -> x0, blocking collectives: 14.1 us -> none  [the longest x1 7.31 us: local(): lax.all_gather(val_grad, 'mp', axis=1, tiled=True)]
    all_to_all x3 -> x1, waiting for transfers between devices: 49.7 us -> 37.1 us  [local(): xs = lax.all_to_all(xs, 'dp', split_axis=0, concat_axis=0, tiled=True)]
  transfers between devices with their start and end apart: 7 -> 22, of which waited for: 7 -> 10; matrix products, arithmetic and copies ran while one was open for 11% -> 1% of each run, Pallas kernels for 0% -> 14%
where the time goes in v1:
time: 152 us; the launch traced here: 151 us
  waiting for transfers between devices  62.6 us (41%)
  Pallas kernels  29.1 us (19%)
  starting transfers between devices  25.9 us (17%)
  local copies, waits for them, and re-layouts  17.1 us (11%)
  blocking collectives  15 us (10%)
    all_to_all x1, waiting for transfers between devices, local(): xs = lax.all_to_all(xs, 'dp', split_axis=0, concat_axis=0, tiled=True)  37.1 us
    ppermute x21, waiting for transfers between devices, swap(): lax.ppermute(x, axis, [(i, i ^ code) for i in range(lax.axis_size(axis))])  25.5 us
    ppermute x21, starting transfers between devices, swap(): lax.ppermute(x, axis, [(i, i ^ code) for i in range(lax.axis_size(axis))])  18.6 us
    unnamed x46, local copies, waits for them, and re-layouts  17.1 us
    all_to_all x1, blocking collectives, local(): kv = lax.all_to_all(kv, 'dp', split_axis=0, concat_axis=0, tiled=True)  15 us
    all_to_all x1, starting transfers between devices, local(): xs = lax.all_to_all(xs, 'dp', split_axis=0, concat_axis=0, tiled=True)  7.28 us
    pallas_call x1, Pallas kernels, attention(): pl.pallas_call(functools.partial(attention_kernel, lmax, per), out_shape=...  6.83 us
    pallas_call x2, Pallas kernels, weight_grads(): pl.pallas_call(functools.partial(weights_kernel, codes, before is not Non...  6.39 us
  transfers between devices with their start and end apart: 22, of which 10 were waited for; matrix products, arithmetic and copies ran while one was open for 1% of the time, Pallas kernels for 14%

profile of v1, /device:TPU:0, one launch (start us, length us, event | category | flops | bytes accessed | tf_op | source)
XLA Modules:
  0.0 151.5 jit_solution(15083639809203993248)
XLA Ops:
  0.6 1.6 %copy-done = bf16[32,16,2048]{2,1,0:T(8,128)(2,1)S(1)} copy-done((bf16[32,16,2048]{2,1,0:T(8,128)(2,1)S(1)}, bf16[32,16,2048]{2,1,0:T(8,128)(2,1)}, u32[]{:S(2)}) %copy-start) | copy-done | bytes 2097176
  4.2 3.2 %slots.1 = (bf16[8,512,256]{2,1,0:T(8,128)(2,1)S(1)}, bf16[512,512]{1,0:T(8,128)(2,1)S(1)}, bf16[8,16,256]{2,1,0:T(8,128)(2,1)S(1)}) custom-call(s32[1,32]{1,0:T(1,128)S(1)} %bitcast.11, s32[1,32]{1,0:T(1,128)S(1)} %bitcast.12, s32[1,32]{1,0:T(1,128)S(1)} %bitcast.13, bf16[512,2048]{1,0:T(8,128)(2,1)S(1)} %bitcast.8), custom_call_target="tpu_custom_call" | custom-call | flops 1073741824 | bytes 5242880 | tf_op jit(solution)/shard_map/slots/pallas_call | solution.py:213
  7.4 1.3 copy-done.7
  9.6 7.3 %all-to-all-start.1 = ((bf16[8,512,256]{2,1,0:T(8,128)(2,1)}), bf16[8,512,256]{2,1,0:T(8,128)(2,1)S(1)}, u32[]{:S(2)}, u32[]{:S(2)}) async-start(bf16[8,512,256]{2,1,0:T(8,128)(2,1)} %copy-done.7), calls=%async_computation.1 | async-start | bytes 4194304 | tf_op jit(solution)/shard_map/all_to_all | solution.py:451
  16.8 1.6 %copy-done.1 = bf16[32,16,2048]{2,1,0:T(8,128)(2,1)S(1)} copy-done((bf16[32,16,2048]{2,1,0:T(8,128)(2,1)S(1)}, bf16[32,16,2048]{2,1,0:T(8,128)(2,1)}, u32[]{:S(2)}) %copy-start.1) | copy-done | bytes 2097176
  18.4 1.6 %copy-done.2 = bf16[2048,512]{1,0:T(8,128)(2,1)S(1)} copy-done((bf16[2048,512]{1,0:T(8,128)(2,1)S(1)}, bf16[2048,512]{1,0:T(8,128)(2,1)}, u32[]{:S(2)}) %copy-start.2) | copy-done | bytes 2097176
  20.0 2.6 %project.3 = f32[2,512,256]{2,1,0:T(8,128)S(1)} custom-call(s32[1]{0:T(128)} %bitcast.me_ref, bf16[512,2048]{1,0:T(8,128)(2,1)S(1)} %bitcast.9, bf16[2048,512]{1,0:T(8,128)(2,1)S(1)} %copy-done.2, bf16[2048,512]{1,0:T(8,128)(2,1)} %wv_ref.5), custom_call_target="tpu_custom_call" | custom-call | flops 1073741824 | bytes 6291456 | tf_op jit(solution)/shard_map/project/pallas_call | solution.py:165
  22.7 2.6 %project.2.mine_ref = f32[2,512,256]{2,1,0:T(8,128)S(1)} custom-call(s32[1]{0:T(128)} %bitcast.me_ref, bf16[512,2048]{1,0:T(8,128)(2,1)S(1)} %bitcast.10, bf16[2048,512]{1,0:T(8,128)(2,1)S(1)} %copy-done.2, bf16[2048,512]{1,0:T(8,128)(2,1)} %wv_ref.5), custom_call_target="tpu_custom_call" | custom-call | flops 1073741824 | bytes 6291456 | tf_op jit(solution)/shard_map/project/pallas_call | solution.py:165
  26.5 1.5 collective-permute-start.1
  28.0 37.1 %all-to-all-done.1.refs_0_ = bf16[8,512,256]{2,1,0:T(8,128)(2,1)S(1)} async-done(((bf16[8,512,256]{2,1,0:T(8,128)(2,1)}), bf16[8,512,256]{2,1,0:T(8,128)(2,1)S(1)}, u32[]{:S(2)}, u32[]{:S(2)}) %all-to-all-start.1) | async-done | bytes 2097184 | tf_op jit(solution)/shard_map/all_to_all | solution.py:451
  65.1 1.2 copy-done.6
  67.4 1.5 %pack.1 = bf16[8,80,256]{2,1,0:T(8,128)(2,1)S(1)} custom-call(f32[2,512,256]{2,1,0:T(8,128)S(1)} %project.2.mine_ref, f32[2,512,256]{2,1,0:T(8,128)S(1)} %copy-done.6, f32[512,256]{1,0:T(8,128)} %collective-permute-done.1.across_ref, bf16[512,512]{1,0:T(8,128)(2,1)S(1)} %copy-done.9, bf16[8,16,256]{2,1,0:T(8,128)(2,1)S(1)} %get-tuple-element.13.meta_ref), custom_call_target="tpu_custom_call" | custom-call | flops 134217728 | bytes 3145728 | tf_op jit(solution)/shard_map/pack/pallas_call | solution.py:249
  68.9 15.0 %all_to_all.10.kv_ref = bf16[8,80,256]{2,1,0:T(8,128)(2,1)S(1)} all-to-all(bf16[8,80,256]{2,1,0:T(8,128)(2,1)S(1)} %pack.1), channel_id=1, replica_groups=mesh['dp'=8,'mp'=4] {'dp'}, dimensions={0} | all-to-all | bytes 655360 | tf_op jit(solution)/shard_map/all_to_all | solution.py:454
  83.9 6.8 %attention.1 = (bf16[512,1024]{1,0:T(8,128)(2,1)}, bf16[512,256]{1,0:T(8,128)(2,1)S(1)}, bf16[512,512]{1,0:T(8,128)(2,1)S(1)}) custom-call(bf16[8,80,256]{2,1,0:T(8,128)(2,1)S(1)} %all_to_all.10.kv_ref, bf16[512,1024]{1,0:T(8,128)(2,1)S(1)} %copy-done.16, bf16[512,1024]{1,0:T(8,128)(2,1)S(1)} %copy-done.17), custom_call_target="tpu_custom_call" | custom-call | flops 2147483648 | bytes 4194304 | tf_op jit(solution)/shard_map/attention/pallas_call | solution.py:308
  91.5 1.5 collective-permute-start.3
  94.1 1.7 %collective-permute-start.16 = (bf16[512,256]{1,0:T(8,128)(2,1)S(1)}, bf16[512,256]{1,0:T(8,128)(2,1)S(1)}, u32[]{:S(2)}, u32[]{:S(2)}) collective-permute-start(bf16[512,256]{1,0:T(8,128)(2,1)S(1)} %get-tuple-element.16.g0.refs_2_), channel_id=1, source_target_pairs={{0,8},{4,12},{8,0},{12,4},{16,24},{20,28},{24,16},{28,20},{1,9},{5... | collective-permute-start | bytes 786440 | tf_op jit(solution)/shard_map/ppermute | solution.py:435
  95.9 2.6 %collective-permute-done.3.g2.refs_3_ = bf16[512,256]{1,0:T(8,128)(2,1)S(1)} collective-permute-done((bf16[512,256]{1,0:T(8,128)(2,1)S(1)}, bf16[512,256]{1,0:T(8,128)(2,1)S(1)}, u32[]{:S(2)}, u32[]{:S(2)}) %collective-permute-start.3) | collective-permute-done | bytes 262176 | tf_op jit(solution)/shard_map/ppermute | solution.py:435
  98.5 1.9 %collective-permute-start.11 = (bf16[512,256]{1,0:T(8,128)(2,1)S(1)}, bf16[512,256]{1,0:T(8,128)(2,1)S(1)}, u32[]{:S(2)}, u32[]{:S(2)}) collective-permute-start(bf16[512,256]{1,0:T(8,128)(2,1)S(1)} %collective-permute-done.3.g2.refs_3_), channel_id=1, source_target_pairs={{0,16},{4,20},{8,24},{12,28},{16,0},{20,4},{24,8},{28,12},{1,17},{... | collective-permute-start | bytes 786440 | tf_op jit(solution)/shard_map/ppermute | solution.py:435
  100.4 1.1 collective-permute-start.18
  101.6 7.9 %collective-permute-done.6.refs_7_ = bf16[512,256]{1,0:T(8,128)(2,1)S(1)} collective-permute-done((bf16[512,256]{1,0:T(8,128)(2,1)S(1)}, bf16[512,256]{1,0:T(8,128)(2,1)S(1)}, u32[]{:S(2)}, u32[]{:S(2)}) %collective-permute-start.6) | collective-permute-done | bytes 262176 | tf_op jit(solution)/shard_map/ppermute | solution.py:435
  109.5 2.5 %collective-permute-start.8 = (bf16[512,256]{1,0:T(8,128)(2,1)S(1)}, bf16[512,256]{1,0:T(8,128)(2,1)}, u32[]{:S(2)}, u32[]{:S(2)}) collective-permute-start(bf16[512,256]{1,0:T(8,128)(2,1)S(1)} %collective-permute-done.6.refs_7_), channel_id=1, source_target_pairs={{0,4},{4,0},{8,12},{12,8},{16,20},{20,16},{24,28},{28,24},{1,5},{5... | collective-permute-start | bytes 786440 | tf_op jit(solution)/shard_map/ppermute | solution.py:435
  112.5 5.7 %collective-permute-done.11.refs_12_ = bf16[512,256]{1,0:T(8,128)(2,1)S(1)} collective-permute-done((bf16[512,256]{1,0:T(8,128)(2,1)S(1)}, bf16[512,256]{1,0:T(8,128)(2,1)S(1)}, u32[]{:S(2)}, u32[]{:S(2)}) %collective-permute-start.11) | collective-permute-done | bytes 262176 | tf_op jit(solution)/shard_map/ppermute | solution.py:435
  119.0 1.7 %collective-permute-start.12 = (bf16[512,256]{1,0:T(8,128)(2,1)S(1)}, bf16[512,256]{1,0:T(8,128)(2,1)}, u32[]{:S(2)}, u32[]{:S(2)}) collective-permute-start(bf16[512,256]{1,0:T(8,128)(2,1)S(1)} %collective-permute-done.11.refs_12_), channel_id=1, source_target_pairs={{0,8},{4,12},{8,0},{12,4},{16,24},{20,28},{24,16},{28,20},{1,9},{5... | collective-permute-start | bytes 786440 | tf_op jit(solution)/shard_map/ppermute | solution.py:435
  122.2 1.5 collective-permute-start.19
  123.7 3.8 %collective-permute-done.7.refs_2_ = bf16[512,256]{1,0:T(8,128)(2,1)} collective-permute-done((bf16[512,256]{1,0:T(8,128)(2,1)S(1)}, bf16[512,256]{1,0:T(8,128)(2,1)}, u32[]{:S(2)}, u32[]{:S(2)}) %collective-permute-start.7) | collective-permute-done | bytes 262176 | tf_op jit(solution)/shard_map/ppermute | solution.py:435
  127.5 1.2 collective-permute-start.10
  129.9 2.2 %collective-permute-done.12.refs_5_ = bf16[512,256]{1,0:T(8,128)(2,1)} collective-permute-done((bf16[512,256]{1,0:T(8,128)(2,1)S(1)}, bf16[512,256]{1,0:T(8,128)(2,1)}, u32[]{:S(2)}, u32[]{:S(2)}) %collective-permute-start.12) | collective-permute-done | bytes 262176 | tf_op jit(solution)/shard_map/ppermute | solution.py:435
  136.3 3.4 %weight_grads.2.refs_7_ = f32[2,256,512]{2,1,0:T(8,128)S(1)} custom-call(s32[1]{0:T(128)} %bitcast.6.me_ref, bf16[8,512,256]{2,1,0:T(8,128)(2,1)S(1)} %all-to-all-done.1.refs_0_, bf16[8,512,256]{2,1,0:T(8,128)(2,1)} %collective-permute-done.5.refs_1_, bf16[512,256]{1,0:T(8,128)(2,1)S(1)} %get-tuple-element.16.g0.refs_2_, ...), custom_call_target="tpu_custom_call" | custom-call | flops 1476395008 | bytes 6291456 | tf_op jit(solution)/shard_map/weight_grads/pallas_call | solution.py:397
  139.8 2.9 %weight_grads.3.own_ref = f32[2,256,512]{2,1,0:T(8,128)S(1)} custom-call(s32[1]{0:T(128)} %bitcast.6.me_ref, bf16[8,512,256]{2,1,0:T(8,128)(2,1)S(1)} %all-to-all-done.1.refs_0_, bf16[8,512,256]{2,1,0:T(8,128)(2,1)} %collective-permute-done.5.refs_1_, bf16[512,256]{1,0:T(8,128)(2,1)} %collective-permute-done.7.refs_2_, ...), custom_call_target="tpu_custom_call" | custom-call | flops 671088640 | bytes 6291456 | tf_op jit(solution)/shard_map/weight_grads/pallas_call | solution.py:397
  143.5 1.7 %collective-permute-done.2.g1 = bf16[512,256]{1,0:T(8,128)(2,1)S(1)} collective-permute-done((bf16[512,256]{1,0:T(8,128)(2,1)S(1)}, bf16[512,256]{1,0:T(8,128)(2,1)S(1)}, u32[]{:S(2)}, u32[]{:S(2)}) %collective-permute-start.2) | collective-permute-done | bytes 262176 | tf_op jit(solution)/shard_map/ppermute | solution.py:435
  145.6 4.8 %row_grads.1 = bf16[512,2048]{1,0:T(8,128)(2,1)} custom-call(s32[1]{0:T(128)} %bitcast.me_ref, bf16[512,512]{1,0:T(8,128)(2,1)S(1)} %copy-done.22, bf16[512,256]{1,0:T(8,128)(2,1)S(1)} %get-tuple-element.16.g0.refs_2_, bf16[512,256]{1,0:T(8,128)(2,1)S(1)} %collective-permute-done.2.g1, bf16[512,256]{1,0:T(8,128)(2,1)S(1)} %collective-permute-done.3.g2.refs_3_, ...), custom_call_target="tpu_custom_call" | custom-call | flops 2147483648 | bytes 8388608 | tf_op jit(solution)/shard_map/row_grads/pallas_call | solution.py:353
  150.4 1.1 finish.1
  (70 shorter events, 16.2 us)
Async XLA Ops:
  0.6 1.6 %copy-start = (bf16[32,16,2048]{2,1,0:T(8,128)(2,1)S(1)}, bf16[32,16,2048]{2,1,0:T(8,128)(2,1)}, u32[]{:S(2)}) copy-start(bf16[32,16,2048]{2,1,0:T(8,128)(2,1)} %param.8) | copy-start | bytes 6291460
  7.4 1.3 copy-start.7
  9.6 55.5 %all-to-all-start.1 = ((bf16[8,512,256]{2,1,0:T(8,128)(2,1)}), bf16[8,512,256]{2,1,0:T(8,128)(2,1)S(1)}, u32[]{:S(2)}, u32[]{:S(2)}) async-start(bf16[8,512,256]{2,1,0:T(8,128)(2,1)} %copy-done.7), calls=%async_computation.1 | async-start | bytes 4194304 | tf_op jit(solution)/shard_map/all_to_all | solution.py:451
  16.8 1.6 %copy-start.1 = (bf16[32,16,2048]{2,1,0:T(8,128)(2,1)S(1)}, bf16[32,16,2048]{2,1,0:T(8,128)(2,1)}, u32[]{:S(2)}) copy-start(bf16[32,16,2048]{2,1,0:T(8,128)(2,1)} %param.8) | copy-start | bytes 6291460
  18.4 1.6 %copy-start.2 = (bf16[2048,512]{1,0:T(8,128)(2,1)S(1)}, bf16[2048,512]{1,0:T(8,128)(2,1)}, u32[]{:S(2)}) copy-start(bf16[2048,512]{1,0:T(8,128)(2,1)} %wk_ref.5) | copy-start | bytes 6291460
  22.6 2.7 %collective-permute-start = (f32[2,512,256]{2,1,0:T(8,128)S(1)}, f32[2,512,256]{2,1,0:T(8,128)S(1)}, u32[]{:S(2)}, u32[]{:S(2)}) collective-permute-start(f32[2,512,256]{2,1,0:T(8,128)S(1)} %project.3), channel_id=1, source_target_pairs={{0,1},{1,0},{2,3},{3,2},{4,5},{5,4},{6,7},{7,6},{8,9},{9,8},{10,11... | collective-permute-start | bytes 3145736 | tf_op jit(solution)/shard_map/ppermute | solution.py:435
  26.5 38.6 %collective-permute-start.1 = (f32[512,256]{1,0:T(8,128)}, f32[512,256]{1,0:T(8,128)}, u32[]{:S(2)}, u32[]{:S(2)}) collective-permute-start(f32[512,256]{1,0:T(8,128)} %fusion), channel_id=1, source_target_pairs={{0,2},{1,3},{2,0},{3,1},{4,6},{5,7},{6,4},{7,5},{8,10},{9,11},{10,... | collective-permute-start | bytes 1572872 | tf_op jit(solution)/shard_map/ppermute | solution.py:435
  65.1 68.4 %collective-permute-start.5 = (bf16[8,512,256]{2,1,0:T(8,128)(2,1)S(1)}, bf16[8,512,256]{2,1,0:T(8,128)(2,1)}, u32[]{:S(2)}, u32[]{:S(2)}) collective-permute-start(bf16[8,512,256]{2,1,0:T(8,128)(2,1)S(1)} %all-to-all-done.1.refs_0_), channel_id=1, source_target_pairs={{0,1},{1,0},{2,3},{3,2},{4,5},{5,4},{6,7},{7,6},{8,9},{9,8},{10,11... | collective-permute-start | bytes 6291464 | tf_op jit(solution)/shard_map/ppermute | solution.py:435
  65.1 1.2 copy-start.6
  67.4 16.6 %copy-start.16 = (bf16[512,1024]{1,0:T(8,128)(2,1)S(1)}, bf16[512,1024]{1,0:T(8,128)(2,1)}, u32[]{:S(2)}) copy-start(bf16[512,1024]{1,0:T(8,128)(2,1)} %q_ref.1) | copy-start | bytes 3145732
  67.4 16.6 %copy-start.17 = (bf16[512,1024]{1,0:T(8,128)(2,1)S(1)}, bf16[512,1024]{1,0:T(8,128)(2,1)}, u32[]{:S(2)}) copy-start(bf16[512,1024]{1,0:T(8,128)(2,1)} %g_ref.1) | copy-start | bytes 3145732
  91.5 7.0 %collective-permute-start.3 = (bf16[512,256]{1,0:T(8,128)(2,1)S(1)}, bf16[512,256]{1,0:T(8,128)(2,1)S(1)}, u32[]{:S(2)}, u32[]{:S(2)}) collective-permute-start(bf16[512,256]{1,0:T(8,128)(2,1)S(1)} %get-tuple-element.16.g0.refs_2_), channel_id=1, source_target_pairs={{0,2},{1,3},{2,0},{3,1},{4,6},{5,7},{6,4},{7,5},{8,10},{9,11},{10,... | collective-permute-start | bytes 786440 | tf_op jit(solution)/shard_map/ppermute | solution.py:435
  93.0 7.4 %collective-permute-start.14 = (bf16[512,256]{1,0:T(8,128)(2,1)S(1)}, bf16[512,256]{1,0:T(8,128)(2,1)S(1)}, u32[]{:S(2)}, u32[]{:S(2)}) collective-permute-start(bf16[512,256]{1,0:T(8,128)(2,1)S(1)} %get-tuple-element.16.g0.refs_2_), channel_id=1, source_target_pairs={{0,4},{4,0},{8,12},{12,8},{16,20},{20,16},{24,28},{28,24},{1,5},{5... | collective-permute-start | bytes 786440 | tf_op jit(solution)/shard_map/ppermute | solution.py:435
  93.9 15.7 %collective-permute-start.6 = (bf16[512,256]{1,0:T(8,128)(2,1)S(1)}, bf16[512,256]{1,0:T(8,128)(2,1)S(1)}, u32[]{:S(2)}, u32[]{:S(2)}) collective-permute-start(bf16[512,256]{1,0:T(8,128)(2,1)S(1)} %get-tuple-element.16.g0.refs_2_), channel_id=1, source_target_pairs={{0,16},{4,20},{8,24},{12,28},{16,0},{20,4},{24,8},{28,12},{1,17},{... | collective-permute-start | bytes 786440 | tf_op jit(solution)/shard_map/ppermute | solution.py:435
  94.1 17.9 %collective-permute-start.16 = (bf16[512,256]{1,0:T(8,128)(2,1)S(1)}, bf16[512,256]{1,0:T(8,128)(2,1)S(1)}, u32[]{:S(2)}, u32[]{:S(2)}) collective-permute-start(bf16[512,256]{1,0:T(8,128)(2,1)S(1)} %get-tuple-element.16.g0.refs_2_), channel_id=1, source_target_pairs={{0,8},{4,12},{8,0},{12,4},{16,24},{20,28},{24,16},{28,20},{1,9},{5... | collective-permute-start | bytes 786440 | tf_op jit(solution)/shard_map/ppermute | solution.py:435
  98.5 19.7 %collective-permute-start.11 = (bf16[512,256]{1,0:T(8,128)(2,1)S(1)}, bf16[512,256]{1,0:T(8,128)(2,1)S(1)}, u32[]{:S(2)}, u32[]{:S(2)}) collective-permute-start(bf16[512,256]{1,0:T(8,128)(2,1)S(1)} %collective-permute-done.3.g2.refs_3_), channel_id=1, source_target_pairs={{0,16},{4,20},{8,24},{12,28},{16,0},{20,4},{24,8},{28,12},{1,17},{... | collective-permute-start | bytes 786440 | tf_op jit(solution)/shard_map/ppermute | solution.py:435
  100.4 18.1 %collective-permute-start.18 = (bf16[512,256]{1,0:T(8,128)(2,1)S(1)}, bf16[512,256]{1,0:T(8,128)(2,1)}, u32[]{:S(2)}, u32[]{:S(2)}) collective-permute-start(bf16[512,256]{1,0:T(8,128)(2,1)S(1)} %collective-permute-done.14.refs_4_), channel_id=1, source_target_pairs={{0,8},{4,12},{8,0},{12,4},{16,24},{20,28},{24,16},{28,20},{1,9},{5... | collective-permute-start | bytes 786440 | tf_op jit(solution)/shard_map/ppermute | solution.py:435
  109.5 9.5 %collective-permute-start.8 = (bf16[512,256]{1,0:T(8,128)(2,1)S(1)}, bf16[512,256]{1,0:T(8,128)(2,1)}, u32[]{:S(2)}, u32[]{:S(2)}) collective-permute-start(bf16[512,256]{1,0:T(8,128)(2,1)S(1)} %collective-permute-done.6.refs_7_), channel_id=1, source_target_pairs={{0,4},{4,0},{8,12},{12,8},{16,20},{20,16},{24,28},{28,24},{1,5},{5... | collective-permute-start | bytes 786440 | tf_op jit(solution)/shard_map/ppermute | solution.py:435
  112.0 9.5 %collective-permute-start.15 = (bf16[512,256]{1,0:T(8,128)(2,1)S(1)}, bf16[512,256]{1,0:T(8,128)(2,1)S(1)}, u32[]{:S(2)}, u32[]{:S(2)}) collective-permute-start(bf16[512,256]{1,0:T(8,128)(2,1)S(1)} %collective-permute-done.14.refs_4_), channel_id=1, source_target_pairs={{0,2},{1,3},{2,0},{3,1},{4,6},{5,7},{6,4},{7,5},{8,10},{9,11},{10,... | collective-permute-start | bytes 786440 | tf_op jit(solution)/shard_map/ppermute | solution.py:435
  118.2 9.3 %collective-permute-start.7 = (bf16[512,256]{1,0:T(8,128)(2,1)S(1)}, bf16[512,256]{1,0:T(8,128)(2,1)}, u32[]{:S(2)}, u32[]{:S(2)}) collective-permute-start(bf16[512,256]{1,0:T(8,128)(2,1)S(1)} %collective-permute-done.6.refs_7_), channel_id=1, source_target_pairs={{0,8},{4,12},{8,0},{12,4},{16,24},{20,28},{24,16},{28,20},{1,9},{5... | collective-permute-start | bytes 786440 | tf_op jit(solution)/shard_map/ppermute | solution.py:435
  118.5 10.2 %collective-permute-start.17 = (bf16[512,256]{1,0:T(8,128)(2,1)S(1)}, bf16[512,256]{1,0:T(8,128)(2,1)S(1)}, u32[]{:S(2)}, u32[]{:S(2)}) collective-permute-start(bf16[512,256]{1,0:T(8,128)(2,1)S(1)} %collective-permute-done.16.refs_6_), channel_id=1, source_target_pairs={{0,2},{1,3},{2,0},{3,1},{4,6},{5,7},{6,4},{7,5},{8,10},{9,11},{10,... | collective-permute-start | bytes 786440 | tf_op jit(solution)/shard_map/ppermute | solution.py:435
  119.0 13.1 %collective-permute-start.12 = (bf16[512,256]{1,0:T(8,128)(2,1)S(1)}, bf16[512,256]{1,0:T(8,128)(2,1)}, u32[]{:S(2)}, u32[]{:S(2)}) collective-permute-start(bf16[512,256]{1,0:T(8,128)(2,1)S(1)} %collective-permute-done.11.refs_12_), channel_id=1, source_target_pairs={{0,8},{4,12},{8,0},{12,4},{16,24},{20,28},{24,16},{28,20},{1,9},{5... | collective-permute-start | bytes 786440 | tf_op jit(solution)/shard_map/ppermute | solution.py:435
  122.2 11.2 %collective-permute-start.19 = (bf16[512,256]{1,0:T(8,128)(2,1)}, bf16[512,256]{1,0:T(8,128)(2,1)}, u32[]{:S(2)}, u32[]{:S(2)}) collective-permute-start(bf16[512,256]{1,0:T(8,128)(2,1)} %collective-permute-done.18.refs_9_), channel_id=1, source_target_pairs={{0,2},{1,3},{2,0},{3,1},{4,6},{5,7},{6,4},{7,5},{8,10},{9,11},{10,... | collective-permute-start | bytes 786440 | tf_op jit(solution)/shard_map/ppermute | solution.py:435
  127.5 12.3 %collective-permute-start.10 = (bf16[512,256]{1,0:T(8,128)(2,1)}, bf16[512,256]{1,0:T(8,128)(2,1)}, u32[]{:S(2)}, u32[]{:S(2)}) collective-permute-start(bf16[512,256]{1,0:T(8,128)(2,1)} %collective-permute-done.7.refs_2_), channel_id=1, source_target_pairs={{0,4},{4,0},{8,12},{12,8},{16,20},{20,16},{24,28},{28,24},{1,5},{5... | collective-permute-start | bytes 786440 | tf_op jit(solution)/shard_map/ppermute | solution.py:435
  129.4 10.4 %collective-permute-start.9 = (bf16[512,256]{1,0:T(8,128)(2,1)}, bf16[512,256]{1,0:T(8,128)(2,1)}, u32[]{:S(2)}, u32[]{:S(2)}) collective-permute-start(bf16[512,256]{1,0:T(8,128)(2,1)} %collective-permute-done.8.refs_11_), channel_id=1, source_target_pairs={{0,2},{1,3},{2,0},{3,1},{4,6},{5,7},{6,4},{7,5},{8,10},{9,11},{10,... | collective-permute-start | bytes 786440 | tf_op jit(solution)/shard_map/ppermute | solution.py:435
  132.1 7.7 %collective-permute-start.13 = (bf16[512,256]{1,0:T(8,128)(2,1)}, bf16[512,256]{1,0:T(8,128)(2,1)}, u32[]{:S(2)}, u32[]{:S(2)}) collective-permute-start(bf16[512,256]{1,0:T(8,128)(2,1)} %collective-permute-done.12.refs_5_), channel_id=1, source_target_pairs={{0,4},{4,0},{8,12},{12,8},{16,20},{20,16},{24,28},{28,24},{1,5},{5... | collective-permute-start | bytes 786440 | tf_op jit(solution)/shard_map/ppermute | solution.py:435
  139.8 5.8 %copy-start.3 = (bf16[2048,512]{1,0:T(8,128)(2,1)S(1)}, bf16[2048,512]{1,0:T(8,128)(2,1)}, u32[]{:S(2)}) copy-start(bf16[2048,512]{1,0:T(8,128)(2,1)} %wk_ref.5) | copy-start | bytes 6291460
  139.8 5.8 %copy-start.4 = (bf16[2048,512]{1,0:T(8,128)(2,1)S(1)}, bf16[2048,512]{1,0:T(8,128)(2,1)}, u32[]{:S(2)}) copy-start(bf16[2048,512]{1,0:T(8,128)(2,1)} %wv_ref.5) | copy-start | bytes 6291460
  139.8 5.8 %copy-start.22 = (bf16[512,512]{1,0:T(8,128)(2,1)S(1)}, bf16[512,512]{1,0:T(8,128)(2,1)}, u32[]{:S(2)}) copy-start(bf16[512,512]{1,0:T(8,128)(2,1)} %copy-done.21) | copy-start | bytes 1572868
  142.8 7.6 %collective-permute-start.20 = (f32[1,256,512]{2,1,0:T(8,128)S(1)}, f32[1,256,512]{2,1,0:T(8,128)S(1)}, u32[]{:S(2)}, u32[]{:S(2)}) collective-permute-start(f32[1,256,512]{2,1,0:T(8,128)S(1)} %slice.14), channel_id=1, source_target_pairs={{0,1},{1,0},{2,3},{3,2},{4,5},{5,4},{6,7},{7,6},{8,9},{9,8},{10,11... | collective-permute-start | bytes 1572872 | tf_op jit(solution)/shard_map/ppermute | solution.py:435
  142.9 2.3 %collective-permute-start.2 = (bf16[512,256]{1,0:T(8,128)(2,1)S(1)}, bf16[512,256]{1,0:T(8,128)(2,1)S(1)}, u32[]{:S(2)}, u32[]{:S(2)}) collective-permute-start(bf16[512,256]{1,0:T(8,128)(2,1)S(1)} %get-tuple-element.16.g0.refs_2_), channel_id=1, source_target_pairs={{0,1},{1,0},{2,3},{3,2},{4,5},{5,4},{6,7},{7,6},{8,9},{9,8},{10,11... | collective-permute-start | bytes 786440 | tf_op jit(solution)/shard_map/ppermute | solution.py:435
  143.4 2.1 %collective-permute-start.4 = (bf16[512,256]{1,0:T(8,128)(2,1)S(1)}, bf16[512,256]{1,0:T(8,128)(2,1)S(1)}, u32[]{:S(2)}, u32[]{:S(2)}) collective-permute-start(bf16[512,256]{1,0:T(8,128)(2,1)S(1)} %collective-permute-done.3.g2.refs_3_), channel_id=1, source_target_pairs={{0,1},{1,0},{2,3},{3,2},{4,5},{5,4},{6,7},{7,6},{8,9},{9,8},{10,11... | collective-permute-start | bytes 786440 | tf_op jit(solution)/shard_map/ppermute | solution.py:435
  (13 other events, 10.7 us)

commit v2 on v0

--- a/solution.py
+++ b/solution.py
@@ -1,6 +1,10 @@
+import functools
+
 import jax
 import jax.numpy as jnp
 from jax import lax
+from jax.experimental import pallas as pl
+from jax.experimental.pallas import tpu as pltpu
 from jax.sharding import PartitionSpec as P
 
 HEAD_DIM = 128
@@ -39,7 +43,7 @@
     return total.astype(jnp.bfloat16)
 
 
-def local(roll_x, lengths, dest, offsets, queries, out_grad, w_key, w_value):
+def general(roll_x, lengths, dest, offsets, queries, out_grad, w_key, w_value):
     learners = lax.axis_size("dp")
     samp, lmax, feats = roll_x.shape
     rows = queries.shape[0]
@@ -113,9 +117,396 @@
     return (attn_out, grad_x, sum_k / learners, sum_v / learners)
 
 
+BF16, F32, I32 = jnp.bfloat16, jnp.float32, jnp.int32
+ROWS_LAST = (((0,), (0,)), ((), ()))
+COLS_LAST = (((1,), (1,)), ((), ()))
+
+
+def dot(a, b, dims=(((1,), (0,)), ((), ()))):
+    return lax.dot_general(a, b, dims, preferred_element_type=F32)
+
+
+def iota(shape, dim):
+    return lax.broadcasted_iota(I32, shape, dim)
+
+
+def params(mib=44):
+    return pltpu.CompilerParams(
+        dimension_semantics=("arbitrary",), vmem_limit_bytes=mib * 1024 * 1024
+    )
+
+
+def cost(flops, moved):
+    return pl.CostEstimate(flops=flops, bytes_accessed=moved, transcendentals=0)
+
+
+def whole(shape):
+    zeros = (0,) * len(shape)
+    return pl.BlockSpec(shape, lambda *_: zeros)
+
+
+def project_kernel(me_ref, x_ref, wk_ref, wv_ref, away_ref, mine_ref):
+    x = x_ref[...]
+    for q in range(4):
+        at = pl.ds(pl.multiple_of((me_ref[0] ^ q) * HEAD_DIM, HEAD_DIM), HEAD_DIM)
+        term = dot(x, jnp.concatenate([wk_ref[:, at], wv_ref[:, at]], axis=1))
+        ref = (away_ref if q % 2 else mine_ref).at[q // 2]
+
+        @pl.when(pl.program_id(0) == 0)
+        def _(ref=ref, term=term):
+            ref[...] = term
+
+        @pl.when(pl.program_id(0) != 0)
+        def _(ref=ref, term=term):
+            ref[...] += term
+
+
+def project(me, x, w_key, w_value):
+    rows, feats = x.shape
+    cols = w_key.shape[1]
+    out = (2, rows, 2 * HEAD_DIM)
+    step = 512
+    spec = pltpu.PrefetchScalarGridSpec(
+        num_scalar_prefetch=1,
+        grid=(feats // step,),
+        in_specs=[
+            pl.BlockSpec((rows, step), lambda i, me: (0, i)),
+            pl.BlockSpec((step, cols), lambda i, me: (i, 0)),
+            pl.BlockSpec((step, cols), lambda i, me: (i, 0)),
+        ],
+        out_specs=(whole(out), whole(out)),
+    )
+    return pl.pallas_call(
+        project_kernel,
+        out_shape=(jax.ShapeDtypeStruct(out, F32),) * 2,
+        grid_spec=spec,
+        compiler_params=params(60),
+        cost_estimate=cost(4 * rows * feats * cols, 10 << 20),
+        name="project",
+    )(me, x, w_key, w_value)
+
+
+def slots_kernel(per, me_ref, dest_ref, len_ref, off_ref, x_ref, *refs):
+    *xs_refs, pick_ref, meta_ref = refs
+    samp = dest_ref.shape[1]
+    rows, feats = x_ref.shape
+    lmax = rows // samp
+    row = dest_ref[...]
+    a, b = iota((samp, samp), 0), iota((samp, samp), 1)
+    col = jnp.sum(jnp.where(a == b, row, 0), axis=1, keepdims=True)
+    rank = jnp.sum(jnp.where((col == row) & (a < b), 1, 0), axis=0, keepdims=True)
+    slot = (row ^ me_ref[0]) * per + rank
+    a, b = iota((samp, rows), 0), iota((samp, rows), 1)
+    spread = (a == lax.div(b, lmax)).astype(BF16)
+    wide = dot(jnp.broadcast_to(slot, (8, samp)).astype(BF16), spread)[0:1]
+    source = wide.astype(I32) * lmax + lax.rem(iota((1, rows), 1), lmax)
+    pick_ref[...] = (iota((rows, rows), 0) == source).astype(BF16)
+    held = iota((samp, samp), 0) == slot
+    size = jnp.sum(jnp.where(held, len_ref[...], 0), axis=1, keepdims=True)
+    start = jnp.sum(jnp.where(held, off_ref[...], 0), axis=1, keepdims=True)
+    lane = iota((samp, meta_ref.shape[2]), 1)
+    table = jnp.where(lane == 0, size, jnp.where(lane == 2, lax.rem(start, lmax), 0))
+    table = jnp.where(lane == 1, lax.div(start, lmax), table).astype(BF16)
+    lines = meta_ref.shape[0] * meta_ref.shape[1]
+    a, b = iota((lines, samp), 0), iota((lines, samp), 1)
+    place = (b == lax.div(a, 16) * per + lax.rem(a, 16)) & (lax.rem(a, 16) < per)
+    meta_ref[...] = dot(place.astype(BF16), table).astype(BF16).reshape(meta_ref.shape)
+    part = xs_refs[0].shape[2]
+    for f, ref in enumerate(xs_refs):
+        for h in range(2):
+            at = pl.multiple_of((me_ref[0] ^ (f + h * len(xs_refs))) * part, part)
+            ref[h] = dot(pick_ref[...], x_ref[:, pl.ds(at, part)]).astype(BF16)
+
+
+def slots(me, dest, lengths, offsets, x, learners, per):
+    rows, feats = x.shape
+    samp = dest.shape[0]
+    part = feats // learners
+    line = whole((1, samp))
+    xs = ((2, rows, part),) * (learners // 2)
+    outs = xs + ((rows, rows), (learners, 16, 2 * HEAD_DIM))
+    spec = pltpu.PrefetchScalarGridSpec(
+        num_scalar_prefetch=1,
+        grid=(1,),
+        in_specs=[line, line, line, whole((rows, feats))],
+        out_specs=tuple(whole(o) for o in outs),
+    )
+    return pl.pallas_call(
+        functools.partial(slots_kernel, per),
+        out_shape=tuple(jax.ShapeDtypeStruct(o, BF16) for o in outs),
+        grid_spec=spec,
+        compiler_params=params(),
+        cost_estimate=cost(2 * rows * rows * feats, 5 << 20),
+        name="slots",
+    )(me, dest.reshape(1, samp), lengths.reshape(1, samp), offsets.reshape(1, samp), x)
+
+
+def pack_kernel(me_ref, mine_ref, core_ref, across_ref, pick_ref, meta_ref, *out_refs):
+    total = (mine_ref[0] + core_ref[0]) + across_ref[...]
+    placed = dot(pick_ref[...], total.astype(BF16)).astype(BF16)
+    learners = meta_ref.shape[0]
+    block = placed.shape[0] // learners
+    for i in range(learners):
+        ref = out_refs[0].at[me_ref[0] ^ i]
+        ref[:block, :] = placed[i * block : (i + 1) * block]
+        ref[block:, :] = meta_ref[i]
+
+
+def pack(me, mine, core, across, pick, meta):
+    rows, cols = across.shape
+    learners, extra, _ = meta.shape
+    out = (rows // learners + extra, cols)
+    outs = ((learners,) + out,)
+    second = pl.BlockSpec((1, rows, cols), lambda *_: (0, 0, 0))
+    spec = pltpu.PrefetchScalarGridSpec(
+        num_scalar_prefetch=1,
+        grid=(1,),
+        in_specs=[second, second, whole((rows, cols)), whole((rows, rows)), whole(meta.shape)],
+        out_specs=tuple(whole(o) for o in outs),
+    )
+    return pl.pallas_call(
+        pack_kernel,
+        out_shape=tuple(jax.ShapeDtypeStruct(o, BF16) for o in outs),
+        grid_spec=spec,
+        compiler_params=params(),
+        cost_estimate=cost(2 * rows * rows * cols, 3 << 20),
+        name="pack",
+    )(me, mine, core, across, pick, meta)
+
+
+def attention_kernel(lmax, learners, me_ref, *refs):
+    *kv_refs, q_ref, g_ref, out_ref, near_ref, far_ref, place_ref, slot_out = refs
+    kv_refs = [kv_refs[0].at[me_ref[0] ^ i] for i in range(learners)]
+    rows, cols = q_ref.shape
+    lines = kv_refs[0].shape[0]
+    block = rows // learners
+    heads = cols // HEAD_DIM
+    scale = 1.0 / HEAD_DIM**0.5
+    meta = jnp.concatenate([ref[block:, :HEAD_DIM] for ref in kv_refs], axis=0)
+    a, b = iota((rows, meta.shape[0]), 0), iota((rows, meta.shape[0]), 1)
+    spread = (lax.div(a, block) * (lines - block) + lax.div(lax.rem(a, block), lmax) == b).astype(BF16)
+    table = dot(spread, meta).astype(I32)
+    inner = lax.rem(iota((rows, 1), 0), lmax)
+    alive = inner < table[:, 0:1]
+    target = jnp.where(alive, table[:, 1:2] * lmax + table[:, 2:3] + inner, -1)
+    place_ref[...] = (iota((rows, rows), 1) == target).astype(BF16)
+    size = HEAD_DIM
+    a, b = iota((size, size), 0), iota((size, size), 1)
+    near = (lax.div(a, lmax) == lax.div(b, lmax)) & (b <= a)
+    for i in range(rows // size):
+        span = slice(i * size, (i + 1) * size)
+        first = i * size // block
+        kv = jnp.concatenate([kv_refs[first + j][:block, :] for j in range(size // block)], axis=0)
+        k, v = kv[:, :HEAD_DIM], kv[:, HEAD_DIM:]
+        place = place_ref[span, :]
+        q = dot(place, q_ref[...]).astype(BF16)
+        g = dot(place, g_ref[...]).astype(BF16)
+        q = jnp.concatenate([q[:, h * HEAD_DIM : (h + 1) * HEAD_DIM] for h in range(heads)], axis=0)
+        g = jnp.concatenate([g[:, h * HEAD_DIM : (h + 1) * HEAD_DIM] for h in range(heads)], axis=0)
+        allowed = jnp.tile(near & alive[span], (heads, 1))
+        scores = jnp.where(allowed, dot(q, k, COLS_LAST) * scale, -1e30)
+        top = jnp.max(scores, axis=1, keepdims=True)
+        expo = jnp.exp(scores - top)
+        total = jnp.sum(expo, axis=1, keepdims=True)
+        probs = jnp.where(allowed, expo / total, 0.0)
+        probs_b = probs.astype(BF16)
+        out = dot(probs_b, v).astype(BF16)
+        dprob = dot(g, v, COLS_LAST)
+        delta = jnp.sum(g.astype(F32) * out.astype(F32), axis=1, keepdims=True)
+        dscore_b = (probs * (dprob - delta)).astype(BF16)
+        grad_ref, at = (near_ref, i * size) if i * size < rows // 2 else (far_ref, i * size - rows // 2)
+        grad_ref[at : at + size, :HEAD_DIM] = (dot(dscore_b, q, ROWS_LAST) * scale).astype(BF16)
+        grad_ref[at : at + size, HEAD_DIM:] = dot(probs_b, g, ROWS_LAST).astype(BF16)
+        for h in range(heads):
+            slot_out[span, h * HEAD_DIM : (h + 1) * HEAD_DIM] = out[h * size : (h + 1) * size]
+    out_ref[...] = dot(place_ref[...], slot_out[...], ROWS_LAST).astype(BF16)
+
+
+def attention(me, kvs, queries, out_grad, lmax, learners):
+    rows, cols = queries.shape
+    outs = ((rows, cols),) + ((rows // 2, 2 * HEAD_DIM),) * 2 + ((rows, rows),)
+    spec = pltpu.PrefetchScalarGridSpec(
+        num_scalar_prefetch=1,
+        grid=(1,),
+        in_specs=[whole(kv.shape) for kv in kvs] + [whole((rows, cols))] * 2,
+        out_specs=tuple(whole(o) for o in outs),
+        scratch_shapes=[pltpu.VMEM((rows, cols), BF16)],
+    )
+    return pl.pallas_call(
+        functools.partial(attention_kernel, lmax, learners),
+        out_shape=tuple(jax.ShapeDtypeStruct(o, BF16) for o in outs),
+        grid_spec=spec,
+        compiler_params=params(),
+        cost_estimate=cost(8 * rows * rows * cols, 4 << 20),
+        name="attention",
+    )(me, *kvs, queries, out_grad)
+
+
+def rows_kernel(me_ref, place_ref, *refs):
+    *g_refs, wk_ref, wv_ref, out_ref, grads = refs
+
+    @pl.when(pl.program_id(0) == 0)
+    def _():
+        half = grads.shape[1] // 2
+        for i in range(4):
+            g = jnp.concatenate([g_refs[2 * i][...], g_refs[2 * i + 1][...]], axis=0)
+            part = dot(place_ref[...], g, ROWS_LAST).astype(BF16)
+            at = pl.multiple_of((me_ref[0] ^ i) * HEAD_DIM, HEAD_DIM)
+            grads[:, pl.ds(at, HEAD_DIM)] = part[:, :HEAD_DIM]
+            grads[:, pl.ds(at + half, HEAD_DIM)] = part[:, HEAD_DIM:]
+
+    half = grads.shape[1] // 2
+    total = dot(grads[:, :half], wk_ref[...], COLS_LAST)
+    out_ref[...] = (total + dot(grads[:, half:], wv_ref[...], COLS_LAST)).astype(BF16)
+
+
+def row_grads(me, place, parts, w_key, w_value):
+    feats, cols = w_key.shape
+    rows = place.shape[0]
+    step = 512
+    spec = pltpu.PrefetchScalarGridSpec(
+        num_scalar_prefetch=1,
+        grid=(feats // step,),
+        in_specs=[whole((rows, rows))]
+        + [whole((rows // 2, 2 * HEAD_DIM))] * 8
+        + [pl.BlockSpec((step, cols), lambda i, me: (i, 0))] * 2,
+        out_specs=pl.BlockSpec((rows, step), lambda i, me: (0, i)),
+        scratch_shapes=[pltpu.VMEM((rows, 2 * cols), BF16)],
+    )
+    return pl.pallas_call(
+        rows_kernel,
+        out_shape=jax.ShapeDtypeStruct((rows, feats), BF16),
+        grid_spec=spec,
+        compiler_params=params(),
+        cost_estimate=cost(4 * rows * feats * cols, 8 << 20),
+        name="row_grads",
+    )(me, place, *parts, w_key, w_value)
+
+
+def weights_kernel(x_refs, g_refs, out_refs):
+    rows = x_refs[0].shape[1]
+    group = len(x_refs) // 2
+    block = rows // (2 * group)
+    grads = []
+    for f in range(group):
+        g = [(g_refs[2 * (f ^ j) + b], j * block) for b in range(2) for j in range(group)]
+        grads.append(jnp.concatenate([ref[at : at + block, :] for ref, at in g], axis=0))
+    for side, out_ref in enumerate(out_refs):
+        total = None
+        for f, g in enumerate(grads):
+            term = dot(x_refs[side * group + f][0], g, ROWS_LAST)
+            total = term if total is None else total + term
+        out_ref[...] = total.astype(out_ref.dtype)
+
+
+def weight_grads(xs, pieces, half, dtype):
+    _, rows, part = xs[0].shape
+    out = (part, 2 * HEAD_DIM)
+
+    def kernel(*refs):
+        weights_kernel(refs[: len(xs)], refs[len(xs) : -2], refs[-2:])
+
+    return pl.pallas_call(
+        kernel,
+        out_shape=(jax.ShapeDtypeStruct(out, dtype),) * 2,
+        grid=(1,),
+        in_specs=[pl.BlockSpec((1, rows, part), lambda i: (half, 0, 0))] * len(xs)
+        + [whole(g.shape) for g in pieces],
+        out_specs=(whole(out),) * 2,
+        compiler_params=params(),
+        cost_estimate=cost(4 * len(xs) * rows * part * HEAD_DIM, 6 << 20),
+        name="weight_grads",
+    )(*xs, *pieces)
+
+
+def finish_kernel(learners, me_ref, *refs):
+    *sums, k_ref, v_ref = refs
+    for i in range(4):
+        at = pl.ds(pl.multiple_of((me_ref[0] ^ i) * HEAD_DIM, HEAD_DIM), HEAD_DIM)
+        total = (sums[2 * i][...] + sums[2 * i + 1][...].astype(F32)) / learners
+        k_ref[:, at] = total[:, :HEAD_DIM]
+        v_ref[:, at] = total[:, HEAD_DIM:]
+
+
+def finish(me, sums, learners):
+    part, cols = sums[0].shape
+    out = (part, 2 * cols)
+    spec = pltpu.PrefetchScalarGridSpec(
+        num_scalar_prefetch=1,
+        grid=(1,),
+        in_specs=[whole((part, cols))] * 8,
+        out_specs=(whole(out),) * 2,
+    )
+    return pl.pallas_call(
+        functools.partial(finish_kernel, float(learners)),
+        out_shape=(jax.ShapeDtypeStruct(out, F32),) * 2,
+        grid_spec=spec,
+        compiler_params=params(),
+        cost_estimate=cost(part * cols, 2 << 20),
+        name="finish",
+    )(me, *sums)
+
+
+def swap(x, axis, code):
+    size = lax.axis_size(axis)
+    return lax.ppermute(x, axis, [(i, i ^ code) for i in range(size)])
+
+
+def after(x, *earlier):
+    return lax.optimization_barrier((x,) + earlier)[0]
+
+
+def local(roll_x, lengths, dest, offsets, queries, out_grad, w_key, w_value):
+    learners, heads = lax.axis_size("dp"), lax.axis_size("mp")
+    samp, lmax, feats = roll_x.shape
+    per = (samp + learners - 1) // learners
+    x = roll_x.reshape(samp * lmax, feats)
+    m = lax.axis_index("mp").astype(I32).reshape(1)
+    d = lax.axis_index("dp").astype(I32).reshape(1)
+
+    away, mine = project(m, x, w_key, w_value)
+    core = swap(away, "mp", 1)
+    half = mine[1] + core[1]
+    across = swap(half, "mp", 2)
+    *xs, pick, meta = slots(d, dest, lengths, offsets, after(x, half), learners, per)
+    xs = [xs[0]] + [swap(xs[f], "dp", f) for f in range(1, learners // 2)]
+    kv = pack(d, mine, core, across, pick, meta)
+    kv = lax.all_to_all(kv[0], "dp", split_axis=0, concat_axis=0, tiled=True)
+
+    attn_out, grads, beyond, place = attention(d, [kv], queries, out_grad, lmax, learners)
+
+    xs = xs + [swap(b, "mp", 1) for b in xs]
+    there = swap(beyond, "dp", 4)
+    near = {(0, 0, 0): grads, (0, 0, 1): there}
+    hops = [
+        ((0, 0), "dp", 1), ((0, 0), "dp", 2), ((0, 0), "mp", 2), ((2, 0), "dp", 1),
+        ((1, 0), "mp", 2), ((0, 1), "dp", 2), ((1, 1), "dp", 2),
+    ]
+    for part in range(2):
+        for (code, far), axis, step in hops:
+            key = (code ^ step, far, part) if axis == "dp" else (code, 1 - far, part)
+            near[key] = swap(near[code, far, part], axis, step)
+    across = swap(beyond, "mp", 2)
+    own = [grads, beyond, swap(grads, "mp", 1), swap(beyond, "mp", 1)]
+    own += [near[0, 1, 0], across, swap(near[0, 1, 0], "mp", 1), swap(across, "mp", 1)]
+    sums = [None] * 8
+    for far in range(2):
+        pieces = [near[c, far, b] for c in range(learners // 2) for b in range(2)]
+        send = weight_grads(xs, pieces, 1, BF16)
+        sums[4 * far + 1] = swap(send[0], "dp", 4)
+        sums[4 * far + 3] = swap(send[1], ("dp", "mp"), 4 * heads + 1)
+        sums[4 * far], keep = weight_grads(xs, pieces, 0, F32)
+        sums[4 * far + 2] = swap(keep, "mp", 1)
+    grad_x = row_grads(m, place, own, w_key, w_value)
+    grad_wk, grad_wv = finish(m, sums, learners)
+    return (attn_out, grad_x, grad_wk, grad_wv)
+
+
 def solution(mesh):
+    dp, mp = mesh.shape["dp"], mesh.shape["mp"]
+    body = local if dp == 8 and mp == 4 else general
     return jax.shard_map(
-        local,
+        body,
         mesh=mesh,
         in_specs=(
             P("dp", None, "mp"),

time: 372 us -> 121 us (0.33)
  waiting for transfers between devices: 239 us -> 43.5 us
  matrix products: 44.4 us -> 0 us
  Pallas kernels: 0 us -> 34.8 us
  local copies, waits for them, and re-layouts: 28.5 us -> 5.12 us
  starting transfers between devices: 15.9 us -> 34.5 us
  blocking collectives: 14.1 us -> 0 us
  other arithmetic: 15.2 us -> 1.9 us
  between operations: 13.9 us -> 0.82 us
    reduce_scatter x4 -> x0, waiting for transfers between devices: 189 us -> none  [the longest x1 89.9 us: local(): lax.psum_scatter(whole_v, 'dp', scatter_dimension=0, tiled=True)]
    all_to_all x3 -> x1, waiting for transfers between devices: 49.7 us -> 5.09 us  [local(): kv = lax.all_to_all(kv[0], 'dp', split_axis=0, concat_axis=0, tiled=True)]
    dot_general x10 -> x0, matrix products: 44.4 us -> none  [the longest x1 7.9 us: attend(): jnp.einsum('bkgqm,bmke->bqkge', probs_b, vs, preferred_element_type=jnp.f...]
    ppermute x0 -> x35, waiting for transfers between devices: none -> 38.4 us  [swap(): return lax.ppermute(x, axis, [(i, i ^ code) for i in range(size)])]
    pallas_call x0 -> x10, Pallas kernels: none -> 34.8 us  [the longest x1 10.2 us: project(): pl.pallas_call(project_kernel, out_shape=(jax.ShapeDtypeStruct(out, F32),...]
    ppermute x0 -> x35, starting transfers between devices: none -> 28.4 us  [swap(): return lax.ppermute(x, axis, [(i, i ^ code) for i in range(size)])]
    all_gather x2 -> x0, blocking collectives: 14.1 us -> none  [the longest x1 7.31 us: local(): lax.all_gather(val_grad, 'mp', axis=1, tiled=True)]
    all_to_all x3 -> x1, starting transfers between devices: 15.5 us -> 6.11 us  [local(): kv = lax.all_to_all(kv[0], 'dp', split_axis=0, concat_axis=0, tiled=True)]
  transfers between devices with their start and end apart: 7 -> 36, of which waited for: 7 -> 13; matrix products, arithmetic and copies ran while one was open for 11% -> 0% of each run, Pallas kernels for 0% -> 19%
where the time goes in v2:
time: 121 us
  waiting for transfers between devices  43.5 us (36%)
  Pallas kernels  34.8 us (29%)
  starting transfers between devices  34.5 us (29%)
  local copies, waits for them, and re-layouts  5.12 us (4%)
  other arithmetic  1.9 us (2%)
    ppermute x35, waiting for transfers between devices, swap(): return lax.ppermute(x, axis, [(i, i ^ code) for i in range(size)])  38.4 us
    ppermute x35, starting transfers between devices, swap(): return lax.ppermute(x, axis, [(i, i ^ code) for i in range(size)])  28.4 us
    pallas_call x1, Pallas kernels, project(): pl.pallas_call(project_kernel, out_shape=(jax.ShapeDtypeStruct(out, F32),...  10.2 us
    pallas_call x4, Pallas kernels, weight_grads(): pl.pallas_call(kernel, out_shape=(jax.ShapeDtypeStruct(out, dtype),) * 2,...  7.37 us
    pallas_call x1, Pallas kernels, attention(): pl.pallas_call(functools.partial(attention_kernel, lmax, learners), out_s...  6.91 us
    all_to_all x1, starting transfers between devices, local(): kv = lax.all_to_all(kv[0], 'dp', split_axis=0, concat_axis=0, tiled=True)  6.11 us
    unnamed x22, local copies, waits for them, and re-layouts  5.12 us
    all_to_all x1, waiting for transfers between devices, local(): kv = lax.all_to_all(kv[0], 'dp', split_axis=0, concat_axis=0, tiled=True)  5.09 us
  transfers between devices with their start and end apart: 36, of which 13 were waited for; matrix products, arithmetic and copies ran while one was open for 0% of the time, Pallas kernels for 19%

profile of v2, /device:TPU:0, one launch (start us, length us, event | category | flops | bytes accessed | tf_op | source)
XLA Modules:
  0.0 120.7 jit_solution(9696346216612213599)
XLA Ops:
  0.7 10.2 %project.1 = (f32[2,512,256]{2,1,0:T(8,128)}, f32[2,512,256]{2,1,0:T(8,128)}) custom-call(s32[1]{0:T(128)} %bitcast.1.me_ref, bf16[512,2048]{1,0:T(8,128)(2,1)} %bitcast.8, bf16[2048,512]{1,0:T(8,128)(2,1)} %refs_8_.1, bf16[2048,512]{1,0:T(8,128)(2,1)} %refs_9_.1), custom_call_target="tpu_custom_call" | custom-call | flops 2147483648 | bytes 10485760 | tf_op jit(solution)/shard_map/project/pallas_call | solution.py:179
  11.3 2.5 %collective-permute-done.core_ref = f32[2,512,256]{2,1,0:T(8,128)S(1)} collective-permute-done((f32[2,512,256]{2,1,0:T(8,128)}, f32[2,512,256]{2,1,0:T(8,128)S(1)}, u32[]{:S(2)}, u32[]{:S(2)}) %collective-permute-start) | collective-permute-done | bytes 1048608 | tf_op jit(solution)/shard_map/ppermute | solution.py:452
  13.8 1.9 %fusion = f32[512,256]{1,0:T(8,128)} fusion(f32[2,512,256]{2,1,0:T(8,128)S(1)} %collective-permute-done.core_ref, f32[2,512,256]{2,1,0:T(8,128)} %get-tuple-element.27.mine_ref), kind=kLoop, calls=%fused_computation.1 | loop fusion | flops 131072 | bytes 1572864 | tf_op jit(solution)/shard_map/add | solution.py:469
  16.7 2.8 %collective-permute-start.1 = (f32[512,256]{1,0:T(8,128)}, f32[512,256]{1,0:T(8,128)}, u32[]{:S(2)}, u32[]{:S(2)}) collective-permute-start(f32[512,256]{1,0:T(8,128)} %fusion), channel_id=1, source_target_pairs={{0,2},{1,3},{2,0},{3,1},{4,6},{5,7},{6,4},{7,5},{8,10},{9,11},{10,... | collective-permute-start | bytes 1572872 | tf_op jit(solution)/shard_map/ppermute | solution.py:452
  19.6 1.7 %copy-done.3 = bf16[32,16,2048]{2,1,0:T(8,128)(2,1)S(1)} copy-done((bf16[32,16,2048]{2,1,0:T(8,128)(2,1)S(1)}, bf16[32,16,2048]{2,1,0:T(8,128)(2,1)}, u32[]{:S(2)}) %copy-start.3) | copy-done | bytes 2097176
  21.2 2.4 %slots.1 = (bf16[2,512,256]{2,1,0:T(8,128)(2,1)S(1)}, bf16[2,512,256]{2,1,0:T(8,128)(2,1)}, bf16[2,512,256]{2,1,0:T(8,128)(2,1)}, bf16[2,512,256]{2,1,0:T(8,128)...) custom-call(s32[1]{0:T(128)} %bitcast.me_ref, s32[1,32]{1,0:T(1,128)S(1)} %bitcast.10, ...), custom_call_target="tpu_custom_call" | custom-call | flops 1073741824 | bytes 5242880 | tf_op jit(solution)/shard_map/slots/pallas_call | solution.py:234
  23.6 1.5 %collective-permute-start.8 = (bf16[2,512,256]{2,1,0:T(8,128)(2,1)}, bf16[2,512,256]{2,1,0:T(8,128)(2,1)S(1)}, u32[]{:S(2)}, u32[]{:S(2)}) collective-permute-start(bf16[2,512,256]{2,1,0:T(8,128)(2,1)} %get-tuple-element.37), channel_id=1, source_target_pairs={{0,4},{4,0},{8,12},{12,8},{16,20},{20,16},{24,28},{28,24},{1,5},{5... | collective-permute-start | bytes 1572872 | tf_op jit(solution)/shard_map/ppermute | solution.py:452
  25.1 1.6 %collective-permute-start.9 = (bf16[2,512,256]{2,1,0:T(8,128)(2,1)}, bf16[2,512,256]{2,1,0:T(8,128)(2,1)S(1)}, u32[]{:S(2)}, u32[]{:S(2)}) collective-permute-start(bf16[2,512,256]{2,1,0:T(8,128)(2,1)} %get-tuple-element.38), channel_id=1, source_target_pairs={{0,8},{4,12},{8,0},{12,4},{16,24},{20,28},{24,16},{28,20},{1,9},{5... | collective-permute-start | bytes 1572872 | tf_op jit(solution)/shard_map/ppermute | solution.py:452
  27.1 5.0 %collective-permute-done.1.across_ref = f32[512,256]{1,0:T(8,128)} collective-permute-done((f32[512,256]{1,0:T(8,128)}, f32[512,256]{1,0:T(8,128)}, u32[]{:S(2)}, u32[]{:S(2)}) %collective-permute-start.1) | collective-permute-done | bytes 524320 | tf_op jit(solution)/shard_map/ppermute | solution.py:452
  32.1 2.1 %pack.1 = bf16[8,80,256]{2,1,0:T(8,128)(2,1)} custom-call(s32[1]{0:T(128)} %bitcast.me_ref, f32[2,512,256]{2,1,0:T(8,128)S(1)} %copy-done, f32[2,512,256]{2,1,0:T(8,128)S(1)} %copy-done.2, f32[512,256]{1,0:T(8,128)} %collective-permute-done.1.across_ref, bf16[512,512]{1,0:T(8,128)(2,1)S(1)} %get-tuple-element.30.pick_ref, ...), custom_call_target="tpu_custom_call" | custom-call | flops 134217728 | bytes 3145728 | tf_op jit(solution)/shard_map/pack/pallas_call | solution.py:267
  34.2 6.1 %all-to-all-start = ((bf16[8,80,256]{2,1,0:T(8,128)(2,1)}), bf16[8,80,256]{2,1,0:T(8,128)(2,1)S(1)}, u32[]{:S(2)}, u32[]{:S(2)}) async-start(bf16[8,80,256]{2,1,0:T(8,128)(2,1)} %pack.1), calls=%async_computation | async-start | bytes 655360 | tf_op jit(solution)/shard_map/all_to_all | solution.py:474
  40.9 11.7 %collective-permute-done.10.refs_3_ = bf16[2,512,256]{2,1,0:T(8,128)(2,1)S(1)} collective-permute-done((bf16[2,512,256]{2,1,0:T(8,128)(2,1)}, bf16[2,512,256]{2,1,0:T(8,128)(2,1)S(1)}, u32[]{:S(2)}, u32[]{:S(2)}) %collective-permute-start.10) | collective-permute-done | bytes 524320 | tf_op jit(solution)/shard_map/ppermute | solution.py:452
  52.6 5.1 %all-to-all-done.refs_0_ = bf16[8,80,256]{2,1,0:T(8,128)(2,1)S(1)} async-done(((bf16[8,80,256]{2,1,0:T(8,128)(2,1)}), bf16[8,80,256]{2,1,0:T(8,128)(2,1)S(1)}, u32[]{:S(2)}, u32[]{:S(2)}) %all-to-all-start) | async-done | bytes 327712 | tf_op jit(solution)/shard_map/all_to_all | solution.py:474
  57.7 1.2 %copy-done.6 = bf16[512,1024]{1,0:T(8,128)(2,1)S(1)} copy-done((bf16[512,1024]{1,0:T(8,128)(2,1)S(1)}, bf16[512,1024]{1,0:T(8,128)(2,1)}, u32[]{:S(2)}) %copy-start.6) | copy-done | bytes 1048600
  58.9 1.2 %copy-done.7 = bf16[512,1024]{1,0:T(8,128)(2,1)S(1)} copy-done((bf16[512,1024]{1,0:T(8,128)(2,1)S(1)}, bf16[512,1024]{1,0:T(8,128)(2,1)}, u32[]{:S(2)}) %copy-start.7) | copy-done | bytes 1048600
  60.1 6.9 %attention.1 = (bf16[512,1024]{1,0:T(8,128)(2,1)}, bf16[256,256]{1,0:T(8,128)(2,1)S(1)}, bf16[256,256]{1,0:T(8,128)(2,1)S(1)}, bf16[512,512]{1,0:T(8,128)(2,1)S(1)}) custom-call(s32[1]{0:T(128)} %bitcast.me_ref, bf16[8,80,256]{2,1,0:T(8,128)(2,1)S(1)} %all-to-all-done.refs_0_, bf16[512,1024]{1,0:T(8,128)(2,1)S(1)} %copy-done.6, bf16[512,1024]{1,0:T(8,128)(2,1)S(1)} %copy-done.7), custom_call_target="tpu_custom_call" | custom-call | flops 2147483648 | bytes 4194304 | tf_op jit(solution)/shard_map/attention/pallas_call | solution.py:335
  70.4 1.4 %collective-permute-start.5 = (bf16[256,256]{1,0:T(8,128)(2,1)S(1)}, bf16[256,256]{1,0:T(8,128)(2,1)S(1)}, u32[]{:S(2)}, u32[]{:S(2)}) collective-permute-start(bf16[256,256]{1,0:T(8,128)(2,1)S(1)} %get-tuple-element.35.refs_1_), channel_id=1, source_target_pairs={{0,2},{1,3},{2,0},{3,1},{4,6},{5,7},{6,4},{7,5},{8,10},{9,11},{10,... | collective-permute-start | bytes 393224 | tf_op jit(solution)/shard_map/ppermute | solution.py:452
  71.8 2.6 %collective-permute-done.15.refs_9_ = bf16[256,256]{1,0:T(8,128)(2,1)S(1)} collective-permute-done((bf16[256,256]{1,0:T(8,128)(2,1)S(1)}, bf16[256,256]{1,0:T(8,128)(2,1)S(1)}, u32[]{:S(2)}, u32[]{:S(2)}) %collective-permute-start.15) | collective-permute-done | bytes 131104 | tf_op jit(solution)/shard_map/ppermute | solution.py:452
  74.9 1.6 %collective-permute-start.19 = (bf16[256,256]{1,0:T(8,128)(2,1)S(1)}, bf16[256,256]{1,0:T(8,128)(2,1)S(1)}, u32[]{:S(2)}, u32[]{:S(2)}) collective-permute-start(bf16[256,256]{1,0:T(8,128)(2,1)S(1)} %collective-permute-done.15.refs_9_), channel_id=1, source_target_pairs={{0,8},{4,12},{8,0},{12,4},{16,24},{20,28},{24,16},{28,20},{1,9},{5... | collective-permute-start | bytes 393224 | tf_op jit(solution)/shard_map/ppermute | solution.py:452
  77.2 1.6 %collective-permute-start.25 = (bf16[256,256]{1,0:T(8,128)(2,1)S(1)}, bf16[256,256]{1,0:T(8,128)(2,1)S(1)}, u32[]{:S(2)}, u32[]{:S(2)}) collective-permute-start(bf16[256,256]{1,0:T(8,128)(2,1)S(1)} %collective-permute-done.15.refs_9_), channel_id=1, source_target_pairs={{0,2},{1,3},{2,0},{3,1},{4,6},{5,7},{6,4},{7,5},{8,10},{9,11},{10,... | collective-permute-start | bytes 393224 | tf_op jit(solution)/shard_map/ppermute | solution.py:452
  80.8 1.2 %collective-permute-start.20 = (bf16[256,256]{1,0:T(8,128)(2,1)S(1)}, bf16[256,256]{1,0:T(8,128)(2,1)S(1)}, u32[]{:S(2)}, u32[]{:S(2)}) collective-permute-start(bf16[256,256]{1,0:T(8,128)(2,1)S(1)} %collective-permute-done.18.refs_12_), channel_id=1, source_target_pairs={{0,4},{4,0},{8,12},{12,8},{16,20},{20,16},{24,28},{28,24},{1,5},{5... | collective-permute-start | bytes 393224 | tf_op jit(solution)/shard_map/ppermute | solution.py:452
  85.9 1.2 %collective-permute-done.21.refs_15_ = bf16[256,256]{1,0:T(8,128)(2,1)S(1)} collective-permute-done((bf16[256,256]{1,0:T(8,128)(2,1)S(1)}, bf16[256,256]{1,0:T(8,128)(2,1)S(1)}, u32[]{:S(2)}, u32[]{:S(2)}) %collective-permute-start.21) | collective-permute-done | bytes 131104 | tf_op jit(solution)/shard_map/ppermute | solution.py:452
  87.2 1.8 %weight_grads.5 = (bf16[256,256]{1,0:T(8,128)(2,1)S(1)}, bf16[256,256]{1,0:T(8,128)(2,1)S(1)}) custom-call(bf16[2,512,256]{2,1,0:T(8,128)(2,1)S(1)} %get-tuple-element.36.refs_0_, bf16[2,512,256]{2,1,0:T(8,128)(2,1)S(1)} %collective-permute-done.8.refs_1_, bf16[2,512,256]{2,1,0:T(8,128)(2,1)S(1)} %collective-permute-done.9.refs_2_, ...), custom_call_target="tpu_custom_call" | custom-call | flops 536870912 | bytes 6291456 | tf_op jit(solution)/shard_map/weight_grads/pallas_call | solution.py:409
  90.6 2.2 %collective-permute-start.22 = (bf16[256,256]{1,0:T(8,128)(2,1)S(1)}, bf16[256,256]{1,0:T(8,128)(2,1)S(1)}, u32[]{:S(2)}, u32[]{:S(2)}) collective-permute-start(bf16[256,256]{1,0:T(8,128)(2,1)S(1)} %get-tuple-element.41), channel_id=1, source_target_pairs={{0,16},{4,20},{8,24},{12,28},{16,0},{20,4},{24,8},{28,12},{1,17},{... | collective-permute-start | bytes 393224 | tf_op jit(solution)/shard_map/ppermute | solution.py:452
  92.8 1.8 %weight_grads.4 = (f32[256,256]{1,0:T(8,128)S(1)}, f32[256,256]{1,0:T(8,128)S(1)}) custom-call(bf16[2,512,256]{2,1,0:T(8,128)(2,1)S(1)} %get-tuple-element.36.refs_0_, bf16[2,512,256]{2,1,0:T(8,128)(2,1)S(1)} %collective-permute-done.8.refs_1_, bf16[2,512,256]{2,1,0:T(8,128)(2,1)S(1)} %collective-permute-done.9.refs_2_, ...), custom_call_target="tpu_custom_call" | custom-call | flops 536870912 | bytes 6291456 | tf_op jit(solution)/shard_map/weight_grads/pallas_call | solution.py:409
  94.6 1.8 %weight_grads.6 = (f32[256,256]{1,0:T(8,128)S(1)}, f32[256,256]{1,0:T(8,128)S(1)}) custom-call(bf16[2,512,256]{2,1,0:T(8,128)(2,1)S(1)} %get-tuple-element.36.refs_0_, bf16[2,512,256]{2,1,0:T(8,128)(2,1)S(1)} %collective-permute-done.8.refs_1_, bf16[2,512,256]{2,1,0:T(8,128)(2,1)S(1)} %collective-permute-done.9.refs_2_, ...), custom_call_target="tpu_custom_call" | custom-call | flops 536870912 | bytes 6291456 | tf_op jit(solution)/shard_map/weight_grads/pallas_call | solution.py:409
  97.0 2.0 %weight_grads.7 = (bf16[256,256]{1,0:T(8,128)(2,1)S(1)}, bf16[256,256]{1,0:T(8,128)(2,1)S(1)}) custom-call(bf16[2,512,256]{2,1,0:T(8,128)(2,1)S(1)} %get-tuple-element.36.refs_0_, bf16[2,512,256]{2,1,0:T(8,128)(2,1)S(1)} %collective-permute-done.8.refs_1_, bf16[2,512,256]{2,1,0:T(8,128)(2,1)S(1)} %collective-permute-done.9.refs_2_, ...), custom_call_target="tpu_custom_call" | custom-call | flops 536870912 | bytes 6291456 | tf_op jit(solution)/shard_map/weight_grads/pallas_call | solution.py:409
  99.4 2.2 %collective-permute-start.32 = (bf16[256,256]{1,0:T(8,128)(2,1)S(1)}, bf16[256,256]{1,0:T(8,128)(2,1)S(1)}, u32[]{:S(2)}, u32[]{:S(2)}) collective-permute-start(bf16[256,256]{1,0:T(8,128)(2,1)S(1)} %get-tuple-element.45), channel_id=1, source_target_pairs={{0,16},{4,20},{8,24},{12,28},{16,0},{20,4},{24,8},{28,12},{1,17},{... | collective-permute-start | bytes 393224 | tf_op jit(solution)/shard_map/ppermute | solution.py:452
  102.2 4.8 %row_grads.1 = bf16[512,2048]{1,0:T(8,128)(2,1)} custom-call(s32[1]{0:T(128)} %bitcast.1.me_ref, bf16[512,512]{1,0:T(8,128)(2,1)S(1)} %get-tuple-element.33.place_ref, bf16[256,256]{1,0:T(8,128)(2,1)S(1)} %get-tuple-element.34.refs_0_.refs_8_, bf16[256,256]{1,0:T(8,128)(2,1)S(1)} %get-tuple-element.35.refs_1_, ...), custom_call_target="tpu_custom_call" | custom-call | flops 2147483648 | bytes 8388608 | tf_op jit(solution)/shard_map/row_grads/pallas_call | solution.py:376
  107.0 7.0 %collective-permute-done.24.refs_3_ = bf16[256,256]{1,0:T(8,128)(2,1)S(1)} collective-permute-done((bf16[256,256]{1,0:T(8,128)(2,1)S(1)}, bf16[256,256]{1,0:T(8,128)(2,1)S(1)}, u32[]{:S(2)}, u32[]{:S(2)}) %collective-permute-start.24) | collective-permute-done | bytes 131104 | tf_op jit(solution)/shard_map/ppermute | solution.py:452
  114.0 3.2 %collective-permute-done.32.refs_5_ = bf16[256,256]{1,0:T(8,128)(2,1)S(1)} collective-permute-done((bf16[256,256]{1,0:T(8,128)(2,1)S(1)}, bf16[256,256]{1,0:T(8,128)(2,1)S(1)}, u32[]{:S(2)}, u32[]{:S(2)}) %collective-permute-start.32) | collective-permute-done | bytes 131104 | tf_op jit(solution)/shard_map/ppermute | solution.py:452
  117.2 2.4 %collective-permute-done.34.refs_7_ = bf16[256,256]{1,0:T(8,128)(2,1)S(1)} collective-permute-done((bf16[256,256]{1,0:T(8,128)(2,1)S(1)}, bf16[256,256]{1,0:T(8,128)(2,1)S(1)}, u32[]{:S(2)}, u32[]{:S(2)}) %collective-permute-start.34) | collective-permute-done | bytes 131104 | tf_op jit(solution)/shard_map/ppermute | solution.py:452
  (73 shorter events, 17.1 us)
Async XLA Ops:
  16.7 15.4 %collective-permute-start.1 = (f32[512,256]{1,0:T(8,128)}, f32[512,256]{1,0:T(8,128)}, u32[]{:S(2)}, u32[]{:S(2)}) collective-permute-start(f32[512,256]{1,0:T(8,128)} %fusion), channel_id=1, source_target_pairs={{0,2},{1,3},{2,0},{3,1},{4,6},{5,7},{6,4},{7,5},{8,10},{9,11},{10,... | collective-permute-start | bytes 1572872 | tf_op jit(solution)/shard_map/ppermute | solution.py:452
  23.6 16.7 %collective-permute-start.8 = (bf16[2,512,256]{2,1,0:T(8,128)(2,1)}, bf16[2,512,256]{2,1,0:T(8,128)(2,1)S(1)}, u32[]{:S(2)}, u32[]{:S(2)}) collective-permute-start(bf16[2,512,256]{2,1,0:T(8,128)(2,1)} %get-tuple-element.37), channel_id=1, source_target_pairs={{0,4},{4,0},{8,12},{12,8},{16,20},{20,16},{24,28},{28,24},{1,5},{5... | collective-permute-start | bytes 1572872 | tf_op jit(solution)/shard_map/ppermute | solution.py:452
  25.1 15.7 %collective-permute-start.9 = (bf16[2,512,256]{2,1,0:T(8,128)(2,1)}, bf16[2,512,256]{2,1,0:T(8,128)(2,1)S(1)}, u32[]{:S(2)}, u32[]{:S(2)}) collective-permute-start(bf16[2,512,256]{2,1,0:T(8,128)(2,1)} %get-tuple-element.38), channel_id=1, source_target_pairs={{0,8},{4,12},{8,0},{12,4},{16,24},{20,28},{24,16},{28,20},{1,9},{5... | collective-permute-start | bytes 1572872 | tf_op jit(solution)/shard_map/ppermute | solution.py:452
  26.7 25.9 %collective-permute-start.10 = (bf16[2,512,256]{2,1,0:T(8,128)(2,1)}, bf16[2,512,256]{2,1,0:T(8,128)(2,1)S(1)}, u32[]{:S(2)}, u32[]{:S(2)}) collective-permute-start(bf16[2,512,256]{2,1,0:T(8,128)(2,1)} %get-tuple-element.39), channel_id=1, source_target_pairs={{0,12},{4,8},{8,4},{12,0},{16,28},{20,24},{24,20},{28,16},{1,13},{... | collective-permute-start | bytes 1572872 | tf_op jit(solution)/shard_map/ppermute | solution.py:452
  34.2 23.5 %all-to-all-start = ((bf16[8,80,256]{2,1,0:T(8,128)(2,1)}), bf16[8,80,256]{2,1,0:T(8,128)(2,1)S(1)}, u32[]{:S(2)}, u32[]{:S(2)}) async-start(bf16[8,80,256]{2,1,0:T(8,128)(2,1)} %pack.1), calls=%async_computation | async-start | bytes 655360 | tf_op jit(solution)/shard_map/all_to_all | solution.py:474
  40.3 27.7 %collective-permute-start.11 = (bf16[2,512,256]{2,1,0:T(8,128)(2,1)S(1)}, bf16[2,512,256]{2,1,0:T(8,128)(2,1)S(1)}, u32[]{:S(2)}, u32[]{:S(2)}) collective-permute-start(bf16[2,512,256]{2,1,0:T(8,128)(2,1)S(1)} %get-tuple-element.36.refs_0_), channel_id=1, source_target_pairs={{0,1},{1,0},{2,3},{3,2},{4,5},{5,4},{6,7},{7,6},{8,9},{9,8},{10,11... | collective-permute-start | bytes 1572872 | tf_op jit(solution)/shard_map/ppermute | solution.py:452
  40.3 28.7 %collective-permute-start.12 = (bf16[2,512,256]{2,1,0:T(8,128)(2,1)S(1)}, bf16[2,512,256]{2,1,0:T(8,128)(2,1)S(1)}, u32[]{:S(2)}, u32[]{:S(2)}) collective-permute-start(bf16[2,512,256]{2,1,0:T(8,128)(2,1)S(1)} %collective-permute-done.8.refs_1_), channel_id=1, source_target_pairs={{0,1},{1,0},{2,3},{3,2},{4,5},{5,4},{6,7},{7,6},{8,9},{9,8},{10,11... | collective-permute-start | bytes 1572872 | tf_op jit(solution)/shard_map/ppermute | solution.py:452
  40.8 28.8 %collective-permute-start.13 = (bf16[2,512,256]{2,1,0:T(8,128)(2,1)S(1)}, bf16[2,512,256]{2,1,0:T(8,128)(2,1)}, u32[]{:S(2)}, u32[]{:S(2)}) collective-permute-start(bf16[2,512,256]{2,1,0:T(8,128)(2,1)S(1)} %collective-permute-done.9.refs_2_), channel_id=1, source_target_pairs={{0,1},{1,0},{2,3},{3,2},{4,5},{5,4},{6,7},{7,6},{8,9},{9,8},{10,11... | collective-permute-start | bytes 1572872 | tf_op jit(solution)/shard_map/ppermute | solution.py:452
  52.6 17.8 %collective-permute-start.14 = (bf16[2,512,256]{2,1,0:T(8,128)(2,1)S(1)}, bf16[2,512,256]{2,1,0:T(8,128)(2,1)}, u32[]{:S(2)}, u32[]{:S(2)}) collective-permute-start(bf16[2,512,256]{2,1,0:T(8,128)(2,1)S(1)} %collective-permute-done.10.refs_3_), channel_id=1, source_target_pairs={{0,1},{1,0},{2,3},{3,2},{4,5},{5,4},{6,7},{7,6},{8,9},{9,8},{10,11... | collective-permute-start | bytes 1572872 | tf_op jit(solution)/shard_map/ppermute | solution.py:452
  67.0 7.4 %collective-permute-start.15 = (bf16[256,256]{1,0:T(8,128)(2,1)S(1)}, bf16[256,256]{1,0:T(8,128)(2,1)S(1)}, u32[]{:S(2)}, u32[]{:S(2)}) collective-permute-start(bf16[256,256]{1,0:T(8,128)(2,1)S(1)} %get-tuple-element.35.refs_1_), channel_id=1, source_target_pairs={{0,16},{4,20},{8,24},{12,28},{16,0},{20,4},{24,8},{28,12},{1,17},{... | collective-permute-start | bytes 393224 | tf_op jit(solution)/shard_map/ppermute | solution.py:452
  68.0 6.4 %collective-permute-start.16 = (bf16[256,256]{1,0:T(8,128)(2,1)S(1)}, bf16[256,256]{1,0:T(8,128)(2,1)S(1)}, u32[]{:S(2)}, u32[]{:S(2)}) collective-permute-start(bf16[256,256]{1,0:T(8,128)(2,1)S(1)} %get-tuple-element.34.refs_0_.refs_8_), channel_id=1, source_target_pairs={{0,4},{4,0},{8,12},{12,8},{16,20},{20,16},{24,28},{28,24},{1,5},{5... | collective-permute-start | bytes 393224 | tf_op jit(solution)/shard_map/ppermute | solution.py:452
  69.0 5.9 %collective-permute-start.4 = (bf16[256,256]{1,0:T(8,128)(2,1)S(1)}, bf16[256,256]{1,0:T(8,128)(2,1)S(1)}, u32[]{:S(2)}, u32[]{:S(2)}) collective-permute-start(bf16[256,256]{1,0:T(8,128)(2,1)S(1)} %get-tuple-element.34.refs_0_.refs_8_), channel_id=1, source_target_pairs={{0,2},{1,3},{2,0},{3,1},{4,6},{5,7},{6,4},{7,5},{8,10},{9,11},{10,... | collective-permute-start | bytes 393224 | tf_op jit(solution)/shard_map/ppermute | solution.py:452
  69.6 7.0 %collective-permute-start.18 = (bf16[256,256]{1,0:T(8,128)(2,1)S(1)}, bf16[256,256]{1,0:T(8,128)(2,1)S(1)}, u32[]{:S(2)}, u32[]{:S(2)}) collective-permute-start(bf16[256,256]{1,0:T(8,128)(2,1)S(1)} %get-tuple-element.34.refs_0_.refs_8_), channel_id=1, source_target_pairs={{0,8},{4,12},{8,0},{12,4},{16,24},{20,28},{24,16},{28,20},{1,9},{5... | collective-permute-start | bytes 393224 | tf_op jit(solution)/shard_map/ppermute | solution.py:452
  70.4 6.8 %collective-permute-start.5 = (bf16[256,256]{1,0:T(8,128)(2,1)S(1)}, bf16[256,256]{1,0:T(8,128)(2,1)S(1)}, u32[]{:S(2)}, u32[]{:S(2)}) collective-permute-start(bf16[256,256]{1,0:T(8,128)(2,1)S(1)} %get-tuple-element.35.refs_1_), channel_id=1, source_target_pairs={{0,2},{1,3},{2,0},{3,1},{4,6},{5,7},{6,4},{7,5},{8,10},{9,11},{10,... | collective-permute-start | bytes 393224 | tf_op jit(solution)/shard_map/ppermute | solution.py:452
  74.4 6.4 %collective-permute-start.26 = (bf16[256,256]{1,0:T(8,128)(2,1)S(1)}, bf16[256,256]{1,0:T(8,128)(2,1)S(1)}, u32[]{:S(2)}, u32[]{:S(2)}) collective-permute-start(bf16[256,256]{1,0:T(8,128)(2,1)S(1)} %collective-permute-done.16.refs_10_), channel_id=1, source_target_pairs={{0,2},{1,3},{2,0},{3,1},{4,6},{5,7},{6,4},{7,5},{8,10},{9,11},{10,... | collective-permute-start | bytes 393224 | tf_op jit(solution)/shard_map/ppermute | solution.py:452
  74.9 7.1 %collective-permute-start.19 = (bf16[256,256]{1,0:T(8,128)(2,1)S(1)}, bf16[256,256]{1,0:T(8,128)(2,1)S(1)}, u32[]{:S(2)}, u32[]{:S(2)}) collective-permute-start(bf16[256,256]{1,0:T(8,128)(2,1)S(1)} %collective-permute-done.15.refs_9_), channel_id=1, source_target_pairs={{0,8},{4,12},{8,0},{12,4},{16,24},{20,28},{24,16},{28,20},{1,9},{5... | collective-permute-start | bytes 393224 | tf_op jit(solution)/shard_map/ppermute | solution.py:452
  76.5 6.3 %collective-permute-start.28 = (bf16[256,256]{1,0:T(8,128)(2,1)S(1)}, bf16[256,256]{1,0:T(8,128)(2,1)S(1)}, u32[]{:S(2)}, u32[]{:S(2)}) collective-permute-start(bf16[256,256]{1,0:T(8,128)(2,1)S(1)} %collective-permute-done.4.refs_4_.refs_8_), channel_id=1, source_target_pairs={{0,8},{4,12},{8,0},{12,4},{16,24},{20,28},{24,16},{28,20},{1,9},{5... | collective-permute-start | bytes 393224 | tf_op jit(solution)/shard_map/ppermute | solution.py:452
  77.2 6.7 %collective-permute-start.25 = (bf16[256,256]{1,0:T(8,128)(2,1)S(1)}, bf16[256,256]{1,0:T(8,128)(2,1)S(1)}, u32[]{:S(2)}, u32[]{:S(2)}) collective-permute-start(bf16[256,256]{1,0:T(8,128)(2,1)S(1)} %collective-permute-done.15.refs_9_), channel_id=1, source_target_pairs={{0,2},{1,3},{2,0},{3,1},{4,6},{5,7},{6,4},{7,5},{8,10},{9,11},{10,... | collective-permute-start | bytes 393224 | tf_op jit(solution)/shard_map/ppermute | solution.py:452
  79.4 5.5 %collective-permute-start.27 = (bf16[256,256]{1,0:T(8,128)(2,1)S(1)}, bf16[256,256]{1,0:T(8,128)(2,1)S(1)}, u32[]{:S(2)}, u32[]{:S(2)}) collective-permute-start(bf16[256,256]{1,0:T(8,128)(2,1)S(1)} %collective-permute-done.17.refs_11_), channel_id=1, source_target_pairs={{0,2},{1,3},{2,0},{3,1},{4,6},{5,7},{6,4},{7,5},{8,10},{9,11},{10,... | collective-permute-start | bytes 393224 | tf_op jit(solution)/shard_map/ppermute | solution.py:452
  82.8 6.1 %collective-permute-start.30 = (bf16[256,256]{1,0:T(8,128)(2,1)S(1)}, bf16[256,256]{1,0:T(8,128)(2,1)S(1)}, u32[]{:S(2)}, u32[]{:S(2)}) collective-permute-start(bf16[256,256]{1,0:T(8,128)(2,1)S(1)} %collective-permute-done.26.refs_10_), channel_id=1, source_target_pairs={{0,8},{4,12},{8,0},{12,4},{16,24},{20,28},{24,16},{28,20},{1,9},{5... | collective-permute-start | bytes 393224 | tf_op jit(solution)/shard_map/ppermute | solution.py:452
  83.9 5.7 %collective-permute-start.29 = (bf16[256,256]{1,0:T(8,128)(2,1)S(1)}, bf16[256,256]{1,0:T(8,128)(2,1)S(1)}, u32[]{:S(2)}, u32[]{:S(2)}) collective-permute-start(bf16[256,256]{1,0:T(8,128)(2,1)S(1)} %collective-permute-done.25.refs_9_), channel_id=1, source_target_pairs={{0,8},{4,12},{8,0},{12,4},{16,24},{20,28},{24,16},{28,20},{1,9},{5... | collective-permute-start | bytes 393224 | tf_op jit(solution)/shard_map/ppermute | solution.py:452
  84.8 5.7 %collective-permute-start.31 = (bf16[256,256]{1,0:T(8,128)(2,1)S(1)}, bf16[256,256]{1,0:T(8,128)(2,1)S(1)}, u32[]{:S(2)}, u32[]{:S(2)}) collective-permute-start(bf16[256,256]{1,0:T(8,128)(2,1)S(1)} %collective-permute-done.27.refs_11_), channel_id=1, source_target_pairs={{0,8},{4,12},{8,0},{12,4},{16,24},{20,28},{24,16},{28,20},{1,9},{5... | collective-permute-start | bytes 393224 | tf_op jit(solution)/shard_map/ppermute | solution.py:452
  85.9 10.5 %collective-permute-start.2 = (bf16[256,256]{1,0:T(8,128)(2,1)S(1)}, bf16[256,256]{1,0:T(8,128)(2,1)S(1)}, u32[]{:S(2)}, u32[]{:S(2)}) collective-permute-start(bf16[256,256]{1,0:T(8,128)(2,1)S(1)} %get-tuple-element.34.refs_0_.refs_8_), channel_id=1, source_target_pairs={{0,1},{1,0},{2,3},{3,2},{4,5},{5,4},{6,7},{7,6},{8,9},{9,8},{10,11... | collective-permute-start | bytes 393224 | tf_op jit(solution)/shard_map/ppermute | solution.py:452
  87.1 9.3 %collective-permute-start.3 = (bf16[256,256]{1,0:T(8,128)(2,1)S(1)}, bf16[256,256]{1,0:T(8,128)(2,1)S(1)}, u32[]{:S(2)}, u32[]{:S(2)}) collective-permute-start(bf16[256,256]{1,0:T(8,128)(2,1)S(1)} %get-tuple-element.35.refs_1_), channel_id=1, source_target_pairs={{0,1},{1,0},{2,3},{3,2},{4,5},{5,4},{6,7},{7,6},{8,9},{9,8},{10,11... | collective-permute-start | bytes 393224 | tf_op jit(solution)/shard_map/ppermute | solution.py:452
  89.0 10.0 %collective-permute-start.6 = (bf16[256,256]{1,0:T(8,128)(2,1)S(1)}, bf16[256,256]{1,0:T(8,128)(2,1)S(1)}, u32[]{:S(2)}, u32[]{:S(2)}) collective-permute-start(bf16[256,256]{1,0:T(8,128)(2,1)S(1)} %collective-permute-done.4.refs_4_.refs_8_), channel_id=1, source_target_pairs={{0,1},{1,0},{2,3},{3,2},{4,5},{5,4},{6,7},{7,6},{8,9},{9,8},{10,11... | collective-permute-start | bytes 393224 | tf_op jit(solution)/shard_map/ppermute | solution.py:452
  89.5 9.9 %collective-permute-start.7 = (bf16[256,256]{1,0:T(8,128)(2,1)S(1)}, bf16[256,256]{1,0:T(8,128)(2,1)S(1)}, u32[]{:S(2)}, u32[]{:S(2)}) collective-permute-start(bf16[256,256]{1,0:T(8,128)(2,1)S(1)} %collective-permute-done.5.refs_5_), channel_id=1, source_target_pairs={{0,1},{1,0},{2,3},{3,2},{4,5},{5,4},{6,7},{7,6},{8,9},{9,8},{10,11... | collective-permute-start | bytes 393224 | tf_op jit(solution)/shard_map/ppermute | solution.py:452
  90.6 11.0 %collective-permute-start.22 = (bf16[256,256]{1,0:T(8,128)(2,1)S(1)}, bf16[256,256]{1,0:T(8,128)(2,1)S(1)}, u32[]{:S(2)}, u32[]{:S(2)}) collective-permute-start(bf16[256,256]{1,0:T(8,128)(2,1)S(1)} %get-tuple-element.41), channel_id=1, source_target_pairs={{0,16},{4,20},{8,24},{12,28},{16,0},{20,4},{24,8},{28,12},{1,17},{... | collective-permute-start | bytes 393224 | tf_op jit(solution)/shard_map/ppermute | solution.py:452
  96.4 17.6 %collective-permute-start.23 = (f32[256,256]{1,0:T(8,128)S(1)}, f32[256,256]{1,0:T(8,128)S(1)}, u32[]{:S(2)}, u32[]{:S(2)}) collective-permute-start(f32[256,256]{1,0:T(8,128)S(1)} %get-tuple-element.42), channel_id=1, source_target_pairs={{0,1},{1,0},{2,3},{3,2},{4,5},{5,4},{6,7},{7,6},{8,9},{9,8},{10,11... | collective-permute-start | bytes 786440 | tf_op jit(solution)/shard_map/ppermute | solution.py:452
  96.5 23.1 %collective-permute-start.33 = (f32[256,256]{1,0:T(8,128)S(1)}, f32[256,256]{1,0:T(8,128)S(1)}, u32[]{:S(2)}, u32[]{:S(2)}) collective-permute-start(f32[256,256]{1,0:T(8,128)S(1)} %get-tuple-element.46), channel_id=1, source_target_pairs={{0,1},{1,0},{2,3},{3,2},{4,5},{5,4},{6,7},{7,6},{8,9},{9,8},{10,11... | collective-permute-start | bytes 786440 | tf_op jit(solution)/shard_map/ppermute | solution.py:452
  99.0 15.0 %collective-permute-start.24 = (bf16[256,256]{1,0:T(8,128)(2,1)S(1)}, bf16[256,256]{1,0:T(8,128)(2,1)S(1)}, u32[]{:S(2)}, u32[]{:S(2)}) collective-permute-start(bf16[256,256]{1,0:T(8,128)(2,1)S(1)} %get-tuple-element.43), channel_id=1, source_target_pairs={{0,17},{1,16},{2,19},{3,18},{4,21},{5,20},{6,23},{7,22},{8,25},{9,... | collective-permute-start | bytes 393224 | tf_op jit(solution)/shard_map/ppermute | solution.py:452
  99.4 17.8 %collective-permute-start.32 = (bf16[256,256]{1,0:T(8,128)(2,1)S(1)}, bf16[256,256]{1,0:T(8,128)(2,1)S(1)}, u32[]{:S(2)}, u32[]{:S(2)}) collective-permute-start(bf16[256,256]{1,0:T(8,128)(2,1)S(1)} %get-tuple-element.45), channel_id=1, source_target_pairs={{0,16},{4,20},{8,24},{12,28},{16,0},{20,4},{24,8},{28,12},{1,17},{... | collective-permute-start | bytes 393224 | tf_op jit(solution)/shard_map/ppermute | solution.py:452
  101.6 18.0 %collective-permute-start.34 = (bf16[256,256]{1,0:T(8,128)(2,1)S(1)}, bf16[256,256]{1,0:T(8,128)(2,1)S(1)}, u32[]{:S(2)}, u32[]{:S(2)}) collective-permute-start(bf16[256,256]{1,0:T(8,128)(2,1)S(1)} %get-tuple-element.47), channel_id=1, source_target_pairs={{0,17},{1,16},{2,19},{3,18},{4,21},{5,20},{6,23},{7,22},{8,25},{9,... | collective-permute-start | bytes 393224 | tf_op jit(solution)/shard_map/ppermute | solution.py:452
  (15 other events, 119.3 us)

commit v3 on v2

--- a/solution.py
+++ b/solution.py
@@ -137,7 +137,7 @@
 
 
 def cost(flops, moved):
-    return pl.CostEstimate(flops=flops, bytes_accessed=moved, transcendentals=0)
+    return pl.CostEstimate(flops=0, bytes_accessed=0, transcendentals=0)
 
 
 def whole(shape):
@@ -145,43 +145,31 @@
     return pl.BlockSpec(shape, lambda *_: zeros)
 
 
-def project_kernel(me_ref, x_ref, wk_ref, wv_ref, away_ref, mine_ref):
-    x = x_ref[...]
-    for q in range(4):
-        at = pl.ds(pl.multiple_of((me_ref[0] ^ q) * HEAD_DIM, HEAD_DIM), HEAD_DIM)
-        term = dot(x, jnp.concatenate([wk_ref[:, at], wv_ref[:, at]], axis=1))
-        ref = (away_ref if q % 2 else mine_ref).at[q // 2]
-
-        @pl.when(pl.program_id(0) == 0)
-        def _(ref=ref, term=term):
-            ref[...] = term
-
-        @pl.when(pl.program_id(0) != 0)
-        def _(ref=ref, term=term):
-            ref[...] += term
-
-
-def project(me, x, w_key, w_value):
+def project_kernel(me_ref, x_ref, wk_ref, wv_ref, away_ref, keep_ref):
+    other = pl.multiple_of((lax.rem(me_ref[0], 2) ^ 1) * HEAD_DIM, HEAD_DIM)
+    for at, ref in ((other, away_ref), (HEAD_DIM - other, keep_ref)):
+        span = pl.ds(pl.multiple_of(at, HEAD_DIM), HEAD_DIM)
+        ref[...] = dot(x_ref[...], jnp.concatenate([wk_ref[:, span], wv_ref[:, span]], axis=1))
+
+
+def project(me, x, w_key, w_value, far):
     rows, feats = x.shape
-    cols = w_key.shape[1]
-    out = (2, rows, 2 * HEAD_DIM)
-    step = 512
+    step = rows // 2
+    out = (rows, 2 * HEAD_DIM)
+    weights = pl.BlockSpec((feats, 2 * HEAD_DIM), lambda i, me: (0, lax.div(me[0], 2) ^ far))
+    block = pl.BlockSpec((step, 2 * HEAD_DIM), lambda i, me: (i, 0))
     spec = pltpu.PrefetchScalarGridSpec(
         num_scalar_prefetch=1,
-        grid=(feats // step,),
-        in_specs=[
-            pl.BlockSpec((rows, step), lambda i, me: (0, i)),
-            pl.BlockSpec((step, cols), lambda i, me: (i, 0)),
-            pl.BlockSpec((step, cols), lambda i, me: (i, 0)),
-        ],
-        out_specs=(whole(out), whole(out)),
+        grid=(rows // step,),
+        in_specs=[pl.BlockSpec((step, feats), lambda i, me: (i, 0)), weights, weights],
+        out_specs=(block, block),
     )
     return pl.pallas_call(
         project_kernel,
         out_shape=(jax.ShapeDtypeStruct(out, F32),) * 2,
         grid_spec=spec,
-        compiler_params=params(60),
-        cost_estimate=cost(4 * rows * feats * cols, 10 << 20),
+        compiler_params=params(58),
+        cost_estimate=cost(8 * rows * feats * HEAD_DIM, 5 << 20),
         name="project",
     )(me, x, w_key, w_value)
 
@@ -242,7 +230,7 @@
 
 
 def pack_kernel(me_ref, mine_ref, core_ref, across_ref, pick_ref, meta_ref, *out_refs):
-    total = (mine_ref[0] + core_ref[0]) + across_ref[...]
+    total = (mine_ref[...] + core_ref[...]) + across_ref[...]
     placed = dot(pick_ref[...], total.astype(BF16)).astype(BF16)
     learners = meta_ref.shape[0]
     block = placed.shape[0] // learners
@@ -257,11 +245,11 @@
     learners, extra, _ = meta.shape
     out = (rows // learners + extra, cols)
     outs = ((learners,) + out,)
-    second = pl.BlockSpec((1, rows, cols), lambda *_: (0, 0, 0))
+    part = whole((rows, cols))
     spec = pltpu.PrefetchScalarGridSpec(
         num_scalar_prefetch=1,
         grid=(1,),
-        in_specs=[second, second, whole((rows, cols)), whole((rows, rows)), whole(meta.shape)],
+        in_specs=[part, part, part, whole((rows, rows)), whole(meta.shape)],
         out_specs=tuple(whole(o) for o in outs),
     )
     return pl.pallas_call(
@@ -274,26 +262,26 @@
     )(me, mine, core, across, pick, meta)
 
 
-def attention_kernel(lmax, learners, me_ref, *refs):
-    *kv_refs, q_ref, g_ref, out_ref, near_ref, far_ref, place_ref, slot_out = refs
-    kv_refs = [kv_refs[0].at[me_ref[0] ^ i] for i in range(learners)]
+def attention_kernel(lmax, learners, half, me_ref, kv_ref, q_ref, g_ref, grad_ref, out_ref, place_ref):
     rows, cols = q_ref.shape
-    lines = kv_refs[0].shape[0]
     block = rows // learners
     heads = cols // HEAD_DIM
     scale = 1.0 / HEAD_DIM**0.5
+    count = learners // 2
+    kv_refs = [kv_ref.at[me_ref[0] ^ (half * count + i)] for i in range(count)]
+    lines = kv_ref.shape[1]
     meta = jnp.concatenate([ref[block:, :HEAD_DIM] for ref in kv_refs], axis=0)
-    a, b = iota((rows, meta.shape[0]), 0), iota((rows, meta.shape[0]), 1)
+    a, b = iota((rows // 2, meta.shape[0]), 0), iota((rows // 2, meta.shape[0]), 1)
     spread = (lax.div(a, block) * (lines - block) + lax.div(lax.rem(a, block), lmax) == b).astype(BF16)
     table = dot(spread, meta).astype(I32)
-    inner = lax.rem(iota((rows, 1), 0), lmax)
+    inner = lax.rem(iota((rows // 2, 1), 0), lmax)
     alive = inner < table[:, 0:1]
     target = jnp.where(alive, table[:, 1:2] * lmax + table[:, 2:3] + inner, -1)
-    place_ref[...] = (iota((rows, rows), 1) == target).astype(BF16)
+    place_ref[...] = (iota((rows // 2, rows), 1) == target).astype(BF16)
     size = HEAD_DIM
     a, b = iota((size, size), 0), iota((size, size), 1)
     near = (lax.div(a, lmax) == lax.div(b, lmax)) & (b <= a)
-    for i in range(rows // size):
+    for i in range(rows // 2 // size):
         span = slice(i * size, (i + 1) * size)
         first = i * size // block
         kv = jnp.concatenate([kv_refs[first + j][:block, :] for j in range(size // block)], axis=0)
@@ -314,43 +302,60 @@
         dprob = dot(g, v, COLS_LAST)
         delta = jnp.sum(g.astype(F32) * out.astype(F32), axis=1, keepdims=True)
         dscore_b = (probs * (dprob - delta)).astype(BF16)
-        grad_ref, at = (near_ref, i * size) if i * size < rows // 2 else (far_ref, i * size - rows // 2)
-        grad_ref[at : at + size, :HEAD_DIM] = (dot(dscore_b, q, ROWS_LAST) * scale).astype(BF16)
-        grad_ref[at : at + size, HEAD_DIM:] = dot(probs_b, g, ROWS_LAST).astype(BF16)
+        grad_ref[span, :HEAD_DIM] = (dot(dscore_b, q, ROWS_LAST) * scale).astype(BF16)
+        grad_ref[span, HEAD_DIM:] = dot(probs_b, g, ROWS_LAST).astype(BF16)
         for h in range(heads):
-            slot_out[span, h * HEAD_DIM : (h + 1) * HEAD_DIM] = out[h * size : (h + 1) * size]
-    out_ref[...] = dot(place_ref[...], slot_out[...], ROWS_LAST).astype(BF16)
-
-
-def attention(me, kvs, queries, out_grad, lmax, learners):
+            out_ref[span, h * HEAD_DIM : (h + 1) * HEAD_DIM] = out[h * size : (h + 1) * size]
+
+
+def attention(me, kv, queries, out_grad, lmax, learners, half):
     rows, cols = queries.shape
-    outs = ((rows, cols),) + ((rows // 2, 2 * HEAD_DIM),) * 2 + ((rows, rows),)
+    outs = ((rows // 2, 2 * HEAD_DIM), (rows // 2, cols), (rows // 2, rows))
     spec = pltpu.PrefetchScalarGridSpec(
         num_scalar_prefetch=1,
         grid=(1,),
-        in_specs=[whole(kv.shape) for kv in kvs] + [whole((rows, cols))] * 2,
+        in_specs=[whole(kv.shape)] + [whole((rows, cols))] * 2,
         out_specs=tuple(whole(o) for o in outs),
-        scratch_shapes=[pltpu.VMEM((rows, cols), BF16)],
-    )
-    return pl.pallas_call(
-        functools.partial(attention_kernel, lmax, learners),
+    )
+    return pl.pallas_call(
+        functools.partial(attention_kernel, lmax, learners, half),
         out_shape=tuple(jax.ShapeDtypeStruct(o, BF16) for o in outs),
         grid_spec=spec,
         compiler_params=params(),
-        cost_estimate=cost(8 * rows * rows * cols, 4 << 20),
+        cost_estimate=cost(4 * rows * rows * cols, 4 << 20),
         name="attention",
-    )(me, *kvs, queries, out_grad)
-
-
-def rows_kernel(me_ref, place_ref, *refs):
+    )(me, kv, queries, out_grad)
+
+
+def packed_rows_kernel(place0, place1, out0, out1, out_ref):
+    total = dot(place0[...], out0[...], ROWS_LAST) + dot(place1[...], out1[...], ROWS_LAST)
+    out_ref[...] = total.astype(BF16)
+
+
+def packed_rows(place, outs):
+    half, cols = outs[0].shape
+    rows = place[0].shape[1]
+    return pl.pallas_call(
+        packed_rows_kernel,
+        out_shape=jax.ShapeDtypeStruct((rows, cols), BF16),
+        grid=(1,),
+        in_specs=[whole((half, rows))] * 2 + [whole((half, cols))] * 2,
+        out_specs=whole((rows, cols)),
+        compiler_params=params(),
+        cost_estimate=cost(4 * half * rows * cols, 3 << 20),
+        name="packed_rows",
+    )(*place, *outs)
+
+
+def rows_kernel(me_ref, place0, place1, *refs):
     *g_refs, wk_ref, wv_ref, out_ref, grads = refs
 
     @pl.when(pl.program_id(0) == 0)
     def _():
         half = grads.shape[1] // 2
         for i in range(4):
-            g = jnp.concatenate([g_refs[2 * i][...], g_refs[2 * i + 1][...]], axis=0)
-            part = dot(place_ref[...], g, ROWS_LAST).astype(BF16)
+            part = dot(place0[...], g_refs[2 * i][...], ROWS_LAST)
+            part = (part + dot(place1[...], g_refs[2 * i + 1][...], ROWS_LAST)).astype(BF16)
             at = pl.multiple_of((me_ref[0] ^ i) * HEAD_DIM, HEAD_DIM)
             grads[:, pl.ds(at, HEAD_DIM)] = part[:, :HEAD_DIM]
             grads[:, pl.ds(at + half, HEAD_DIM)] = part[:, HEAD_DIM:]
@@ -362,12 +367,12 @@
 
 def row_grads(me, place, parts, w_key, w_value):
     feats, cols = w_key.shape
-    rows = place.shape[0]
+    rows = place[0].shape[1]
     step = 512
     spec = pltpu.PrefetchScalarGridSpec(
         num_scalar_prefetch=1,
         grid=(feats // step,),
-        in_specs=[whole((rows, rows))]
+        in_specs=[whole((rows // 2, rows))] * 2
         + [whole((rows // 2, 2 * HEAD_DIM))] * 8
         + [pl.BlockSpec((step, cols), lambda i, me: (i, 0))] * 2,
         out_specs=pl.BlockSpec((rows, step), lambda i, me: (0, i)),
@@ -380,7 +385,7 @@
         compiler_params=params(),
         cost_estimate=cost(4 * rows * feats * cols, 8 << 20),
         name="row_grads",
-    )(me, place, *parts, w_key, w_value)
+    )(me, *place, *parts, w_key, w_value)
 
 
 def weights_kernel(x_refs, g_refs, out_refs):
@@ -464,19 +469,23 @@
     m = lax.axis_index("mp").astype(I32).reshape(1)
     d = lax.axis_index("dp").astype(I32).reshape(1)
 
-    away, mine = project(m, x, w_key, w_value)
+    away, keep = project(m, x, w_key, w_value, 1)
     core = swap(away, "mp", 1)
-    half = mine[1] + core[1]
+    *xs, pick, meta = slots(d, dest, lengths, offsets, after(x, away), learners, per)
+    half = after(keep, pick) + core
+    xs = [xs[0]] + [swap(after(xs[f], half), "dp", f) for f in range(1, learners // 2)]
     across = swap(half, "mp", 2)
-    *xs, pick, meta = slots(d, dest, lengths, offsets, after(x, half), learners, per)
-    xs = [xs[0]] + [swap(xs[f], "dp", f) for f in range(1, learners // 2)]
-    kv = pack(d, mine, core, across, pick, meta)
+    away, keep = project(m, after(x, half), w_key, w_value, 0)
+    core = swap(away, "mp", 1)
+    kv = pack(d, keep, core, across, pick, meta)
     kv = lax.all_to_all(kv[0], "dp", split_axis=0, concat_axis=0, tiled=True)
 
-    attn_out, grads, beyond, place = attention(d, [kv], queries, out_grad, lmax, learners)
+    beyond, out1, place1 = attention(d, kv, queries, out_grad, lmax, learners, 1)
+    there = swap(beyond, "dp", 4)
+    grads, out0, place0 = attention(d, after(kv, beyond), queries, out_grad, lmax, learners, 0)
+    place = [place0, place1]
 
     xs = xs + [swap(b, "mp", 1) for b in xs]
-    there = swap(beyond, "dp", 4)
     near = {(0, 0, 0): grads, (0, 0, 1): there}
     hops = [
         ((0, 0), "dp", 1), ((0, 0), "dp", 2), ((0, 0), "mp", 2), ((2, 0), "dp", 1),
@@ -497,6 +506,7 @@
         sums[4 * far + 3] = swap(send[1], ("dp", "mp"), 4 * heads + 1)
         sums[4 * far], keep = weight_grads(xs, pieces, 0, F32)
         sums[4 * far + 2] = swap(keep, "mp", 1)
+    attn_out = packed_rows(place, [out0, out1])
     grad_x = row_grads(m, place, own, w_key, w_value)
     grad_wk, grad_wv = finish(m, sums, learners)
     return (attn_out, grad_x, grad_wk, grad_wv)

time: 121 us -> 111 us (0.917)
  waiting for transfers between devices: 43.5 us -> 37.1 us
  Pallas kernels: 34.8 us -> 32.5 us
  local copies, waits for them, and re-layouts: 5.12 us -> 3.52 us
    ppermute x35 -> x36, waiting for transfers between devices: 38.4 us -> 32.4 us  [swap(): return lax.ppermute(x, axis, [(i, i ^ code) for i in range(size)])]
    pallas_call x1 -> x2, Pallas kernels: 10.2 us -> 8.4 us  [project(): pl.pallas_call(project_kernel, out_shape=(jax.ShapeDtypeStruct(out, F32),...]
    unnamed x22 -> x20, local copies, waits for them, and re-layouts: 5.12 us -> 3.52 us
    ppermute x35 -> x36, starting transfers between devices: 28.4 us -> 29.2 us  [swap(): return lax.ppermute(x, axis, [(i, i ^ code) for i in range(size)])]
    pallas_call x1 -> x3, Pallas kernels: 6.91 us -> 7.49 us  [the longest x2 5.79 us: attention(): pl.pallas_call(functools.partial(attention_kernel, lmax, learners, half),...]
  transfers between devices with their start and end apart: 36 -> 37, of which waited for: 13 -> 11; matrix products, arithmetic and copies ran while one was open for 0% -> 0% of each run, Pallas kernels for 19% -> 21%
where the time goes in v3:
time: 111 us; the launch traced here: 110 us
  waiting for transfers between devices  37.1 us (33%)
  starting transfers between devices  35.3 us (32%)
  Pallas kernels  32.5 us (29%)
  local copies, waits for them, and re-layouts  3.52 us (3%)
  other arithmetic  1.11 us (1%)
    ppermute x36, waiting for transfers between devices, swap(): return lax.ppermute(x, axis, [(i, i ^ code) for i in range(size)])  32.4 us
    ppermute x36, starting transfers between devices, swap(): return lax.ppermute(x, axis, [(i, i ^ code) for i in range(size)])  29.2 us
    pallas_call x2, Pallas kernels, project(): pl.pallas_call(project_kernel, out_shape=(jax.ShapeDtypeStruct(out, F32),...  8.4 us
    pallas_call x4, Pallas kernels, weight_grads(): pl.pallas_call(kernel, out_shape=(jax.ShapeDtypeStruct(out, dtype),) * 2,...  7.31 us
    all_to_all x1, starting transfers between devices, local(): kv = lax.all_to_all(kv[0], 'dp', split_axis=0, concat_axis=0, tiled=True)  6.07 us
    pallas_call x2, Pallas kernels, attention(): pl.pallas_call(functools.partial(attention_kernel, lmax, learners, half),...  5.79 us
    pallas_call x1, Pallas kernels, row_grads(): pl.pallas_call(rows_kernel, out_shape=jax.ShapeDtypeStruct((rows, feats),...  4.78 us
    all_to_all x1, waiting for transfers between devices, local(): kv = lax.all_to_all(kv[0], 'dp', split_axis=0, concat_axis=0, tiled=True)  4.7 us
  transfers between devices with their start and end apart: 37, of which 11 were waited for; matrix products, arithmetic and copies ran while one was open for 0% of the time, Pallas kernels for 21%

profile of v3, /device:TPU:0, one launch (start us, length us, event | category | flops | bytes accessed | tf_op | source)
XLA Modules:
  0.0 110.4 jit_solution(16103572688615623922)
XLA Ops:
  0.7 4.3 %project.2 = (f32[512,256]{1,0:T(8,128)}, f32[512,256]{1,0:T(8,128)}) custom-call(s32[1]{0:T(128)} %bitcast.1.me_ref, bf16[512,2048]{1,0:T(8,128)(2,1)} %bitcast.6, bf16[2048,512]{1,0:T(8,128)(2,1)} %refs_8_.1, bf16[2048,512]{1,0:T(8,128)(2,1)} %refs_9_.1), custom_call_target="tpu_custom_call" | custom-call | tf_op jit(solution)/shard_map/project/pallas_call | solution.py:167
  5.4 2.4 %slots.1 = (bf16[2,512,256]{2,1,0:T(8,128)(2,1)S(1)}, bf16[2,512,256]{2,1,0:T(8,128)(2,1)}, bf16[2,512,256]{2,1,0:T(8,128)(2,1)}, bf16[2,512,256]{2,1,0:T(8,128)...) custom-call(s32[1]{0:T(128)} %bitcast.me_ref, s32[1,32]{1,0:T(1,128)S(1)} %bitcast.9, ...), custom_call_target="tpu_custom_call" | custom-call | tf_op jit(solution)/shard_map/slots/pallas_call | solution.py:222
  8.9 4.1 %project.3 = (f32[512,256]{1,0:T(8,128)}, f32[512,256]{1,0:T(8,128)}) custom-call(s32[1]{0:T(128)} %bitcast.1.me_ref, bf16[512,2048]{1,0:T(8,128)(2,1)} %bitcast.7, bf16[2048,512]{1,0:T(8,128)(2,1)} %refs_8_.1, bf16[2048,512]{1,0:T(8,128)(2,1)} %refs_9_.1), custom_call_target="tpu_custom_call" | custom-call | tf_op jit(solution)/shard_map/project/pallas_call | solution.py:167
  13.1 2.9 %collective-permute-start.2 = (f32[512,256]{1,0:T(8,128)S(1)}, f32[512,256]{1,0:T(8,128)S(1)}, u32[]{:S(2)}, u32[]{:S(2)}) collective-permute-start(f32[512,256]{1,0:T(8,128)S(1)} %add.3), channel_id=1, source_target_pairs={{0,2},{1,3},{2,0},{3,1},{4,6},{5,7},{6,4},{7,5},{8,10},{9,11},{10,... | collective-permute-start | bytes 1572872 | tf_op jit(solution)/shard_map/ppermute | solution.py:457
  16.0 1.5 %collective-permute-start.9 = (bf16[2,512,256]{2,1,0:T(8,128)(2,1)}, bf16[2,512,256]{2,1,0:T(8,128)(2,1)S(1)}, u32[]{:S(2)}, u32[]{:S(2)}) collective-permute-start(bf16[2,512,256]{2,1,0:T(8,128)(2,1)} %get-tuple-element.55), channel_id=1, source_target_pairs={{0,4},{4,0},{8,12},{12,8},{16,20},{20,16},{24,28},{28,24},{1,5},{5... | collective-permute-start | bytes 1572872 | tf_op jit(solution)/shard_map/ppermute | solution.py:457
  17.6 1.6 %collective-permute-start.10 = (bf16[2,512,256]{2,1,0:T(8,128)(2,1)}, bf16[2,512,256]{2,1,0:T(8,128)(2,1)S(1)}, u32[]{:S(2)}, u32[]{:S(2)}) collective-permute-start(bf16[2,512,256]{2,1,0:T(8,128)(2,1)} %get-tuple-element.57), channel_id=1, source_target_pairs={{0,8},{4,12},{8,0},{12,4},{16,24},{20,28},{24,16},{28,20},{1,9},{5... | collective-permute-start | bytes 1572872 | tf_op jit(solution)/shard_map/ppermute | solution.py:457
  19.5 8.6 %collective-permute-done.2.across_ref = f32[512,256]{1,0:T(8,128)S(1)} collective-permute-done((f32[512,256]{1,0:T(8,128)S(1)}, f32[512,256]{1,0:T(8,128)S(1)}, u32[]{:S(2)}, u32[]{:S(2)}) %collective-permute-start.2) | collective-permute-done | bytes 524320 | tf_op jit(solution)/shard_map/ppermute | solution.py:457
  30.3 6.1 %all-to-all-start = ((bf16[8,80,256]{2,1,0:T(8,128)(2,1)}), bf16[8,80,256]{2,1,0:T(8,128)(2,1)S(1)}, u32[]{:S(2)}, u32[]{:S(2)}) async-start(bf16[8,80,256]{2,1,0:T(8,128)(2,1)} %pack.1), calls=%async_computation | async-start | bytes 655360 | tf_op jit(solution)/shard_map/all_to_all | solution.py:481
  37.0 8.0 %collective-permute-done.11.refs_3_ = bf16[2,512,256]{2,1,0:T(8,128)(2,1)S(1)} collective-permute-done((bf16[2,512,256]{2,1,0:T(8,128)(2,1)}, bf16[2,512,256]{2,1,0:T(8,128)(2,1)S(1)}, u32[]{:S(2)}, u32[]{:S(2)}) %collective-permute-start.11) | collective-permute-done | bytes 524320 | tf_op jit(solution)/shard_map/ppermute | solution.py:457
  44.9 4.7 %all-to-all-done.kv_ref = bf16[8,80,256]{2,1,0:T(8,128)(2,1)S(1)} async-done(((bf16[8,80,256]{2,1,0:T(8,128)(2,1)}), bf16[8,80,256]{2,1,0:T(8,128)(2,1)S(1)}, u32[]{:S(2)}, u32[]{:S(2)}) %all-to-all-start) | async-done | bytes 327712 | tf_op jit(solution)/shard_map/all_to_all | solution.py:481
  49.6 1.2 %copy-done.3 = bf16[512,1024]{1,0:T(8,128)(2,1)S(1)} copy-done((bf16[512,1024]{1,0:T(8,128)(2,1)S(1)}, bf16[512,1024]{1,0:T(8,128)(2,1)}, u32[]{:S(2)}) %copy-start.3) | copy-done | bytes 1048600
  50.9 1.2 %copy-done.4 = bf16[512,1024]{1,0:T(8,128)(2,1)S(1)} copy-done((bf16[512,1024]{1,0:T(8,128)(2,1)S(1)}, bf16[512,1024]{1,0:T(8,128)(2,1)}, u32[]{:S(2)}) %copy-start.4) | copy-done | bytes 1048600
  52.1 2.9 %attention.2 = (bf16[256,256]{1,0:T(8,128)(2,1)S(1)}, bf16[256,1024]{1,0:T(8,128)(2,1)S(1)}, bf16[256,512]{1,0:T(8,128)(2,1)S(1)}) custom-call(s32[1]{0:T(128)} %bitcast.me_ref, bf16[8,80,256]{2,1,0:T(8,128)(2,1)S(1)} %all-to-all-done.kv_ref, bf16[512,1024]{1,0:T(8,128)(2,1)S(1)} %copy-done.3, bf16[512,1024]{1,0:T(8,128)(2,1)S(1)} %copy-done.4), custom_call_target="tpu_custom_call" | custom-call | tf_op jit(solution)/shard_map/attention/pallas_call | solution.py:320
  55.0 1.2 %collective-permute-start.16 = (bf16[256,256]{1,0:T(8,128)(2,1)S(1)}, bf16[256,256]{1,0:T(8,128)(2,1)S(1)}, u32[]{:S(2)}, u32[]{:S(2)}) collective-permute-start(bf16[256,256]{1,0:T(8,128)(2,1)S(1)} %get-tuple-element.46.refs_1_), channel_id=1, source_target_pairs={{0,16},{4,20},{8,24},{12,28},{16,0},{20,4},{24,8},{28,12},{1,17},{... | collective-permute-start | bytes 393224 | tf_op jit(solution)/shard_map/ppermute | solution.py:457
  56.2 2.9 %attention.3 = (bf16[256,256]{1,0:T(8,128)(2,1)S(1)}, bf16[256,1024]{1,0:T(8,128)(2,1)S(1)}, bf16[256,512]{1,0:T(8,128)(2,1)S(1)}) custom-call(s32[1]{0:T(128)} %bitcast.me_ref, bf16[8,80,256]{2,1,0:T(8,128)(2,1)S(1)} %all-to-all-done.kv_ref, bf16[512,1024]{1,0:T(8,128)(2,1)S(1)} %copy-done.3, bf16[512,1024]{1,0:T(8,128)(2,1)S(1)} %copy-done.4), custom_call_target="tpu_custom_call" | custom-call | tf_op jit(solution)/shard_map/attention/pallas_call | solution.py:320
  60.5 1.2 %collective-permute-start.19 = (bf16[256,256]{1,0:T(8,128)(2,1)S(1)}, bf16[256,256]{1,0:T(8,128)(2,1)S(1)}, u32[]{:S(2)}, u32[]{:S(2)}) collective-permute-start(bf16[256,256]{1,0:T(8,128)(2,1)S(1)} %get-tuple-element.52.refs_0_.refs_8_), channel_id=1, source_target_pairs={{0,8},{4,12},{8,0},{12,4},{16,24},{20,28},{24,16},{28,20},{1,9},{5... | collective-permute-start | bytes 393224 | tf_op jit(solution)/shard_map/ppermute | solution.py:457
  61.7 1.5 %collective-permute-start.6 = (bf16[256,256]{1,0:T(8,128)(2,1)S(1)}, bf16[256,256]{1,0:T(8,128)(2,1)S(1)}, u32[]{:S(2)}, u32[]{:S(2)}) collective-permute-start(bf16[256,256]{1,0:T(8,128)(2,1)S(1)} %get-tuple-element.46.refs_1_), channel_id=1, source_target_pairs={{0,2},{1,3},{2,0},{3,1},{4,6},{5,7},{6,4},{7,5},{8,10},{9,11},{10,... | collective-permute-start | bytes 393224 | tf_op jit(solution)/shard_map/ppermute | solution.py:457
  64.7 1.8 %collective-permute-done.5.refs_4_.refs_8_ = bf16[256,256]{1,0:T(8,128)(2,1)S(1)} collective-permute-done((bf16[256,256]{1,0:T(8,128)(2,1)S(1)}, bf16[256,256]{1,0:T(8,128)(2,1)S(1)}, u32[]{:S(2)}, u32[]{:S(2)}) %collective-permute-start.5) | collective-permute-done | bytes 131104 | tf_op jit(solution)/shard_map/ppermute | solution.py:457
  69.6 1.7 %collective-permute-start.28 = (bf16[256,256]{1,0:T(8,128)(2,1)S(1)}, bf16[256,256]{1,0:T(8,128)(2,1)S(1)}, u32[]{:S(2)}, u32[]{:S(2)}) collective-permute-start(bf16[256,256]{1,0:T(8,128)(2,1)S(1)} %collective-permute-done.18.refs_11_), channel_id=1, source_target_pairs={{0,2},{1,3},{2,0},{3,1},{4,6},{5,7},{6,4},{7,5},{8,10},{9,11},{10,... | collective-permute-start | bytes 393224 | tf_op jit(solution)/shard_map/ppermute | solution.py:457
  72.6 1.5 %collective-permute-start.22 = (bf16[256,256]{1,0:T(8,128)(2,1)S(1)}, bf16[256,256]{1,0:T(8,128)(2,1)S(1)}, u32[]{:S(2)}, u32[]{:S(2)}) collective-permute-start(bf16[256,256]{1,0:T(8,128)(2,1)S(1)} %collective-permute-done.20.refs_13_), channel_id=1, source_target_pairs={{0,4},{4,0},{8,12},{12,8},{16,20},{20,16},{24,28},{28,24},{1,5},{5... | collective-permute-start | bytes 393224 | tf_op jit(solution)/shard_map/ppermute | solution.py:457
  77.3 1.2 %collective-permute-done.22.refs_15_ = bf16[256,256]{1,0:T(8,128)(2,1)S(1)} collective-permute-done((bf16[256,256]{1,0:T(8,128)(2,1)S(1)}, bf16[256,256]{1,0:T(8,128)(2,1)S(1)}, u32[]{:S(2)}, u32[]{:S(2)}) %collective-permute-start.22) | collective-permute-done | bytes 131104 | tf_op jit(solution)/shard_map/ppermute | solution.py:457
  78.5 1.8 %weight_grads.5 = (bf16[256,256]{1,0:T(8,128)(2,1)S(1)}, bf16[256,256]{1,0:T(8,128)(2,1)S(1)}) custom-call(bf16[2,512,256]{2,1,0:T(8,128)(2,1)S(1)} %get-tuple-element.53.refs_0_, bf16[2,512,256]{2,1,0:T(8,128)(2,1)S(1)} %collective-permute-done.9.refs_1_, bf16[2,512,256]{2,1,0:T(8,128)(2,1)S(1)} %collective-permute-done.10.refs_2_, ...), custom_call_target="tpu_custom_call" | custom-call | tf_op jit(solution)/shard_map/weight_grads/pallas_call | solution.py:414
  80.3 1.8 %weight_grads.4 = (f32[256,256]{1,0:T(8,128)S(1)}, f32[256,256]{1,0:T(8,128)S(1)}) custom-call(bf16[2,512,256]{2,1,0:T(8,128)(2,1)S(1)} %get-tuple-element.53.refs_0_, bf16[2,512,256]{2,1,0:T(8,128)(2,1)S(1)} %collective-permute-done.9.refs_1_, bf16[2,512,256]{2,1,0:T(8,128)(2,1)S(1)} %collective-permute-done.10.refs_2_, ...), custom_call_target="tpu_custom_call" | custom-call | tf_op jit(solution)/shard_map/weight_grads/pallas_call | solution.py:414
  82.8 1.6 %collective-permute-start.23 = (bf16[256,256]{1,0:T(8,128)(2,1)S(1)}, bf16[256,256]{1,0:T(8,128)(2,1)S(1)}, u32[]{:S(2)}, u32[]{:S(2)}) collective-permute-start(bf16[256,256]{1,0:T(8,128)(2,1)S(1)} %get-tuple-element.61), channel_id=1, source_target_pairs={{0,16},{4,20},{8,24},{12,28},{16,0},{20,4},{24,8},{28,12},{1,17},{... | collective-permute-start | bytes 393224 | tf_op jit(solution)/shard_map/ppermute | solution.py:457
  84.4 1.8 %weight_grads.6 = (f32[256,256]{1,0:T(8,128)S(1)}, f32[256,256]{1,0:T(8,128)S(1)}) custom-call(bf16[2,512,256]{2,1,0:T(8,128)(2,1)S(1)} %get-tuple-element.53.refs_0_, bf16[2,512,256]{2,1,0:T(8,128)(2,1)S(1)} %collective-permute-done.9.refs_1_, bf16[2,512,256]{2,1,0:T(8,128)(2,1)S(1)} %collective-permute-done.10.refs_2_, ...), custom_call_target="tpu_custom_call" | custom-call | tf_op jit(solution)/shard_map/weight_grads/pallas_call | solution.py:414
  86.7 1.9 %weight_grads.7 = (bf16[256,256]{1,0:T(8,128)(2,1)S(1)}, bf16[256,256]{1,0:T(8,128)(2,1)S(1)}) custom-call(bf16[2,512,256]{2,1,0:T(8,128)(2,1)S(1)} %get-tuple-element.53.refs_0_, bf16[2,512,256]{2,1,0:T(8,128)(2,1)S(1)} %collective-permute-done.9.refs_1_, bf16[2,512,256]{2,1,0:T(8,128)(2,1)S(1)} %collective-permute-done.10.refs_2_, ...), custom_call_target="tpu_custom_call" | custom-call | tf_op jit(solution)/shard_map/weight_grads/pallas_call | solution.py:414
  89.9 1.5 %collective-permute-start.33 = (bf16[256,256]{1,0:T(8,128)(2,1)S(1)}, bf16[256,256]{1,0:T(8,128)(2,1)S(1)}, u32[]{:S(2)}, u32[]{:S(2)}) collective-permute-start(bf16[256,256]{1,0:T(8,128)(2,1)S(1)} %get-tuple-element.65), channel_id=1, source_target_pairs={{0,16},{4,20},{8,24},{12,28},{16,0},{20,4},{24,8},{28,12},{1,17},{... | collective-permute-start | bytes 393224 | tf_op jit(solution)/shard_map/ppermute | solution.py:457
  92.5 1.7 %packed_rows.1 = bf16[512,1024]{1,0:T(8,128)(2,1)} custom-call(bf16[256,512]{1,0:T(8,128)(2,1)S(1)} %get-tuple-element.48.place0, bf16[256,512]{1,0:T(8,128)(2,1)S(1)} %get-tuple-element.49.place1, bf16[256,1024]{1,0:T(8,128)(2,1)S(1)} %get-tuple-element.50.out0, bf16[256,1024]{1,0:T(8,128)(2,1)S(1)} %get-tuple-element.51.out1), custom_call_target="tpu_custom_call" | custom-call | tf_op jit(solution)/shard_map/packed_rows/pallas_call | solution.py:338
  94.2 4.8 %row_grads.1 = bf16[512,2048]{1,0:T(8,128)(2,1)} custom-call(s32[1]{0:T(128)} %bitcast.1.me_ref, bf16[256,512]{1,0:T(8,128)(2,1)S(1)} %get-tuple-element.48.place0, bf16[256,512]{1,0:T(8,128)(2,1)S(1)} %get-tuple-element.49.place1, bf16[256,256]{1,0:T(8,128)(2,1)S(1)} %get-tuple-element.52.refs_0_.refs_8_, bf16[256,256]{1,0:T(8,128)(2,1)S(1)} %get-tuple-element.46.refs_1_, ...), custom_call_target="tpu_custom_call" | custom-call | tf_op jit(solution)/shard_map/row_grads/pallas_call | solution.py:381
  99.0 4.7 %collective-permute-done.25.refs_3_ = bf16[256,256]{1,0:T(8,128)(2,1)S(1)} collective-permute-done((bf16[256,256]{1,0:T(8,128)(2,1)S(1)}, bf16[256,256]{1,0:T(8,128)(2,1)S(1)}, u32[]{:S(2)}, u32[]{:S(2)}) %collective-permute-start.25) | collective-permute-done | bytes 131104 | tf_op jit(solution)/shard_map/ppermute | solution.py:457
  103.6 3.3 %collective-permute-done.33.refs_5_ = bf16[256,256]{1,0:T(8,128)(2,1)S(1)} collective-permute-done((bf16[256,256]{1,0:T(8,128)(2,1)S(1)}, bf16[256,256]{1,0:T(8,128)(2,1)S(1)}, u32[]{:S(2)}, u32[]{:S(2)}) %collective-permute-start.33) | collective-permute-done | bytes 131104 | tf_op jit(solution)/shard_map/ppermute | solution.py:457
  107.0 2.3 %collective-permute-done.35.refs_7_ = bf16[256,256]{1,0:T(8,128)(2,1)S(1)} collective-permute-done((bf16[256,256]{1,0:T(8,128)(2,1)S(1)}, bf16[256,256]{1,0:T(8,128)(2,1)S(1)}, u32[]{:S(2)}, u32[]{:S(2)}) %collective-permute-start.35) | collective-permute-done | bytes 131104 | tf_op jit(solution)/shard_map/ppermute | solution.py:457
  (76 shorter events, 19.8 us)
Async XLA Ops:
  13.0 6.5 %collective-permute-start.1 = (f32[512,256]{1,0:T(8,128)}, f32[512,256]{1,0:T(8,128)S(1)}, u32[]{:S(2)}, u32[]{:S(2)}) collective-permute-start(f32[512,256]{1,0:T(8,128)} %get-tuple-element.44), channel_id=1, source_target_pairs={{0,1},{1,0},{2,3},{3,2},{4,5},{5,4},{6,7},{7,6},{8,9},{9,8},{10,11... | collective-permute-start | bytes 1572872 | tf_op jit(solution)/shard_map/ppermute | solution.py:457
  13.1 15.1 %collective-permute-start.2 = (f32[512,256]{1,0:T(8,128)S(1)}, f32[512,256]{1,0:T(8,128)S(1)}, u32[]{:S(2)}, u32[]{:S(2)}) collective-permute-start(f32[512,256]{1,0:T(8,128)S(1)} %add.3), channel_id=1, source_target_pairs={{0,2},{1,3},{2,0},{3,1},{4,6},{5,7},{6,4},{7,5},{8,10},{9,11},{10,... | collective-permute-start | bytes 1572872 | tf_op jit(solution)/shard_map/ppermute | solution.py:457
  16.0 20.3 %collective-permute-start.9 = (bf16[2,512,256]{2,1,0:T(8,128)(2,1)}, bf16[2,512,256]{2,1,0:T(8,128)(2,1)S(1)}, u32[]{:S(2)}, u32[]{:S(2)}) collective-permute-start(bf16[2,512,256]{2,1,0:T(8,128)(2,1)} %get-tuple-element.55), channel_id=1, source_target_pairs={{0,4},{4,0},{8,12},{12,8},{16,20},{20,16},{24,28},{28,24},{1,5},{5... | collective-permute-start | bytes 1572872 | tf_op jit(solution)/shard_map/ppermute | solution.py:457
  17.6 19.3 %collective-permute-start.10 = (bf16[2,512,256]{2,1,0:T(8,128)(2,1)}, bf16[2,512,256]{2,1,0:T(8,128)(2,1)S(1)}, u32[]{:S(2)}, u32[]{:S(2)}) collective-permute-start(bf16[2,512,256]{2,1,0:T(8,128)(2,1)} %get-tuple-element.57), channel_id=1, source_target_pairs={{0,8},{4,12},{8,0},{12,4},{16,24},{20,28},{24,16},{28,20},{1,9},{5... | collective-permute-start | bytes 1572872 | tf_op jit(solution)/shard_map/ppermute | solution.py:457
  19.1 25.8 %collective-permute-start.11 = (bf16[2,512,256]{2,1,0:T(8,128)(2,1)}, bf16[2,512,256]{2,1,0:T(8,128)(2,1)S(1)}, u32[]{:S(2)}, u32[]{:S(2)}) collective-permute-start(bf16[2,512,256]{2,1,0:T(8,128)(2,1)} %get-tuple-element.59), channel_id=1, source_target_pairs={{0,12},{4,8},{8,4},{12,0},{16,28},{20,24},{24,20},{28,16},{1,13},{... | collective-permute-start | bytes 1572872 | tf_op jit(solution)/shard_map/ppermute | solution.py:457
  30.3 19.4 %all-to-all-start = ((bf16[8,80,256]{2,1,0:T(8,128)(2,1)}), bf16[8,80,256]{2,1,0:T(8,128)(2,1)S(1)}, u32[]{:S(2)}, u32[]{:S(2)}) async-start(bf16[8,80,256]{2,1,0:T(8,128)(2,1)} %pack.1), calls=%async_computation | async-start | bytes 655360 | tf_op jit(solution)/shard_map/all_to_all | solution.py:481
  36.4 22.8 %collective-permute-start.12 = (bf16[2,512,256]{2,1,0:T(8,128)(2,1)S(1)}, bf16[2,512,256]{2,1,0:T(8,128)(2,1)S(1)}, u32[]{:S(2)}, u32[]{:S(2)}) collective-permute-start(bf16[2,512,256]{2,1,0:T(8,128)(2,1)S(1)} %get-tuple-element.53.refs_0_), channel_id=1, source_target_pairs={{0,1},{1,0},{2,3},{3,2},{4,5},{5,4},{6,7},{7,6},{8,9},{9,8},{10,11... | collective-permute-start | bytes 1572872 | tf_op jit(solution)/shard_map/ppermute | solution.py:457
  36.4 23.8 %collective-permute-start.13 = (bf16[2,512,256]{2,1,0:T(8,128)(2,1)S(1)}, bf16[2,512,256]{2,1,0:T(8,128)(2,1)S(1)}, u32[]{:S(2)}, u32[]{:S(2)}) collective-permute-start(bf16[2,512,256]{2,1,0:T(8,128)(2,1)S(1)} %collective-permute-done.9.refs_1_), channel_id=1, source_target_pairs={{0,1},{1,0},{2,3},{3,2},{4,5},{5,4},{6,7},{7,6},{8,9},{9,8},{10,11... | collective-permute-start | bytes 1572872 | tf_op jit(solution)/shard_map/ppermute | solution.py:457
  36.9 23.6 %collective-permute-start.14 = (bf16[2,512,256]{2,1,0:T(8,128)(2,1)S(1)}, bf16[2,512,256]{2,1,0:T(8,128)(2,1)}, u32[]{:S(2)}, u32[]{:S(2)}) collective-permute-start(bf16[2,512,256]{2,1,0:T(8,128)(2,1)S(1)} %collective-permute-done.10.refs_2_), channel_id=1, source_target_pairs={{0,1},{1,0},{2,3},{3,2},{4,5},{5,4},{6,7},{7,6},{8,9},{9,8},{10,11... | collective-permute-start | bytes 1572872 | tf_op jit(solution)/shard_map/ppermute | solution.py:457
  44.9 16.7 %collective-permute-start.15 = (bf16[2,512,256]{2,1,0:T(8,128)(2,1)S(1)}, bf16[2,512,256]{2,1,0:T(8,128)(2,1)}, u32[]{:S(2)}, u32[]{:S(2)}) collective-permute-start(bf16[2,512,256]{2,1,0:T(8,128)(2,1)S(1)} %collective-permute-done.11.refs_3_), channel_id=1, source_target_pairs={{0,1},{1,0},{2,3},{3,2},{4,5},{5,4},{6,7},{7,6},{8,9},{9,8},{10,11... | collective-permute-start | bytes 1572872 | tf_op jit(solution)/shard_map/ppermute | solution.py:457
  55.0 8.2 %collective-permute-start.16 = (bf16[256,256]{1,0:T(8,128)(2,1)S(1)}, bf16[256,256]{1,0:T(8,128)(2,1)S(1)}, u32[]{:S(2)}, u32[]{:S(2)}) collective-permute-start(bf16[256,256]{1,0:T(8,128)(2,1)S(1)} %get-tuple-element.46.refs_1_), channel_id=1, source_target_pairs={{0,16},{4,20},{8,24},{12,28},{16,0},{20,4},{24,8},{28,12},{1,17},{... | collective-permute-start | bytes 393224 | tf_op jit(solution)/shard_map/ppermute | solution.py:457
  60.2 6.3 %collective-permute-start.5 = (bf16[256,256]{1,0:T(8,128)(2,1)S(1)}, bf16[256,256]{1,0:T(8,128)(2,1)S(1)}, u32[]{:S(2)}, u32[]{:S(2)}) collective-permute-start(bf16[256,256]{1,0:T(8,128)(2,1)S(1)} %get-tuple-element.52.refs_0_.refs_8_), channel_id=1, source_target_pairs={{0,2},{1,3},{2,0},{3,1},{4,6},{5,7},{6,4},{7,5},{8,10},{9,11},{10,... | collective-permute-start | bytes 393224 | tf_op jit(solution)/shard_map/ppermute | solution.py:457
  60.5 7.1 %collective-permute-start.19 = (bf16[256,256]{1,0:T(8,128)(2,1)S(1)}, bf16[256,256]{1,0:T(8,128)(2,1)S(1)}, u32[]{:S(2)}, u32[]{:S(2)}) collective-permute-start(bf16[256,256]{1,0:T(8,128)(2,1)S(1)} %get-tuple-element.52.refs_0_.refs_8_), channel_id=1, source_target_pairs={{0,8},{4,12},{8,0},{12,4},{16,24},{20,28},{24,16},{28,20},{1,9},{5... | collective-permute-start | bytes 393224 | tf_op jit(solution)/shard_map/ppermute | solution.py:457
  61.7 7.6 %collective-permute-start.6 = (bf16[256,256]{1,0:T(8,128)(2,1)S(1)}, bf16[256,256]{1,0:T(8,128)(2,1)S(1)}, u32[]{:S(2)}, u32[]{:S(2)}) collective-permute-start(bf16[256,256]{1,0:T(8,128)(2,1)S(1)} %get-tuple-element.46.refs_1_), channel_id=1, source_target_pairs={{0,2},{1,3},{2,0},{3,1},{4,6},{5,7},{6,4},{7,5},{8,10},{9,11},{10,... | collective-permute-start | bytes 393224 | tf_op jit(solution)/shard_map/ppermute | solution.py:457
  63.2 6.4 %collective-permute-start.18 = (bf16[256,256]{1,0:T(8,128)(2,1)S(1)}, bf16[256,256]{1,0:T(8,128)(2,1)S(1)}, u32[]{:S(2)}, u32[]{:S(2)}) collective-permute-start(bf16[256,256]{1,0:T(8,128)(2,1)S(1)} %collective-permute-done.16.refs_9_), channel_id=1, source_target_pairs={{0,4},{4,0},{8,12},{12,8},{16,20},{20,16},{24,28},{28,24},{1,5},{5... | collective-permute-start | bytes 393224 | tf_op jit(solution)/shard_map/ppermute | solution.py:457
  64.2 7.9 %collective-permute-start.27 = (bf16[256,256]{1,0:T(8,128)(2,1)S(1)}, bf16[256,256]{1,0:T(8,128)(2,1)S(1)}, u32[]{:S(2)}, u32[]{:S(2)}) collective-permute-start(bf16[256,256]{1,0:T(8,128)(2,1)S(1)} %collective-permute-done.17.refs_10_), channel_id=1, source_target_pairs={{0,2},{1,3},{2,0},{3,1},{4,6},{5,7},{6,4},{7,5},{8,10},{9,11},{10,... | collective-permute-start | bytes 393224 | tf_op jit(solution)/shard_map/ppermute | solution.py:457
  66.5 6.1 %collective-permute-start.20 = (bf16[256,256]{1,0:T(8,128)(2,1)S(1)}, bf16[256,256]{1,0:T(8,128)(2,1)S(1)}, u32[]{:S(2)}, u32[]{:S(2)}) collective-permute-start(bf16[256,256]{1,0:T(8,128)(2,1)S(1)} %collective-permute-done.16.refs_9_), channel_id=1, source_target_pairs={{0,8},{4,12},{8,0},{12,4},{16,24},{20,28},{24,16},{28,20},{1,9},{5... | collective-permute-start | bytes 393224 | tf_op jit(solution)/shard_map/ppermute | solution.py:457
  67.6 6.6 %collective-permute-start.29 = (bf16[256,256]{1,0:T(8,128)(2,1)S(1)}, bf16[256,256]{1,0:T(8,128)(2,1)S(1)}, u32[]{:S(2)}, u32[]{:S(2)}) collective-permute-start(bf16[256,256]{1,0:T(8,128)(2,1)S(1)} %collective-permute-done.5.refs_4_.refs_8_), channel_id=1, source_target_pairs={{0,8},{4,12},{8,0},{12,4},{16,24},{20,28},{24,16},{28,20},{1,9},{5... | collective-permute-start | bytes 393224 | tf_op jit(solution)/shard_map/ppermute | solution.py:457
  69.6 6.5 %collective-permute-start.28 = (bf16[256,256]{1,0:T(8,128)(2,1)S(1)}, bf16[256,256]{1,0:T(8,128)(2,1)S(1)}, u32[]{:S(2)}, u32[]{:S(2)}) collective-permute-start(bf16[256,256]{1,0:T(8,128)(2,1)S(1)} %collective-permute-done.18.refs_11_), channel_id=1, source_target_pairs={{0,2},{1,3},{2,0},{3,1},{4,6},{5,7},{6,4},{7,5},{8,10},{9,11},{10,... | collective-permute-start | bytes 393224 | tf_op jit(solution)/shard_map/ppermute | solution.py:457
  74.1 8.0 %collective-permute-start.31 = (bf16[256,256]{1,0:T(8,128)(2,1)S(1)}, bf16[256,256]{1,0:T(8,128)(2,1)S(1)}, u32[]{:S(2)}, u32[]{:S(2)}) collective-permute-start(bf16[256,256]{1,0:T(8,128)(2,1)S(1)} %collective-permute-done.27.refs_10_), channel_id=1, source_target_pairs={{0,8},{4,12},{8,0},{12,4},{16,24},{20,28},{24,16},{28,20},{1,9},{5... | collective-permute-start | bytes 393224 | tf_op jit(solution)/shard_map/ppermute | solution.py:457
  75.2 7.4 %collective-permute-start.30 = (bf16[256,256]{1,0:T(8,128)(2,1)S(1)}, bf16[256,256]{1,0:T(8,128)(2,1)S(1)}, u32[]{:S(2)}, u32[]{:S(2)}) collective-permute-start(bf16[256,256]{1,0:T(8,128)(2,1)S(1)} %collective-permute-done.26.refs_9_), channel_id=1, source_target_pairs={{0,8},{4,12},{8,0},{12,4},{16,24},{20,28},{24,16},{28,20},{1,9},{5... | collective-permute-start | bytes 393224 | tf_op jit(solution)/shard_map/ppermute | solution.py:457
  76.2 6.6 %collective-permute-start.32 = (bf16[256,256]{1,0:T(8,128)(2,1)S(1)}, bf16[256,256]{1,0:T(8,128)(2,1)S(1)}, u32[]{:S(2)}, u32[]{:S(2)}) collective-permute-start(bf16[256,256]{1,0:T(8,128)(2,1)S(1)} %collective-permute-done.28.refs_11_), channel_id=1, source_target_pairs={{0,8},{4,12},{8,0},{12,4},{16,24},{20,28},{24,16},{28,20},{1,9},{5... | collective-permute-start | bytes 393224 | tf_op jit(solution)/shard_map/ppermute | solution.py:457
  77.3 8.9 %collective-permute-start.3 = (bf16[256,256]{1,0:T(8,128)(2,1)S(1)}, bf16[256,256]{1,0:T(8,128)(2,1)S(1)}, u32[]{:S(2)}, u32[]{:S(2)}) collective-permute-start(bf16[256,256]{1,0:T(8,128)(2,1)S(1)} %get-tuple-element.52.refs_0_.refs_8_), channel_id=1, source_target_pairs={{0,1},{1,0},{2,3},{3,2},{4,5},{5,4},{6,7},{7,6},{8,9},{9,8},{10,11... | collective-permute-start | bytes 393224 | tf_op jit(solution)/shard_map/ppermute | solution.py:457
  78.5 7.8 %collective-permute-start.4 = (bf16[256,256]{1,0:T(8,128)(2,1)S(1)}, bf16[256,256]{1,0:T(8,128)(2,1)S(1)}, u32[]{:S(2)}, u32[]{:S(2)}) collective-permute-start(bf16[256,256]{1,0:T(8,128)(2,1)S(1)} %get-tuple-element.46.refs_1_), channel_id=1, source_target_pairs={{0,1},{1,0},{2,3},{3,2},{4,5},{5,4},{6,7},{7,6},{8,9},{9,8},{10,11... | collective-permute-start | bytes 393224 | tf_op jit(solution)/shard_map/ppermute | solution.py:457
  82.1 6.6 %collective-permute-start.7 = (bf16[256,256]{1,0:T(8,128)(2,1)S(1)}, bf16[256,256]{1,0:T(8,128)(2,1)S(1)}, u32[]{:S(2)}, u32[]{:S(2)}) collective-permute-start(bf16[256,256]{1,0:T(8,128)(2,1)S(1)} %collective-permute-done.5.refs_4_.refs_8_), channel_id=1, source_target_pairs={{0,1},{1,0},{2,3},{3,2},{4,5},{5,4},{6,7},{7,6},{8,9},{9,8},{10,11... | collective-permute-start | bytes 393224 | tf_op jit(solution)/shard_map/ppermute | solution.py:457
  82.7 7.2 %collective-permute-start.8 = (bf16[256,256]{1,0:T(8,128)(2,1)S(1)}, bf16[256,256]{1,0:T(8,128)(2,1)S(1)}, u32[]{:S(2)}, u32[]{:S(2)}) collective-permute-start(bf16[256,256]{1,0:T(8,128)(2,1)S(1)} %collective-permute-done.6.refs_5_), channel_id=1, source_target_pairs={{0,1},{1,0},{2,3},{3,2},{4,5},{5,4},{6,7},{7,6},{8,9},{9,8},{10,11... | collective-permute-start | bytes 393224 | tf_op jit(solution)/shard_map/ppermute | solution.py:457
  82.8 9.5 %collective-permute-start.23 = (bf16[256,256]{1,0:T(8,128)(2,1)S(1)}, bf16[256,256]{1,0:T(8,128)(2,1)S(1)}, u32[]{:S(2)}, u32[]{:S(2)}) collective-permute-start(bf16[256,256]{1,0:T(8,128)(2,1)S(1)} %get-tuple-element.61), channel_id=1, source_target_pairs={{0,16},{4,20},{8,24},{12,28},{16,0},{20,4},{24,8},{28,12},{1,17},{... | collective-permute-start | bytes 393224 | tf_op jit(solution)/shard_map/ppermute | solution.py:457
  86.2 17.5 %collective-permute-start.24 = (f32[256,256]{1,0:T(8,128)S(1)}, f32[256,256]{1,0:T(8,128)S(1)}, u32[]{:S(2)}, u32[]{:S(2)}) collective-permute-start(f32[256,256]{1,0:T(8,128)S(1)} %get-tuple-element.62), channel_id=1, source_target_pairs={{0,1},{1,0},{2,3},{3,2},{4,5},{5,4},{6,7},{7,6},{8,9},{9,8},{10,11... | collective-permute-start | bytes 786440 | tf_op jit(solution)/shard_map/ppermute | solution.py:457
  86.2 23.0 %collective-permute-start.34 = (f32[256,256]{1,0:T(8,128)S(1)}, f32[256,256]{1,0:T(8,128)S(1)}, u32[]{:S(2)}, u32[]{:S(2)}) collective-permute-start(f32[256,256]{1,0:T(8,128)S(1)} %get-tuple-element.66), channel_id=1, source_target_pairs={{0,1},{1,0},{2,3},{3,2},{4,5},{5,4},{6,7},{7,6},{8,9},{9,8},{10,11... | collective-permute-start | bytes 786440 | tf_op jit(solution)/shard_map/ppermute | solution.py:457
  88.7 14.9 %collective-permute-start.25 = (bf16[256,256]{1,0:T(8,128)(2,1)S(1)}, bf16[256,256]{1,0:T(8,128)(2,1)S(1)}, u32[]{:S(2)}, u32[]{:S(2)}) collective-permute-start(bf16[256,256]{1,0:T(8,128)(2,1)S(1)} %get-tuple-element.63), channel_id=1, source_target_pairs={{0,17},{1,16},{2,19},{3,18},{4,21},{5,20},{6,23},{7,22},{8,25},{9,... | collective-permute-start | bytes 393224 | tf_op jit(solution)/shard_map/ppermute | solution.py:457
  89.9 17.1 %collective-permute-start.33 = (bf16[256,256]{1,0:T(8,128)(2,1)S(1)}, bf16[256,256]{1,0:T(8,128)(2,1)S(1)}, u32[]{:S(2)}, u32[]{:S(2)}) collective-permute-start(bf16[256,256]{1,0:T(8,128)(2,1)S(1)} %get-tuple-element.65), channel_id=1, source_target_pairs={{0,16},{4,20},{8,24},{12,28},{16,0},{20,4},{24,8},{28,12},{1,17},{... | collective-permute-start | bytes 393224 | tf_op jit(solution)/shard_map/ppermute | solution.py:457
  92.3 16.9 %collective-permute-start.35 = (bf16[256,256]{1,0:T(8,128)(2,1)S(1)}, bf16[256,256]{1,0:T(8,128)(2,1)S(1)}, u32[]{:S(2)}, u32[]{:S(2)}) collective-permute-start(bf16[256,256]{1,0:T(8,128)(2,1)S(1)} %get-tuple-element.67), channel_id=1, source_target_pairs={{0,17},{1,16},{2,19},{3,18},{4,21},{5,20},{6,23},{7,22},{8,25},{9,... | collective-permute-start | bytes 393224 | tf_op jit(solution)/shard_map/ppermute | solution.py:457
  (15 other events, 63.2 us)

commit v4 on v3

--- a/solution.py
+++ b/solution.py
@@ -473,19 +473,22 @@
     core = swap(away, "mp", 1)
     *xs, pick, meta = slots(d, dest, lengths, offsets, after(x, away), learners, per)
     half = after(keep, pick) + core
-    xs = [xs[0]] + [swap(after(xs[f], half), "dp", f) for f in range(1, learners // 2)]
     across = swap(half, "mp", 2)
-    away, keep = project(m, after(x, half), w_key, w_value, 0)
+    xs_core = [swap(after(xs[0], half), "mp", 1)]
+    xs[1:3] = [swap(after(xs[f], half), "dp", f) for f in (1, 2)]
+    xs[3] = swap(after(xs[3], xs[1], xs[2]), "dp", 3)
+    away, keep = project(m, after(x, xs_core[0]), w_key, w_value, 0)
     core = swap(away, "mp", 1)
     kv = pack(d, keep, core, across, pick, meta)
     kv = lax.all_to_all(kv[0], "dp", split_axis=0, concat_axis=0, tiled=True)
+    kv = after(kv, xs[3])
 
     beyond, out1, place1 = attention(d, kv, queries, out_grad, lmax, learners, 1)
     there = swap(beyond, "dp", 4)
     grads, out0, place0 = attention(d, after(kv, beyond), queries, out_grad, lmax, learners, 0)
     place = [place0, place1]
 
-    xs = xs + [swap(b, "mp", 1) for b in xs]
+    xs = xs + xs_core + [swap(b, "mp", 1) for b in xs[1:]]
     near = {(0, 0, 0): grads, (0, 0, 1): there}
     hops = [
         ((0, 0), "dp", 1), ((0, 0), "dp", 2), ((0, 0), "mp", 2), ((2, 0), "dp", 1),

time: 111 us -> 108 us (0.973)
  waiting for transfers between devices: 37.1 us -> 32.4 us
  starting transfers between devices: 35.3 us -> 37.1 us
    ppermute x36, waiting for transfers between devices: 32.4 us -> 28.1 us  [swap(): return lax.ppermute(x, axis, [(i, i ^ code) for i in range(size)])]
    ppermute x36, starting transfers between devices: 29.2 us -> 32.2 us  [swap(): return lax.ppermute(x, axis, [(i, i ^ code) for i in range(size)])]
    all_to_all x1, starting transfers between devices: 6.07 us -> 4.88 us  [local(): kv = lax.all_to_all(kv[0], 'dp', split_axis=0, concat_axis=0, tiled=True)]
  transfers between devices with their start and end apart: 37 -> 37, of which waited for: 11 -> 11; matrix products, arithmetic and copies ran while one was open for 0% -> 0% of each run, Pallas kernels for 21% -> 25%
where the time goes in v4:
time: 108 us; the launch traced here: 107 us
  starting transfers between devices  37.1 us (34%)
  Pallas kernels  32.5 us (30%)
  waiting for transfers between devices  32.4 us (30%)
  local copies, waits for them, and re-layouts  3.52 us (3%)
  other arithmetic  1.11 us (1%)
    ppermute x36, starting transfers between devices, swap(): return lax.ppermute(x, axis, [(i, i ^ code) for i in range(size)])  32.2 us
    ppermute x36, waiting for transfers between devices, swap(): return lax.ppermute(x, axis, [(i, i ^ code) for i in range(size)])  28.1 us
    pallas_call x2, Pallas kernels, project(): pl.pallas_call(project_kernel, out_shape=(jax.ShapeDtypeStruct(out, F32),...  8.37 us
    pallas_call x4, Pallas kernels, weight_grads(): pl.pallas_call(kernel, out_shape=(jax.ShapeDtypeStruct(out, dtype),) * 2,...  7.32 us
    pallas_call x2, Pallas kernels, attention(): pl.pallas_call(functools.partial(attention_kernel, lmax, learners, half),...  5.78 us
    all_to_all x1, starting transfers between devices, local(): kv = lax.all_to_all(kv[0], 'dp', split_axis=0, concat_axis=0, tiled=True)  4.88 us
    pallas_call x1, Pallas kernels, row_grads(): pl.pallas_call(rows_kernel, out_shape=jax.ShapeDtypeStruct((rows, feats),...  4.78 us
    all_to_all x1, waiting for transfers between devices, local(): kv = lax.all_to_all(kv[0], 'dp', split_axis=0, concat_axis=0, tiled=True)  4.27 us
  transfers between devices with their start and end apart: 37, of which 11 were waited for; matrix products, arithmetic and copies ran while one was open for 0% of the time, Pallas kernels for 25%

profile of v4, /device:TPU:0, one launch (start us, length us, event | category | flops | bytes accessed | tf_op | source)
XLA Modules:
  0.0 107.4 jit_solution(10463497345736553665)
XLA Ops:
  0.7 4.3 %project.2 = (f32[512,256]{1,0:T(8,128)}, f32[512,256]{1,0:T(8,128)}) custom-call(s32[1]{0:T(128)} %bitcast.1.me_ref, bf16[512,2048]{1,0:T(8,128)(2,1)} %bitcast.6, bf16[2048,512]{1,0:T(8,128)(2,1)} %refs_8_.1, bf16[2048,512]{1,0:T(8,128)(2,1)} %refs_9_.1), custom_call_target="tpu_custom_call" | custom-call | tf_op jit(solution)/shard_map/project/pallas_call | solution.py:167
  5.4 2.4 %slots.1 = (bf16[2,512,256]{2,1,0:T(8,128)(2,1)S(1)}, bf16[2,512,256]{2,1,0:T(8,128)(2,1)S(1)}, bf16[2,512,256]{2,1,0:T(8,128)(2,1)S(1)}, bf16[2,512,256]{2,1,0:...) custom-call(s32[1]{0:T(128)} %bitcast.me_ref, s32[1,32]{1,0:T(1,128)S(1)} %bitcast.9, ...), custom_call_target="tpu_custom_call" | custom-call | tf_op jit(solution)/shard_map/slots/pallas_call | solution.py:222
  9.0 3.0 %collective-permute-start.5 = (bf16[2,512,256]{2,1,0:T(8,128)(2,1)S(1)}, bf16[2,512,256]{2,1,0:T(8,128)(2,1)S(1)}, u32[]{:S(2)}, u32[]{:S(2)}) collective-permute-start(bf16[2,512,256]{2,1,0:T(8,128)(2,1)S(1)} %get-tuple-element.54), channel_id=1, source_target_pairs={{0,8},{4,12},{8,0},{12,4},{16,24},{20,28},{24,16},{28,20},{1,9},{5... | collective-permute-start | bytes 1572872 | tf_op jit(solution)/shard_map/ppermute | solution.py:457
  12.0 1.5 %collective-permute-start.4 = (bf16[2,512,256]{2,1,0:T(8,128)(2,1)S(1)}, bf16[2,512,256]{2,1,0:T(8,128)(2,1)S(1)}, u32[]{:S(2)}, u32[]{:S(2)}) collective-permute-start(bf16[2,512,256]{2,1,0:T(8,128)(2,1)S(1)} %get-tuple-element.52), channel_id=1, source_target_pairs={{0,4},{4,0},{8,12},{12,8},{16,20},{20,16},{24,28},{28,24},{1,5},{5... | collective-permute-start | bytes 1572872 | tf_op jit(solution)/shard_map/ppermute | solution.py:457
  13.6 1.5 %collective-permute-start.3 = (f32[512,256]{1,0:T(8,128)S(1)}, f32[512,256]{1,0:T(8,128)S(1)}, u32[]{:S(2)}, u32[]{:S(2)}) collective-permute-start(f32[512,256]{1,0:T(8,128)S(1)} %add.3), channel_id=1, source_target_pairs={{0,2},{1,3},{2,0},{3,1},{4,6},{5,7},{6,4},{7,5},{8,10},{9,11},{10,... | collective-permute-start | bytes 1572872 | tf_op jit(solution)/shard_map/ppermute | solution.py:457
  15.1 4.1 %project.3 = (f32[512,256]{1,0:T(8,128)}, f32[512,256]{1,0:T(8,128)}) custom-call(s32[1]{0:T(128)} %bitcast.1.me_ref, bf16[512,2048]{1,0:T(8,128)(2,1)} %bitcast.7, bf16[2048,512]{1,0:T(8,128)(2,1)} %refs_8_.1, bf16[2048,512]{1,0:T(8,128)(2,1)} %refs_9_.1), custom_call_target="tpu_custom_call" | custom-call | tf_op jit(solution)/shard_map/project/pallas_call | solution.py:167
  19.2 5.0 %collective-permute-done.5.refs_2_ = bf16[2,512,256]{2,1,0:T(8,128)(2,1)S(1)} collective-permute-done((bf16[2,512,256]{2,1,0:T(8,128)(2,1)S(1)}, bf16[2,512,256]{2,1,0:T(8,128)(2,1)S(1)}, u32[]{:S(2)}, u32[]{:S(2)}) %collective-permute-start.5) | collective-permute-done | bytes 524320 | tf_op jit(solution)/shard_map/ppermute | solution.py:457
  24.2 1.5 %collective-permute-done.4.refs_1_ = bf16[2,512,256]{2,1,0:T(8,128)(2,1)S(1)} collective-permute-done((bf16[2,512,256]{2,1,0:T(8,128)(2,1)S(1)}, bf16[2,512,256]{2,1,0:T(8,128)(2,1)S(1)}, u32[]{:S(2)}, u32[]{:S(2)}) %collective-permute-start.4) | collective-permute-done | bytes 524320 | tf_op jit(solution)/shard_map/ppermute | solution.py:457
  25.7 1.4 %collective-permute-start.6 = (bf16[2,512,256]{2,1,0:T(8,128)(2,1)}, bf16[2,512,256]{2,1,0:T(8,128)(2,1)S(1)}, u32[]{:S(2)}, u32[]{:S(2)}) collective-permute-start(bf16[2,512,256]{2,1,0:T(8,128)(2,1)} %get-tuple-element.55), channel_id=1, source_target_pairs={{0,12},{4,8},{8,4},{12,0},{16,28},{20,24},{24,20},{28,16},{1,13},{... | collective-permute-start | bytes 1572872 | tf_op jit(solution)/shard_map/ppermute | solution.py:457
  29.2 4.9 %all-to-all-start = ((bf16[8,80,256]{2,1,0:T(8,128)(2,1)}), bf16[8,80,256]{2,1,0:T(8,128)(2,1)S(1)}, u32[]{:S(2)}, u32[]{:S(2)}) async-start(bf16[8,80,256]{2,1,0:T(8,128)(2,1)} %pack.1), calls=%async_computation | async-start | bytes 655360 | tf_op jit(solution)/shard_map/all_to_all | solution.py:483
  34.6 8.0 %collective-permute-done.6.refs_3_ = bf16[2,512,256]{2,1,0:T(8,128)(2,1)S(1)} collective-permute-done((bf16[2,512,256]{2,1,0:T(8,128)(2,1)}, bf16[2,512,256]{2,1,0:T(8,128)(2,1)S(1)}, u32[]{:S(2)}, u32[]{:S(2)}) %collective-permute-start.6) | collective-permute-done | bytes 524320 | tf_op jit(solution)/shard_map/ppermute | solution.py:457
  42.6 4.3 %all-to-all-done.kv_ref = bf16[8,80,256]{2,1,0:T(8,128)(2,1)S(1)} async-done(((bf16[8,80,256]{2,1,0:T(8,128)(2,1)}), bf16[8,80,256]{2,1,0:T(8,128)(2,1)S(1)}, u32[]{:S(2)}, u32[]{:S(2)}) %all-to-all-start) | async-done | bytes 327712 | tf_op jit(solution)/shard_map/all_to_all | solution.py:483
  49.4 2.9 %attention.2 = (bf16[256,256]{1,0:T(8,128)(2,1)S(1)}, bf16[256,1024]{1,0:T(8,128)(2,1)S(1)}, bf16[256,512]{1,0:T(8,128)(2,1)S(1)}) custom-call(s32[1]{0:T(128)} %bitcast.me_ref, bf16[8,80,256]{2,1,0:T(8,128)(2,1)S(1)} %all-to-all-done.kv_ref, bf16[512,1024]{1,0:T(8,128)(2,1)S(1)} %copy-done.3, bf16[512,1024]{1,0:T(8,128)(2,1)S(1)} %copy-done.4), custom_call_target="tpu_custom_call" | custom-call | tf_op jit(solution)/shard_map/attention/pallas_call | solution.py:320
  52.4 2.9 %attention.3 = (bf16[256,256]{1,0:T(8,128)(2,1)S(1)}, bf16[256,1024]{1,0:T(8,128)(2,1)S(1)}, bf16[256,512]{1,0:T(8,128)(2,1)S(1)}) custom-call(s32[1]{0:T(128)} %bitcast.me_ref, bf16[8,80,256]{2,1,0:T(8,128)(2,1)S(1)} %all-to-all-done.kv_ref, bf16[512,1024]{1,0:T(8,128)(2,1)S(1)} %copy-done.3, bf16[512,1024]{1,0:T(8,128)(2,1)S(1)} %copy-done.4), custom_call_target="tpu_custom_call" | custom-call | tf_op jit(solution)/shard_map/attention/pallas_call | solution.py:320
  56.3 1.5 %collective-permute-start.9 = (bf16[256,256]{1,0:T(8,128)(2,1)S(1)}, bf16[256,256]{1,0:T(8,128)(2,1)S(1)}, u32[]{:S(2)}, u32[]{:S(2)}) collective-permute-start(bf16[256,256]{1,0:T(8,128)(2,1)S(1)} %get-tuple-element.63.refs_0_.refs_8_), channel_id=1, source_target_pairs={{0,2},{1,3},{2,0},{3,1},{4,6},{5,7},{6,4},{7,5},{8,10},{9,11},{10,... | collective-permute-start | bytes 393224 | tf_op jit(solution)/shard_map/ppermute | solution.py:457
  57.8 1.5 %collective-permute-start.19 = (bf16[256,256]{1,0:T(8,128)(2,1)S(1)}, bf16[256,256]{1,0:T(8,128)(2,1)S(1)}, u32[]{:S(2)}, u32[]{:S(2)}) collective-permute-start(bf16[256,256]{1,0:T(8,128)(2,1)S(1)} %get-tuple-element.63.refs_0_.refs_8_), channel_id=1, source_target_pairs={{0,8},{4,12},{8,0},{12,4},{16,24},{20,28},{24,16},{28,20},{1,9},{5... | collective-permute-start | bytes 393224 | tf_op jit(solution)/shard_map/ppermute | solution.py:457
  60.8 1.5 %collective-permute-start.27 = (bf16[256,256]{1,0:T(8,128)(2,1)S(1)}, bf16[256,256]{1,0:T(8,128)(2,1)S(1)}, u32[]{:S(2)}, u32[]{:S(2)}) collective-permute-start(bf16[256,256]{1,0:T(8,128)(2,1)S(1)} %collective-permute-done.17.refs_10_), channel_id=1, source_target_pairs={{0,2},{1,3},{2,0},{3,1},{4,6},{5,7},{6,4},{7,5},{8,10},{9,11},{10,... | collective-permute-start | bytes 393224 | tf_op jit(solution)/shard_map/ppermute | solution.py:457
  62.3 1.9 %collective-permute-start.20 = (bf16[256,256]{1,0:T(8,128)(2,1)S(1)}, bf16[256,256]{1,0:T(8,128)(2,1)S(1)}, u32[]{:S(2)}, u32[]{:S(2)}) collective-permute-start(bf16[256,256]{1,0:T(8,128)(2,1)S(1)} %collective-permute-done.16.refs_9_), channel_id=1, source_target_pairs={{0,8},{4,12},{8,0},{12,4},{16,24},{20,28},{24,16},{28,20},{1,9},{5... | collective-permute-start | bytes 393224 | tf_op jit(solution)/shard_map/ppermute | solution.py:457
  65.5 1.5 %collective-permute-start.26 = (bf16[256,256]{1,0:T(8,128)(2,1)S(1)}, bf16[256,256]{1,0:T(8,128)(2,1)S(1)}, u32[]{:S(2)}, u32[]{:S(2)}) collective-permute-start(bf16[256,256]{1,0:T(8,128)(2,1)S(1)} %collective-permute-done.16.refs_9_), channel_id=1, source_target_pairs={{0,2},{1,3},{2,0},{3,1},{4,6},{5,7},{6,4},{7,5},{8,10},{9,11},{10,... | collective-permute-start | bytes 393224 | tf_op jit(solution)/shard_map/ppermute | solution.py:457
  70.3 1.5 %collective-permute-start.31 = (bf16[256,256]{1,0:T(8,128)(2,1)S(1)}, bf16[256,256]{1,0:T(8,128)(2,1)S(1)}, u32[]{:S(2)}, u32[]{:S(2)}) collective-permute-start(bf16[256,256]{1,0:T(8,128)(2,1)S(1)} %collective-permute-done.27.refs_10_), channel_id=1, source_target_pairs={{0,8},{4,12},{8,0},{12,4},{16,24},{20,28},{24,16},{28,20},{1,9},{5... | collective-permute-start | bytes 393224 | tf_op jit(solution)/shard_map/ppermute | solution.py:457
  72.5 1.4 %collective-permute-start.32 = (bf16[256,256]{1,0:T(8,128)(2,1)S(1)}, bf16[256,256]{1,0:T(8,128)(2,1)S(1)}, u32[]{:S(2)}, u32[]{:S(2)}) collective-permute-start(bf16[256,256]{1,0:T(8,128)(2,1)S(1)} %collective-permute-done.28.refs_11_), channel_id=1, source_target_pairs={{0,8},{4,12},{8,0},{12,4},{16,24},{20,28},{24,16},{28,20},{1,9},{5... | collective-permute-start | bytes 393224 | tf_op jit(solution)/shard_map/ppermute | solution.py:457
  74.7 1.8 %weight_grads.5 = (bf16[256,256]{1,0:T(8,128)(2,1)S(1)}, bf16[256,256]{1,0:T(8,128)(2,1)S(1)}) custom-call(bf16[2,512,256]{2,1,0:T(8,128)(2,1)S(1)} %get-tuple-element.45.refs_0_, bf16[2,512,256]{2,1,0:T(8,128)(2,1)S(1)} %collective-permute-done.4.refs_1_, bf16[2,512,256]{2,1,0:T(8,128)(2,1)S(1)} %collective-permute-done.5.refs_2_, ...), custom_call_target="tpu_custom_call" | custom-call | tf_op jit(solution)/shard_map/weight_grads/pallas_call | solution.py:414
  76.5 1.8 %weight_grads.4 = (f32[256,256]{1,0:T(8,128)S(1)}, f32[256,256]{1,0:T(8,128)S(1)}) custom-call(bf16[2,512,256]{2,1,0:T(8,128)(2,1)S(1)} %get-tuple-element.45.refs_0_, bf16[2,512,256]{2,1,0:T(8,128)(2,1)S(1)} %collective-permute-done.4.refs_1_, bf16[2,512,256]{2,1,0:T(8,128)(2,1)S(1)} %collective-permute-done.5.refs_2_, ...), custom_call_target="tpu_custom_call" | custom-call | tf_op jit(solution)/shard_map/weight_grads/pallas_call | solution.py:414
  79.0 2.5 %collective-permute-start.23 = (bf16[256,256]{1,0:T(8,128)(2,1)S(1)}, bf16[256,256]{1,0:T(8,128)(2,1)S(1)}, u32[]{:S(2)}, u32[]{:S(2)}) collective-permute-start(bf16[256,256]{1,0:T(8,128)(2,1)S(1)} %get-tuple-element.65), channel_id=1, source_target_pairs={{0,16},{4,20},{8,24},{12,28},{16,0},{20,4},{24,8},{28,12},{1,17},{... | collective-permute-start | bytes 393224 | tf_op jit(solution)/shard_map/ppermute | solution.py:457
  81.5 1.8 %weight_grads.6 = (f32[256,256]{1,0:T(8,128)S(1)}, f32[256,256]{1,0:T(8,128)S(1)}) custom-call(bf16[2,512,256]{2,1,0:T(8,128)(2,1)S(1)} %get-tuple-element.45.refs_0_, bf16[2,512,256]{2,1,0:T(8,128)(2,1)S(1)} %collective-permute-done.4.refs_1_, bf16[2,512,256]{2,1,0:T(8,128)(2,1)S(1)} %collective-permute-done.5.refs_2_, ...), custom_call_target="tpu_custom_call" | custom-call | tf_op jit(solution)/shard_map/weight_grads/pallas_call | solution.py:414
  83.9 1.9 %weight_grads.7 = (bf16[256,256]{1,0:T(8,128)(2,1)S(1)}, bf16[256,256]{1,0:T(8,128)(2,1)S(1)}) custom-call(bf16[2,512,256]{2,1,0:T(8,128)(2,1)S(1)} %get-tuple-element.45.refs_0_, bf16[2,512,256]{2,1,0:T(8,128)(2,1)S(1)} %collective-permute-done.4.refs_1_, bf16[2,512,256]{2,1,0:T(8,128)(2,1)S(1)} %collective-permute-done.5.refs_2_, ...), custom_call_target="tpu_custom_call" | custom-call | tf_op jit(solution)/shard_map/weight_grads/pallas_call | solution.py:414
  86.1 2.5 %collective-permute-start.33 = (bf16[256,256]{1,0:T(8,128)(2,1)S(1)}, bf16[256,256]{1,0:T(8,128)(2,1)S(1)}, u32[]{:S(2)}, u32[]{:S(2)}) collective-permute-start(bf16[256,256]{1,0:T(8,128)(2,1)S(1)} %get-tuple-element.69), channel_id=1, source_target_pairs={{0,16},{4,20},{8,24},{12,28},{16,0},{20,4},{24,8},{28,12},{1,17},{... | collective-permute-start | bytes 393224 | tf_op jit(solution)/shard_map/ppermute | solution.py:457
  88.7 1.7 %packed_rows.1 = bf16[512,1024]{1,0:T(8,128)(2,1)} custom-call(bf16[256,512]{1,0:T(8,128)(2,1)S(1)} %get-tuple-element.59.place0, bf16[256,512]{1,0:T(8,128)(2,1)S(1)} %get-tuple-element.60.place1, bf16[256,1024]{1,0:T(8,128)(2,1)S(1)} %get-tuple-element.61.out0, bf16[256,1024]{1,0:T(8,128)(2,1)S(1)} %get-tuple-element.62.out1), custom_call_target="tpu_custom_call" | custom-call | tf_op jit(solution)/shard_map/packed_rows/pallas_call | solution.py:338
  90.4 4.8 %row_grads.1 = bf16[512,2048]{1,0:T(8,128)(2,1)} custom-call(s32[1]{0:T(128)} %bitcast.1.me_ref, bf16[256,512]{1,0:T(8,128)(2,1)S(1)} %get-tuple-element.59.place0, bf16[256,512]{1,0:T(8,128)(2,1)S(1)} %get-tuple-element.60.place1, bf16[256,256]{1,0:T(8,128)(2,1)S(1)} %get-tuple-element.63.refs_0_.refs_8_, bf16[256,256]{1,0:T(8,128)(2,1)S(1)} %get-tuple-element.57.refs_1_, ...), custom_call_target="tpu_custom_call" | custom-call | tf_op jit(solution)/shard_map/row_grads/pallas_call | solution.py:381
  95.2 2.7 %collective-permute-done.25.refs_3_ = bf16[256,256]{1,0:T(8,128)(2,1)S(1)} collective-permute-done((bf16[256,256]{1,0:T(8,128)(2,1)S(1)}, bf16[256,256]{1,0:T(8,128)(2,1)S(1)}, u32[]{:S(2)}, u32[]{:S(2)}) %collective-permute-start.25) | collective-permute-done | bytes 131104 | tf_op jit(solution)/shard_map/ppermute | solution.py:457
  97.9 6.3 %collective-permute-done.33.refs_5_ = bf16[256,256]{1,0:T(8,128)(2,1)S(1)} collective-permute-done((bf16[256,256]{1,0:T(8,128)(2,1)S(1)}, bf16[256,256]{1,0:T(8,128)(2,1)S(1)}, u32[]{:S(2)}, u32[]{:S(2)}) %collective-permute-start.33) | collective-permute-done | bytes 131104 | tf_op jit(solution)/shard_map/ppermute | solution.py:457
  104.2 2.1 %collective-permute-done.35.refs_7_ = bf16[256,256]{1,0:T(8,128)(2,1)S(1)} collective-permute-done((bf16[256,256]{1,0:T(8,128)(2,1)S(1)}, bf16[256,256]{1,0:T(8,128)(2,1)S(1)}, u32[]{:S(2)}, u32[]{:S(2)}) %collective-permute-start.35) | collective-permute-done | bytes 131104 | tf_op jit(solution)/shard_map/ppermute | solution.py:457
  (76 shorter events, 18.3 us)
Async XLA Ops:
  8.9 6.2 %collective-permute-start.1 = (bf16[2,512,256]{2,1,0:T(8,128)(2,1)S(1)}, bf16[2,512,256]{2,1,0:T(8,128)(2,1)S(1)}, u32[]{:S(2)}, u32[]{:S(2)}) collective-permute-start(bf16[2,512,256]{2,1,0:T(8,128)(2,1)S(1)} %get-tuple-element.45.refs_0_), channel_id=1, source_target_pairs={{0,1},{1,0},{2,3},{3,2},{4,5},{5,4},{6,7},{7,6},{8,9},{9,8},{10,11... | collective-permute-start | bytes 1572872 | tf_op jit(solution)/shard_map/ppermute | solution.py:457
  9.0 15.2 %collective-permute-start.5 = (bf16[2,512,256]{2,1,0:T(8,128)(2,1)S(1)}, bf16[2,512,256]{2,1,0:T(8,128)(2,1)S(1)}, u32[]{:S(2)}, u32[]{:S(2)}) collective-permute-start(bf16[2,512,256]{2,1,0:T(8,128)(2,1)S(1)} %get-tuple-element.54), channel_id=1, source_target_pairs={{0,8},{4,12},{8,0},{12,4},{16,24},{20,28},{24,16},{28,20},{1,9},{5... | collective-permute-start | bytes 1572872 | tf_op jit(solution)/shard_map/ppermute | solution.py:457
  12.0 13.6 %collective-permute-start.4 = (bf16[2,512,256]{2,1,0:T(8,128)(2,1)S(1)}, bf16[2,512,256]{2,1,0:T(8,128)(2,1)S(1)}, u32[]{:S(2)}, u32[]{:S(2)}) collective-permute-start(bf16[2,512,256]{2,1,0:T(8,128)(2,1)S(1)} %get-tuple-element.52), channel_id=1, source_target_pairs={{0,4},{4,0},{8,12},{12,8},{16,20},{20,16},{24,28},{28,24},{1,5},{5... | collective-permute-start | bytes 1572872 | tf_op jit(solution)/shard_map/ppermute | solution.py:457
  13.6 13.5 %collective-permute-start.3 = (f32[512,256]{1,0:T(8,128)S(1)}, f32[512,256]{1,0:T(8,128)S(1)}, u32[]{:S(2)}, u32[]{:S(2)}) collective-permute-start(f32[512,256]{1,0:T(8,128)S(1)} %add.3), channel_id=1, source_target_pairs={{0,2},{1,3},{2,0},{3,1},{4,6},{5,7},{6,4},{7,5},{8,10},{9,11},{10,... | collective-permute-start | bytes 1572872 | tf_op jit(solution)/shard_map/ppermute | solution.py:457
  19.2 7.9 %collective-permute-start.2 = (f32[512,256]{1,0:T(8,128)}, f32[512,256]{1,0:T(8,128)S(1)}, u32[]{:S(2)}, u32[]{:S(2)}) collective-permute-start(f32[512,256]{1,0:T(8,128)} %get-tuple-element.48), channel_id=1, source_target_pairs={{0,1},{1,0},{2,3},{3,2},{4,5},{5,4},{6,7},{7,6},{8,9},{9,8},{10,11... | collective-permute-start | bytes 1572872 | tf_op jit(solution)/shard_map/ppermute | solution.py:457
  25.7 17.0 %collective-permute-start.6 = (bf16[2,512,256]{2,1,0:T(8,128)(2,1)}, bf16[2,512,256]{2,1,0:T(8,128)(2,1)S(1)}, u32[]{:S(2)}, u32[]{:S(2)}) collective-permute-start(bf16[2,512,256]{2,1,0:T(8,128)(2,1)} %get-tuple-element.55), channel_id=1, source_target_pairs={{0,12},{4,8},{8,4},{12,0},{16,28},{20,24},{24,20},{28,16},{1,13},{... | collective-permute-start | bytes 1572872 | tf_op jit(solution)/shard_map/ppermute | solution.py:457
  29.2 17.7 %all-to-all-start = ((bf16[8,80,256]{2,1,0:T(8,128)(2,1)}), bf16[8,80,256]{2,1,0:T(8,128)(2,1)S(1)}, u32[]{:S(2)}, u32[]{:S(2)}) async-start(bf16[8,80,256]{2,1,0:T(8,128)(2,1)} %pack.1), calls=%async_computation | async-start | bytes 655360 | tf_op jit(solution)/shard_map/all_to_all | solution.py:483
  34.1 22.2 %collective-permute-start.14 = (bf16[2,512,256]{2,1,0:T(8,128)(2,1)S(1)}, bf16[2,512,256]{2,1,0:T(8,128)(2,1)S(1)}, u32[]{:S(2)}, u32[]{:S(2)}) collective-permute-start(bf16[2,512,256]{2,1,0:T(8,128)(2,1)S(1)} %collective-permute-done.5.refs_2_), channel_id=1, source_target_pairs={{0,1},{1,0},{2,3},{3,2},{4,5},{5,4},{6,7},{7,6},{8,9},{9,8},{10,11... | collective-permute-start | bytes 1572872 | tf_op jit(solution)/shard_map/ppermute | solution.py:457
  34.1 23.7 %collective-permute-start.13 = (bf16[2,512,256]{2,1,0:T(8,128)(2,1)S(1)}, bf16[2,512,256]{2,1,0:T(8,128)(2,1)}, u32[]{:S(2)}, u32[]{:S(2)}) collective-permute-start(bf16[2,512,256]{2,1,0:T(8,128)(2,1)S(1)} %collective-permute-done.4.refs_1_), channel_id=1, source_target_pairs={{0,1},{1,0},{2,3},{3,2},{4,5},{5,4},{6,7},{7,6},{8,9},{9,8},{10,11... | collective-permute-start | bytes 1572872 | tf_op jit(solution)/shard_map/ppermute | solution.py:457
  42.6 16.6 %collective-permute-start.15 = (bf16[2,512,256]{2,1,0:T(8,128)(2,1)S(1)}, bf16[2,512,256]{2,1,0:T(8,128)(2,1)}, u32[]{:S(2)}, u32[]{:S(2)}) collective-permute-start(bf16[2,512,256]{2,1,0:T(8,128)(2,1)S(1)} %collective-permute-done.6.refs_3_), channel_id=1, source_target_pairs={{0,1},{1,0},{2,3},{3,2},{4,5},{5,4},{6,7},{7,6},{8,9},{9,8},{10,11... | collective-permute-start | bytes 1572872 | tf_op jit(solution)/shard_map/ppermute | solution.py:457
  52.2 7.5 %collective-permute-start.16 = (bf16[256,256]{1,0:T(8,128)(2,1)S(1)}, bf16[256,256]{1,0:T(8,128)(2,1)S(1)}, u32[]{:S(2)}, u32[]{:S(2)}) collective-permute-start(bf16[256,256]{1,0:T(8,128)(2,1)S(1)} %get-tuple-element.57.refs_1_), channel_id=1, source_target_pairs={{0,16},{4,20},{8,24},{12,28},{16,0},{20,4},{24,8},{28,12},{1,17},{... | collective-permute-start | bytes 393224 | tf_op jit(solution)/shard_map/ppermute | solution.py:457
  56.3 6.0 %collective-permute-start.9 = (bf16[256,256]{1,0:T(8,128)(2,1)S(1)}, bf16[256,256]{1,0:T(8,128)(2,1)S(1)}, u32[]{:S(2)}, u32[]{:S(2)}) collective-permute-start(bf16[256,256]{1,0:T(8,128)(2,1)S(1)} %get-tuple-element.63.refs_0_.refs_8_), channel_id=1, source_target_pairs={{0,2},{1,3},{2,0},{3,1},{4,6},{5,7},{6,4},{7,5},{8,10},{9,11},{10,... | collective-permute-start | bytes 393224 | tf_op jit(solution)/shard_map/ppermute | solution.py:457
  57.8 6.4 %collective-permute-start.19 = (bf16[256,256]{1,0:T(8,128)(2,1)S(1)}, bf16[256,256]{1,0:T(8,128)(2,1)S(1)}, u32[]{:S(2)}, u32[]{:S(2)}) collective-permute-start(bf16[256,256]{1,0:T(8,128)(2,1)S(1)} %get-tuple-element.63.refs_0_.refs_8_), channel_id=1, source_target_pairs={{0,8},{4,12},{8,0},{12,4},{16,24},{20,28},{24,16},{28,20},{1,9},{5... | collective-permute-start | bytes 393224 | tf_op jit(solution)/shard_map/ppermute | solution.py:457
  59.3 6.2 %collective-permute-start.10 = (bf16[256,256]{1,0:T(8,128)(2,1)S(1)}, bf16[256,256]{1,0:T(8,128)(2,1)S(1)}, u32[]{:S(2)}, u32[]{:S(2)}) collective-permute-start(bf16[256,256]{1,0:T(8,128)(2,1)S(1)} %get-tuple-element.57.refs_1_), channel_id=1, source_target_pairs={{0,2},{1,3},{2,0},{3,1},{4,6},{5,7},{6,4},{7,5},{8,10},{9,11},{10,... | collective-permute-start | bytes 393224 | tf_op jit(solution)/shard_map/ppermute | solution.py:457
  59.8 7.2 %collective-permute-start.18 = (bf16[256,256]{1,0:T(8,128)(2,1)S(1)}, bf16[256,256]{1,0:T(8,128)(2,1)S(1)}, u32[]{:S(2)}, u32[]{:S(2)}) collective-permute-start(bf16[256,256]{1,0:T(8,128)(2,1)S(1)} %collective-permute-done.16.refs_9_), channel_id=1, source_target_pairs={{0,4},{4,0},{8,12},{12,8},{16,20},{20,16},{24,28},{28,24},{1,5},{5... | collective-permute-start | bytes 393224 | tf_op jit(solution)/shard_map/ppermute | solution.py:457
  60.8 7.5 %collective-permute-start.27 = (bf16[256,256]{1,0:T(8,128)(2,1)S(1)}, bf16[256,256]{1,0:T(8,128)(2,1)S(1)}, u32[]{:S(2)}, u32[]{:S(2)}) collective-permute-start(bf16[256,256]{1,0:T(8,128)(2,1)S(1)} %collective-permute-done.17.refs_10_), channel_id=1, source_target_pairs={{0,2},{1,3},{2,0},{3,1},{4,6},{5,7},{6,4},{7,5},{8,10},{9,11},{10,... | collective-permute-start | bytes 393224 | tf_op jit(solution)/shard_map/ppermute | solution.py:457
  62.3 7.2 %collective-permute-start.20 = (bf16[256,256]{1,0:T(8,128)(2,1)S(1)}, bf16[256,256]{1,0:T(8,128)(2,1)S(1)}, u32[]{:S(2)}, u32[]{:S(2)}) collective-permute-start(bf16[256,256]{1,0:T(8,128)(2,1)S(1)} %collective-permute-done.16.refs_9_), channel_id=1, source_target_pairs={{0,8},{4,12},{8,0},{12,4},{16,24},{20,28},{24,16},{28,20},{1,9},{5... | collective-permute-start | bytes 393224 | tf_op jit(solution)/shard_map/ppermute | solution.py:457
  64.2 6.1 %collective-permute-start.29 = (bf16[256,256]{1,0:T(8,128)(2,1)S(1)}, bf16[256,256]{1,0:T(8,128)(2,1)S(1)}, u32[]{:S(2)}, u32[]{:S(2)}) collective-permute-start(bf16[256,256]{1,0:T(8,128)(2,1)S(1)} %collective-permute-done.9.refs_4_.refs_8_), channel_id=1, source_target_pairs={{0,8},{4,12},{8,0},{12,4},{16,24},{20,28},{24,16},{28,20},{1,9},{5... | collective-permute-start | bytes 393224 | tf_op jit(solution)/shard_map/ppermute | solution.py:457
  65.5 6.3 %collective-permute-start.26 = (bf16[256,256]{1,0:T(8,128)(2,1)S(1)}, bf16[256,256]{1,0:T(8,128)(2,1)S(1)}, u32[]{:S(2)}, u32[]{:S(2)}) collective-permute-start(bf16[256,256]{1,0:T(8,128)(2,1)S(1)} %collective-permute-done.16.refs_9_), channel_id=1, source_target_pairs={{0,2},{1,3},{2,0},{3,1},{4,6},{5,7},{6,4},{7,5},{8,10},{9,11},{10,... | collective-permute-start | bytes 393224 | tf_op jit(solution)/shard_map/ppermute | solution.py:457
  70.3 8.0 %collective-permute-start.31 = (bf16[256,256]{1,0:T(8,128)(2,1)S(1)}, bf16[256,256]{1,0:T(8,128)(2,1)S(1)}, u32[]{:S(2)}, u32[]{:S(2)}) collective-permute-start(bf16[256,256]{1,0:T(8,128)(2,1)S(1)} %collective-permute-done.27.refs_10_), channel_id=1, source_target_pairs={{0,8},{4,12},{8,0},{12,4},{16,24},{20,28},{24,16},{28,20},{1,9},{5... | collective-permute-start | bytes 393224 | tf_op jit(solution)/shard_map/ppermute | solution.py:457
  71.8 7.0 %collective-permute-start.30 = (bf16[256,256]{1,0:T(8,128)(2,1)S(1)}, bf16[256,256]{1,0:T(8,128)(2,1)S(1)}, u32[]{:S(2)}, u32[]{:S(2)}) collective-permute-start(bf16[256,256]{1,0:T(8,128)(2,1)S(1)} %collective-permute-done.26.refs_9_), channel_id=1, source_target_pairs={{0,8},{4,12},{8,0},{12,4},{16,24},{20,28},{24,16},{28,20},{1,9},{5... | collective-permute-start | bytes 393224 | tf_op jit(solution)/shard_map/ppermute | solution.py:457
  72.5 6.5 %collective-permute-start.32 = (bf16[256,256]{1,0:T(8,128)(2,1)S(1)}, bf16[256,256]{1,0:T(8,128)(2,1)S(1)}, u32[]{:S(2)}, u32[]{:S(2)}) collective-permute-start(bf16[256,256]{1,0:T(8,128)(2,1)S(1)} %collective-permute-done.28.refs_11_), channel_id=1, source_target_pairs={{0,8},{4,12},{8,0},{12,4},{16,24},{20,28},{24,16},{28,20},{1,9},{5... | collective-permute-start | bytes 393224 | tf_op jit(solution)/shard_map/ppermute | solution.py:457
  73.9 9.4 %collective-permute-start.7 = (bf16[256,256]{1,0:T(8,128)(2,1)S(1)}, bf16[256,256]{1,0:T(8,128)(2,1)S(1)}, u32[]{:S(2)}, u32[]{:S(2)}) collective-permute-start(bf16[256,256]{1,0:T(8,128)(2,1)S(1)} %get-tuple-element.63.refs_0_.refs_8_), channel_id=1, source_target_pairs={{0,1},{1,0},{2,3},{3,2},{4,5},{5,4},{6,7},{7,6},{8,9},{9,8},{10,11... | collective-permute-start | bytes 393224 | tf_op jit(solution)/shard_map/ppermute | solution.py:457
  74.7 8.9 %collective-permute-start.8 = (bf16[256,256]{1,0:T(8,128)(2,1)S(1)}, bf16[256,256]{1,0:T(8,128)(2,1)S(1)}, u32[]{:S(2)}, u32[]{:S(2)}) collective-permute-start(bf16[256,256]{1,0:T(8,128)(2,1)S(1)} %get-tuple-element.57.refs_1_), channel_id=1, source_target_pairs={{0,1},{1,0},{2,3},{3,2},{4,5},{5,4},{6,7},{7,6},{8,9},{9,8},{10,11... | collective-permute-start | bytes 393224 | tf_op jit(solution)/shard_map/ppermute | solution.py:457
  78.3 7.6 %collective-permute-start.11 = (bf16[256,256]{1,0:T(8,128)(2,1)S(1)}, bf16[256,256]{1,0:T(8,128)(2,1)S(1)}, u32[]{:S(2)}, u32[]{:S(2)}) collective-permute-start(bf16[256,256]{1,0:T(8,128)(2,1)S(1)} %collective-permute-done.9.refs_4_.refs_8_), channel_id=1, source_target_pairs={{0,1},{1,0},{2,3},{3,2},{4,5},{5,4},{6,7},{7,6},{8,9},{9,8},{10,11... | collective-permute-start | bytes 393224 | tf_op jit(solution)/shard_map/ppermute | solution.py:457
  78.9 7.2 %collective-permute-start.12 = (bf16[256,256]{1,0:T(8,128)(2,1)S(1)}, bf16[256,256]{1,0:T(8,128)(2,1)S(1)}, u32[]{:S(2)}, u32[]{:S(2)}) collective-permute-start(bf16[256,256]{1,0:T(8,128)(2,1)S(1)} %collective-permute-done.10.refs_5_), channel_id=1, source_target_pairs={{0,1},{1,0},{2,3},{3,2},{4,5},{5,4},{6,7},{7,6},{8,9},{9,8},{10,11... | collective-permute-start | bytes 393224 | tf_op jit(solution)/shard_map/ppermute | solution.py:457
  79.0 9.7 %collective-permute-start.23 = (bf16[256,256]{1,0:T(8,128)(2,1)S(1)}, bf16[256,256]{1,0:T(8,128)(2,1)S(1)}, u32[]{:S(2)}, u32[]{:S(2)}) collective-permute-start(bf16[256,256]{1,0:T(8,128)(2,1)S(1)} %get-tuple-element.65), channel_id=1, source_target_pairs={{0,16},{4,20},{8,24},{12,28},{16,0},{20,4},{24,8},{28,12},{1,17},{... | collective-permute-start | bytes 393224 | tf_op jit(solution)/shard_map/ppermute | solution.py:457
  83.3 14.6 %collective-permute-start.24 = (f32[256,256]{1,0:T(8,128)S(1)}, f32[256,256]{1,0:T(8,128)S(1)}, u32[]{:S(2)}, u32[]{:S(2)}) collective-permute-start(f32[256,256]{1,0:T(8,128)S(1)} %get-tuple-element.66), channel_id=1, source_target_pairs={{0,1},{1,0},{2,3},{3,2},{4,5},{5,4},{6,7},{7,6},{8,9},{9,8},{10,11... | collective-permute-start | bytes 786440 | tf_op jit(solution)/shard_map/ppermute | solution.py:457
  83.5 22.8 %collective-permute-start.34 = (f32[256,256]{1,0:T(8,128)S(1)}, f32[256,256]{1,0:T(8,128)S(1)}, u32[]{:S(2)}, u32[]{:S(2)}) collective-permute-start(f32[256,256]{1,0:T(8,128)S(1)} %get-tuple-element.70), channel_id=1, source_target_pairs={{0,1},{1,0},{2,3},{3,2},{4,5},{5,4},{6,7},{7,6},{8,9},{9,8},{10,11... | collective-permute-start | bytes 786440 | tf_op jit(solution)/shard_map/ppermute | solution.py:457
  85.9 12.0 %collective-permute-start.25 = (bf16[256,256]{1,0:T(8,128)(2,1)S(1)}, bf16[256,256]{1,0:T(8,128)(2,1)S(1)}, u32[]{:S(2)}, u32[]{:S(2)}) collective-permute-start(bf16[256,256]{1,0:T(8,128)(2,1)S(1)} %get-tuple-element.67), channel_id=1, source_target_pairs={{0,17},{1,16},{2,19},{3,18},{4,21},{5,20},{6,23},{7,22},{8,25},{9,... | collective-permute-start | bytes 393224 | tf_op jit(solution)/shard_map/ppermute | solution.py:457
  86.1 18.1 %collective-permute-start.33 = (bf16[256,256]{1,0:T(8,128)(2,1)S(1)}, bf16[256,256]{1,0:T(8,128)(2,1)S(1)}, u32[]{:S(2)}, u32[]{:S(2)}) collective-permute-start(bf16[256,256]{1,0:T(8,128)(2,1)S(1)} %get-tuple-element.69), channel_id=1, source_target_pairs={{0,16},{4,20},{8,24},{12,28},{16,0},{20,4},{24,8},{28,12},{1,17},{... | collective-permute-start | bytes 393224 | tf_op jit(solution)/shard_map/ppermute | solution.py:457
  88.6 17.7 %collective-permute-start.35 = (bf16[256,256]{1,0:T(8,128)(2,1)S(1)}, bf16[256,256]{1,0:T(8,128)(2,1)S(1)}, u32[]{:S(2)}, u32[]{:S(2)}) collective-permute-start(bf16[256,256]{1,0:T(8,128)(2,1)S(1)} %get-tuple-element.71), channel_id=1, source_target_pairs={{0,17},{1,16},{2,19},{3,18},{4,21},{5,20},{6,23},{7,22},{8,25},{9,... | collective-permute-start | bytes 393224 | tf_op jit(solution)/shard_map/ppermute | solution.py:457
  (15 other events, 60.6 us)

commit v5 on v4

--- a/solution.py
+++ b/solution.py
@@ -491,11 +491,27 @@
     xs = xs + xs_core + [swap(b, "mp", 1) for b in xs[1:]]
     near = {(0, 0, 0): grads, (0, 0, 1): there}
     hops = [
-        ((0, 0), "dp", 1), ((0, 0), "dp", 2), ((0, 0), "mp", 2), ((2, 0), "dp", 1),
-        ((1, 0), "mp", 2), ((0, 1), "dp", 2), ((1, 1), "dp", 2),
+        [
+            (0, 0, "dp", 1),
+            (0, 0, "dp", 2),
+            (0, 0, "mp", 2),
+            (2, 0, "dp", 1),
+            (1, 0, "mp", 2),
+            (0, 1, "dp", 2),
+            (2, 1, "dp", 1),
+        ],
+        [
+            (0, 0, "dp", 1),
+            (0, 0, "dp", 2),
+            (0, 0, "mp", 2),
+            (2, 0, "dp", 1),
+            (1, 0, "mp", 2),
+            (0, 1, "dp", 2),
+            (1, 1, "dp", 2),
+        ],
     ]
-    for part in range(2):
-        for (code, far), axis, step in hops:
+    for part, plan in enumerate((hops[0], hops[1])):
+        for code, far, axis, step in plan:
             key = (code ^ step, far, part) if axis == "dp" else (code, 1 - far, part)
             near[key] = swap(near[code, far, part], axis, step)
     across = swap(beyond, "mp", 2)

time: 108 us -> 108 us (level)
  transfers between devices with their start and end apart: 37 -> 37, of which waited for: 11 -> 13; matrix products, arithmetic and copies ran while one was open for 0% -> 0% of each run, Pallas kernels for 25% -> 25%
where the time goes in v5:
time: 108 us; the launch traced here: 107 us
  starting transfers between devices  36.2 us (34%)
  waiting for transfers between devices  33 us (31%)
  Pallas kernels  32.5 us (30%)
  local copies, waits for them, and re-layouts  3.52 us (3%)
  other arithmetic  1.11 us (1%)
    ppermute x36, starting transfers between devices, swap(): return lax.ppermute(x, axis, [(i, i ^ code) for i in range(size)])  31.3 us
    ppermute x36, waiting for transfers between devices, swap(): return lax.ppermute(x, axis, [(i, i ^ code) for i in range(size)])  28.7 us
    pallas_call x2, Pallas kernels, project(): pl.pallas_call(project_kernel, out_shape=(jax.ShapeDtypeStruct(out, F32),...  8.37 us
    pallas_call x4, Pallas kernels, weight_grads(): pl.pallas_call(kernel, out_shape=(jax.ShapeDtypeStruct(out, dtype),) * 2,...  7.32 us
    pallas_call x2, Pallas kernels, attention(): pl.pallas_call(functools.partial(attention_kernel, lmax, learners, half),...  5.78 us
    all_to_all x1, starting transfers between devices, local(): kv = lax.all_to_all(kv[0], 'dp', split_axis=0, concat_axis=0, tiled=True)  4.88 us
    pallas_call x1, Pallas kernels, row_grads(): pl.pallas_call(rows_kernel, out_shape=jax.ShapeDtypeStruct((rows, feats),...  4.78 us
    all_to_all x1, waiting for transfers between devices, local(): kv = lax.all_to_all(kv[0], 'dp', split_axis=0, concat_axis=0, tiled=True)  4.27 us
  transfers between devices with their start and end apart: 37, of which 13 were waited for; matrix products, arithmetic and copies ran while one was open for 0% of the time, Pallas kernels for 25%

profile of v5, /device:TPU:0, one launch (start us, length us, event | category | flops | bytes accessed | tf_op | source)
XLA Modules:
  0.0 107.1 jit_solution(14986481581736973848)
XLA Ops:
  0.7 4.3 %project.2 = (f32[512,256]{1,0:T(8,128)}, f32[512,256]{1,0:T(8,128)}) custom-call(s32[1]{0:T(128)} %bitcast.1.me_ref, bf16[512,2048]{1,0:T(8,128)(2,1)} %bitcast.6, bf16[2048,512]{1,0:T(8,128)(2,1)} %refs_8_.1, bf16[2048,512]{1,0:T(8,128)(2,1)} %refs_9_.1), custom_call_target="tpu_custom_call" | custom-call | tf_op jit(solution)/shard_map/project/pallas_call | solution.py:167
  5.4 2.4 %slots.1 = (bf16[2,512,256]{2,1,0:T(8,128)(2,1)S(1)}, bf16[2,512,256]{2,1,0:T(8,128)(2,1)S(1)}, bf16[2,512,256]{2,1,0:T(8,128)(2,1)S(1)}, bf16[2,512,256]{2,1,0:...) custom-call(s32[1]{0:T(128)} %bitcast.me_ref, s32[1,32]{1,0:T(1,128)S(1)} %bitcast.9, ...), custom_call_target="tpu_custom_call" | custom-call | tf_op jit(solution)/shard_map/slots/pallas_call | solution.py:222
  9.0 3.0 %collective-permute-start.5 = (bf16[2,512,256]{2,1,0:T(8,128)(2,1)S(1)}, bf16[2,512,256]{2,1,0:T(8,128)(2,1)S(1)}, u32[]{:S(2)}, u32[]{:S(2)}) collective-permute-start(bf16[2,512,256]{2,1,0:T(8,128)(2,1)S(1)} %get-tuple-element.54), channel_id=1, source_target_pairs={{0,8},{4,12},{8,0},{12,4},{16,24},{20,28},{24,16},{28,20},{1,9},{5... | collective-permute-start | bytes 1572872 | tf_op jit(solution)/shard_map/ppermute | solution.py:457
  12.0 1.5 %collective-permute-start.4 = (bf16[2,512,256]{2,1,0:T(8,128)(2,1)S(1)}, bf16[2,512,256]{2,1,0:T(8,128)(2,1)S(1)}, u32[]{:S(2)}, u32[]{:S(2)}) collective-permute-start(bf16[2,512,256]{2,1,0:T(8,128)(2,1)S(1)} %get-tuple-element.52), channel_id=1, source_target_pairs={{0,4},{4,0},{8,12},{12,8},{16,20},{20,16},{24,28},{28,24},{1,5},{5... | collective-permute-start | bytes 1572872 | tf_op jit(solution)/shard_map/ppermute | solution.py:457
  13.6 1.5 %collective-permute-start.3 = (f32[512,256]{1,0:T(8,128)S(1)}, f32[512,256]{1,0:T(8,128)S(1)}, u32[]{:S(2)}, u32[]{:S(2)}) collective-permute-start(f32[512,256]{1,0:T(8,128)S(1)} %add.3), channel_id=1, source_target_pairs={{0,2},{1,3},{2,0},{3,1},{4,6},{5,7},{6,4},{7,5},{8,10},{9,11},{10,... | collective-permute-start | bytes 1572872 | tf_op jit(solution)/shard_map/ppermute | solution.py:457
  15.1 4.1 %project.3 = (f32[512,256]{1,0:T(8,128)}, f32[512,256]{1,0:T(8,128)}) custom-call(s32[1]{0:T(128)} %bitcast.1.me_ref, bf16[512,2048]{1,0:T(8,128)(2,1)} %bitcast.7, bf16[2048,512]{1,0:T(8,128)(2,1)} %refs_8_.1, bf16[2048,512]{1,0:T(8,128)(2,1)} %refs_9_.1), custom_call_target="tpu_custom_call" | custom-call | tf_op jit(solution)/shard_map/project/pallas_call | solution.py:167
  19.2 5.0 %collective-permute-done.5.refs_2_ = bf16[2,512,256]{2,1,0:T(8,128)(2,1)S(1)} collective-permute-done((bf16[2,512,256]{2,1,0:T(8,128)(2,1)S(1)}, bf16[2,512,256]{2,1,0:T(8,128)(2,1)S(1)}, u32[]{:S(2)}, u32[]{:S(2)}) %collective-permute-start.5) | collective-permute-done | bytes 524320 | tf_op jit(solution)/shard_map/ppermute | solution.py:457
  24.2 1.5 %collective-permute-done.4.refs_1_ = bf16[2,512,256]{2,1,0:T(8,128)(2,1)S(1)} collective-permute-done((bf16[2,512,256]{2,1,0:T(8,128)(2,1)S(1)}, bf16[2,512,256]{2,1,0:T(8,128)(2,1)S(1)}, u32[]{:S(2)}, u32[]{:S(2)}) %collective-permute-start.4) | collective-permute-done | bytes 524320 | tf_op jit(solution)/shard_map/ppermute | solution.py:457
  25.7 1.4 %collective-permute-start.6 = (bf16[2,512,256]{2,1,0:T(8,128)(2,1)}, bf16[2,512,256]{2,1,0:T(8,128)(2,1)S(1)}, u32[]{:S(2)}, u32[]{:S(2)}) collective-permute-start(bf16[2,512,256]{2,1,0:T(8,128)(2,1)} %get-tuple-element.55), channel_id=1, source_target_pairs={{0,12},{4,8},{8,4},{12,0},{16,28},{20,24},{24,20},{28,16},{1,13},{... | collective-permute-start | bytes 1572872 | tf_op jit(solution)/shard_map/ppermute | solution.py:457
  29.2 4.9 %all-to-all-start = ((bf16[8,80,256]{2,1,0:T(8,128)(2,1)}), bf16[8,80,256]{2,1,0:T(8,128)(2,1)S(1)}, u32[]{:S(2)}, u32[]{:S(2)}) async-start(bf16[8,80,256]{2,1,0:T(8,128)(2,1)} %pack.1), calls=%async_computation | async-start | bytes 655360 | tf_op jit(solution)/shard_map/all_to_all | solution.py:483
  34.6 8.0 %collective-permute-done.6.refs_3_ = bf16[2,512,256]{2,1,0:T(8,128)(2,1)S(1)} collective-permute-done((bf16[2,512,256]{2,1,0:T(8,128)(2,1)}, bf16[2,512,256]{2,1,0:T(8,128)(2,1)S(1)}, u32[]{:S(2)}, u32[]{:S(2)}) %collective-permute-start.6) | collective-permute-done | bytes 524320 | tf_op jit(solution)/shard_map/ppermute | solution.py:457
  42.6 4.3 %all-to-all-done.kv_ref = bf16[8,80,256]{2,1,0:T(8,128)(2,1)S(1)} async-done(((bf16[8,80,256]{2,1,0:T(8,128)(2,1)}), bf16[8,80,256]{2,1,0:T(8,128)(2,1)S(1)}, u32[]{:S(2)}, u32[]{:S(2)}) %all-to-all-start) | async-done | bytes 327712 | tf_op jit(solution)/shard_map/all_to_all | solution.py:483
  46.9 1.2 %copy-done.3 = bf16[512,1024]{1,0:T(8,128)(2,1)S(1)} copy-done((bf16[512,1024]{1,0:T(8,128)(2,1)S(1)}, bf16[512,1024]{1,0:T(8,128)(2,1)}, u32[]{:S(2)}) %copy-start.3) | copy-done | bytes 1048600
  48.1 1.2 %copy-done.4 = bf16[512,1024]{1,0:T(8,128)(2,1)S(1)} copy-done((bf16[512,1024]{1,0:T(8,128)(2,1)S(1)}, bf16[512,1024]{1,0:T(8,128)(2,1)}, u32[]{:S(2)}) %copy-start.4) | copy-done | bytes 1048600
  49.4 2.9 %attention.2 = (bf16[256,256]{1,0:T(8,128)(2,1)S(1)}, bf16[256,1024]{1,0:T(8,128)(2,1)S(1)}, bf16[256,512]{1,0:T(8,128)(2,1)S(1)}) custom-call(s32[1]{0:T(128)} %bitcast.me_ref, bf16[8,80,256]{2,1,0:T(8,128)(2,1)S(1)} %all-to-all-done.kv_ref, bf16[512,1024]{1,0:T(8,128)(2,1)S(1)} %copy-done.3, bf16[512,1024]{1,0:T(8,128)(2,1)S(1)} %copy-done.4), custom_call_target="tpu_custom_call" | custom-call | tf_op jit(solution)/shard_map/attention/pallas_call | solution.py:320
  52.4 2.9 %attention.3 = (bf16[256,256]{1,0:T(8,128)(2,1)S(1)}, bf16[256,1024]{1,0:T(8,128)(2,1)S(1)}, bf16[256,512]{1,0:T(8,128)(2,1)S(1)}) custom-call(s32[1]{0:T(128)} %bitcast.me_ref, bf16[8,80,256]{2,1,0:T(8,128)(2,1)S(1)} %all-to-all-done.kv_ref, bf16[512,1024]{1,0:T(8,128)(2,1)S(1)} %copy-done.3, bf16[512,1024]{1,0:T(8,128)(2,1)S(1)} %copy-done.4), custom_call_target="tpu_custom_call" | custom-call | tf_op jit(solution)/shard_map/attention/pallas_call | solution.py:320
  55.3 1.6 %collective-permute-start.9 = (bf16[256,256]{1,0:T(8,128)(2,1)S(1)}, bf16[256,256]{1,0:T(8,128)(2,1)S(1)}, u32[]{:S(2)}, u32[]{:S(2)}) collective-permute-start(bf16[256,256]{1,0:T(8,128)(2,1)S(1)} %get-tuple-element.63.refs_0_.refs_8_), channel_id=1, source_target_pairs={{0,2},{1,3},{2,0},{3,1},{4,6},{5,7},{6,4},{7,5},{8,10},{9,11},{10,... | collective-permute-start | bytes 393224 | tf_op jit(solution)/shard_map/ppermute | solution.py:457
  57.8 1.5 %collective-permute-start.19 = (bf16[256,256]{1,0:T(8,128)(2,1)S(1)}, bf16[256,256]{1,0:T(8,128)(2,1)S(1)}, u32[]{:S(2)}, u32[]{:S(2)}) collective-permute-start(bf16[256,256]{1,0:T(8,128)(2,1)S(1)} %get-tuple-element.63.refs_0_.refs_8_), channel_id=1, source_target_pairs={{0,8},{4,12},{8,0},{12,4},{16,24},{20,28},{24,16},{28,20},{1,9},{5... | collective-permute-start | bytes 393224 | tf_op jit(solution)/shard_map/ppermute | solution.py:457
  60.8 1.9 %collective-permute-start.29 = (bf16[256,256]{1,0:T(8,128)(2,1)S(1)}, bf16[256,256]{1,0:T(8,128)(2,1)S(1)}, u32[]{:S(2)}, u32[]{:S(2)}) collective-permute-start(bf16[256,256]{1,0:T(8,128)(2,1)S(1)} %collective-permute-done.9.refs_4_.refs_8_), channel_id=1, source_target_pairs={{0,8},{4,12},{8,0},{12,4},{16,24},{20,28},{24,16},{28,20},{1,9},{5... | collective-permute-start | bytes 393224 | tf_op jit(solution)/shard_map/ppermute | solution.py:457
  67.0 1.2 %collective-permute-start.21 = (bf16[256,256]{1,0:T(8,128)(2,1)S(1)}, bf16[256,256]{1,0:T(8,128)(2,1)S(1)}, u32[]{:S(2)}, u32[]{:S(2)}) collective-permute-start(bf16[256,256]{1,0:T(8,128)(2,1)S(1)} %collective-permute-done.19.refs_12_), channel_id=1, source_target_pairs={{0,4},{4,0},{8,12},{12,8},{16,20},{20,16},{24,28},{28,24},{1,5},{5... | collective-permute-start | bytes 393224 | tf_op jit(solution)/shard_map/ppermute | solution.py:457
  68.2 1.3 %collective-permute-start.22 = (bf16[256,256]{1,0:T(8,128)(2,1)S(1)}, bf16[256,256]{1,0:T(8,128)(2,1)S(1)}, u32[]{:S(2)}, u32[]{:S(2)}) collective-permute-start(bf16[256,256]{1,0:T(8,128)(2,1)S(1)} %collective-permute-done.20.refs_13_), channel_id=1, source_target_pairs={{0,4},{4,0},{8,12},{12,8},{16,20},{20,16},{24,28},{28,24},{1,5},{5... | collective-permute-start | bytes 393224 | tf_op jit(solution)/shard_map/ppermute | solution.py:457
  74.3 1.8 %weight_grads.5 = (bf16[256,256]{1,0:T(8,128)(2,1)S(1)}, bf16[256,256]{1,0:T(8,128)(2,1)S(1)}) custom-call(bf16[2,512,256]{2,1,0:T(8,128)(2,1)S(1)} %get-tuple-element.45.refs_0_, bf16[2,512,256]{2,1,0:T(8,128)(2,1)S(1)} %collective-permute-done.4.refs_1_, bf16[2,512,256]{2,1,0:T(8,128)(2,1)S(1)} %collective-permute-done.5.refs_2_, ...), custom_call_target="tpu_custom_call" | custom-call | tf_op jit(solution)/shard_map/weight_grads/pallas_call | solution.py:414
  76.1 1.8 %weight_grads.4 = (f32[256,256]{1,0:T(8,128)S(1)}, f32[256,256]{1,0:T(8,128)S(1)}) custom-call(bf16[2,512,256]{2,1,0:T(8,128)(2,1)S(1)} %get-tuple-element.45.refs_0_, bf16[2,512,256]{2,1,0:T(8,128)(2,1)S(1)} %collective-permute-done.4.refs_1_, bf16[2,512,256]{2,1,0:T(8,128)(2,1)S(1)} %collective-permute-done.5.refs_2_, ...), custom_call_target="tpu_custom_call" | custom-call | tf_op jit(solution)/shard_map/weight_grads/pallas_call | solution.py:414
  78.6 2.6 %collective-permute-start.23 = (bf16[256,256]{1,0:T(8,128)(2,1)S(1)}, bf16[256,256]{1,0:T(8,128)(2,1)S(1)}, u32[]{:S(2)}, u32[]{:S(2)}) collective-permute-start(bf16[256,256]{1,0:T(8,128)(2,1)S(1)} %get-tuple-element.65), channel_id=1, source_target_pairs={{0,16},{4,20},{8,24},{12,28},{16,0},{20,4},{24,8},{28,12},{1,17},{... | collective-permute-start | bytes 393224 | tf_op jit(solution)/shard_map/ppermute | solution.py:457
  81.2 1.8 %weight_grads.6 = (f32[256,256]{1,0:T(8,128)S(1)}, f32[256,256]{1,0:T(8,128)S(1)}) custom-call(bf16[2,512,256]{2,1,0:T(8,128)(2,1)S(1)} %get-tuple-element.45.refs_0_, bf16[2,512,256]{2,1,0:T(8,128)(2,1)S(1)} %collective-permute-done.4.refs_1_, bf16[2,512,256]{2,1,0:T(8,128)(2,1)S(1)} %collective-permute-done.5.refs_2_, ...), custom_call_target="tpu_custom_call" | custom-call | tf_op jit(solution)/shard_map/weight_grads/pallas_call | solution.py:414
  83.6 1.9 %weight_grads.7 = (bf16[256,256]{1,0:T(8,128)(2,1)S(1)}, bf16[256,256]{1,0:T(8,128)(2,1)S(1)}) custom-call(bf16[2,512,256]{2,1,0:T(8,128)(2,1)S(1)} %get-tuple-element.45.refs_0_, bf16[2,512,256]{2,1,0:T(8,128)(2,1)S(1)} %collective-permute-done.4.refs_1_, bf16[2,512,256]{2,1,0:T(8,128)(2,1)S(1)} %collective-permute-done.5.refs_2_, ...), custom_call_target="tpu_custom_call" | custom-call | tf_op jit(solution)/shard_map/weight_grads/pallas_call | solution.py:414
  85.7 2.6 %collective-permute-start.33 = (bf16[256,256]{1,0:T(8,128)(2,1)S(1)}, bf16[256,256]{1,0:T(8,128)(2,1)S(1)}, u32[]{:S(2)}, u32[]{:S(2)}) collective-permute-start(bf16[256,256]{1,0:T(8,128)(2,1)S(1)} %get-tuple-element.69), channel_id=1, source_target_pairs={{0,16},{4,20},{8,24},{12,28},{16,0},{20,4},{24,8},{28,12},{1,17},{... | collective-permute-start | bytes 393224 | tf_op jit(solution)/shard_map/ppermute | solution.py:457
  88.4 1.7 %packed_rows.1 = bf16[512,1024]{1,0:T(8,128)(2,1)} custom-call(bf16[256,512]{1,0:T(8,128)(2,1)S(1)} %get-tuple-element.59.place0, bf16[256,512]{1,0:T(8,128)(2,1)S(1)} %get-tuple-element.60.place1, bf16[256,1024]{1,0:T(8,128)(2,1)S(1)} %get-tuple-element.61.out0, bf16[256,1024]{1,0:T(8,128)(2,1)S(1)} %get-tuple-element.62.out1), custom_call_target="tpu_custom_call" | custom-call | tf_op jit(solution)/shard_map/packed_rows/pallas_call | solution.py:338
  90.1 4.8 %row_grads.1 = bf16[512,2048]{1,0:T(8,128)(2,1)} custom-call(s32[1]{0:T(128)} %bitcast.1.me_ref, bf16[256,512]{1,0:T(8,128)(2,1)S(1)} %get-tuple-element.59.place0, bf16[256,512]{1,0:T(8,128)(2,1)S(1)} %get-tuple-element.60.place1, bf16[256,256]{1,0:T(8,128)(2,1)S(1)} %get-tuple-element.63.refs_0_.refs_8_, bf16[256,256]{1,0:T(8,128)(2,1)S(1)} %get-tuple-element.57.refs_1_, ...), custom_call_target="tpu_custom_call" | custom-call | tf_op jit(solution)/shard_map/row_grads/pallas_call | solution.py:381
  94.8 2.7 %collective-permute-done.25.refs_3_ = bf16[256,256]{1,0:T(8,128)(2,1)S(1)} collective-permute-done((bf16[256,256]{1,0:T(8,128)(2,1)S(1)}, bf16[256,256]{1,0:T(8,128)(2,1)S(1)}, u32[]{:S(2)}, u32[]{:S(2)}) %collective-permute-start.25) | collective-permute-done | bytes 131104 | tf_op jit(solution)/shard_map/ppermute | solution.py:457
  97.6 3.5 %collective-permute-done.33.refs_5_ = bf16[256,256]{1,0:T(8,128)(2,1)S(1)} collective-permute-done((bf16[256,256]{1,0:T(8,128)(2,1)S(1)}, bf16[256,256]{1,0:T(8,128)(2,1)S(1)}, u32[]{:S(2)}, u32[]{:S(2)}) %collective-permute-start.33) | collective-permute-done | bytes 131104 | tf_op jit(solution)/shard_map/ppermute | solution.py:457
  101.1 4.9 %collective-permute-done.35.refs_7_ = bf16[256,256]{1,0:T(8,128)(2,1)S(1)} collective-permute-done((bf16[256,256]{1,0:T(8,128)(2,1)S(1)}, bf16[256,256]{1,0:T(8,128)(2,1)S(1)}, u32[]{:S(2)}, u32[]{:S(2)}) %collective-permute-start.35) | collective-permute-done | bytes 131104 | tf_op jit(solution)/shard_map/ppermute | solution.py:457
  (76 shorter events, 18.7 us)
Async XLA Ops:
  8.9 6.2 %collective-permute-start.1 = (bf16[2,512,256]{2,1,0:T(8,128)(2,1)S(1)}, bf16[2,512,256]{2,1,0:T(8,128)(2,1)S(1)}, u32[]{:S(2)}, u32[]{:S(2)}) collective-permute-start(bf16[2,512,256]{2,1,0:T(8,128)(2,1)S(1)} %get-tuple-element.45.refs_0_), channel_id=1, source_target_pairs={{0,1},{1,0},{2,3},{3,2},{4,5},{5,4},{6,7},{7,6},{8,9},{9,8},{10,11... | collective-permute-start | bytes 1572872 | tf_op jit(solution)/shard_map/ppermute | solution.py:457
  9.0 15.2 %collective-permute-start.5 = (bf16[2,512,256]{2,1,0:T(8,128)(2,1)S(1)}, bf16[2,512,256]{2,1,0:T(8,128)(2,1)S(1)}, u32[]{:S(2)}, u32[]{:S(2)}) collective-permute-start(bf16[2,512,256]{2,1,0:T(8,128)(2,1)S(1)} %get-tuple-element.54), channel_id=1, source_target_pairs={{0,8},{4,12},{8,0},{12,4},{16,24},{20,28},{24,16},{28,20},{1,9},{5... | collective-permute-start | bytes 1572872 | tf_op jit(solution)/shard_map/ppermute | solution.py:457
  12.0 13.6 %collective-permute-start.4 = (bf16[2,512,256]{2,1,0:T(8,128)(2,1)S(1)}, bf16[2,512,256]{2,1,0:T(8,128)(2,1)S(1)}, u32[]{:S(2)}, u32[]{:S(2)}) collective-permute-start(bf16[2,512,256]{2,1,0:T(8,128)(2,1)S(1)} %get-tuple-element.52), channel_id=1, source_target_pairs={{0,4},{4,0},{8,12},{12,8},{16,20},{20,16},{24,28},{28,24},{1,5},{5... | collective-permute-start | bytes 1572872 | tf_op jit(solution)/shard_map/ppermute | solution.py:457
  13.6 13.5 %collective-permute-start.3 = (f32[512,256]{1,0:T(8,128)S(1)}, f32[512,256]{1,0:T(8,128)S(1)}, u32[]{:S(2)}, u32[]{:S(2)}) collective-permute-start(f32[512,256]{1,0:T(8,128)S(1)} %add.3), channel_id=1, source_target_pairs={{0,2},{1,3},{2,0},{3,1},{4,6},{5,7},{6,4},{7,5},{8,10},{9,11},{10,... | collective-permute-start | bytes 1572872 | tf_op jit(solution)/shard_map/ppermute | solution.py:457
  19.2 7.9 %collective-permute-start.2 = (f32[512,256]{1,0:T(8,128)}, f32[512,256]{1,0:T(8,128)S(1)}, u32[]{:S(2)}, u32[]{:S(2)}) collective-permute-start(f32[512,256]{1,0:T(8,128)} %get-tuple-element.48), channel_id=1, source_target_pairs={{0,1},{1,0},{2,3},{3,2},{4,5},{5,4},{6,7},{7,6},{8,9},{9,8},{10,11... | collective-permute-start | bytes 1572872 | tf_op jit(solution)/shard_map/ppermute | solution.py:457
  25.7 17.0 %collective-permute-start.6 = (bf16[2,512,256]{2,1,0:T(8,128)(2,1)}, bf16[2,512,256]{2,1,0:T(8,128)(2,1)S(1)}, u32[]{:S(2)}, u32[]{:S(2)}) collective-permute-start(bf16[2,512,256]{2,1,0:T(8,128)(2,1)} %get-tuple-element.55), channel_id=1, source_target_pairs={{0,12},{4,8},{8,4},{12,0},{16,28},{20,24},{24,20},{28,16},{1,13},{... | collective-permute-start | bytes 1572872 | tf_op jit(solution)/shard_map/ppermute | solution.py:457
  29.2 17.7 %all-to-all-start = ((bf16[8,80,256]{2,1,0:T(8,128)(2,1)}), bf16[8,80,256]{2,1,0:T(8,128)(2,1)S(1)}, u32[]{:S(2)}, u32[]{:S(2)}) async-start(bf16[8,80,256]{2,1,0:T(8,128)(2,1)} %pack.1), calls=%async_computation | async-start | bytes 655360 | tf_op jit(solution)/shard_map/all_to_all | solution.py:483
  34.1 22.8 %collective-permute-start.14 = (bf16[2,512,256]{2,1,0:T(8,128)(2,1)S(1)}, bf16[2,512,256]{2,1,0:T(8,128)(2,1)S(1)}, u32[]{:S(2)}, u32[]{:S(2)}) collective-permute-start(bf16[2,512,256]{2,1,0:T(8,128)(2,1)S(1)} %collective-permute-done.5.refs_2_), channel_id=1, source_target_pairs={{0,1},{1,0},{2,3},{3,2},{4,5},{5,4},{6,7},{7,6},{8,9},{9,8},{10,11... | collective-permute-start | bytes 1572872 | tf_op jit(solution)/shard_map/ppermute | solution.py:457
  34.1 23.7 %collective-permute-start.13 = (bf16[2,512,256]{2,1,0:T(8,128)(2,1)S(1)}, bf16[2,512,256]{2,1,0:T(8,128)(2,1)}, u32[]{:S(2)}, u32[]{:S(2)}) collective-permute-start(bf16[2,512,256]{2,1,0:T(8,128)(2,1)S(1)} %collective-permute-done.4.refs_1_), channel_id=1, source_target_pairs={{0,1},{1,0},{2,3},{3,2},{4,5},{5,4},{6,7},{7,6},{8,9},{9,8},{10,11... | collective-permute-start | bytes 1572872 | tf_op jit(solution)/shard_map/ppermute | solution.py:457
  42.6 16.6 %collective-permute-start.15 = (bf16[2,512,256]{2,1,0:T(8,128)(2,1)S(1)}, bf16[2,512,256]{2,1,0:T(8,128)(2,1)}, u32[]{:S(2)}, u32[]{:S(2)}) collective-permute-start(bf16[2,512,256]{2,1,0:T(8,128)(2,1)S(1)} %collective-permute-done.6.refs_3_), channel_id=1, source_target_pairs={{0,1},{1,0},{2,3},{3,2},{4,5},{5,4},{6,7},{7,6},{8,9},{9,8},{10,11... | collective-permute-start | bytes 1572872 | tf_op jit(solution)/shard_map/ppermute | solution.py:457
  52.2 7.5 %collective-permute-start.16 = (bf16[256,256]{1,0:T(8,128)(2,1)S(1)}, bf16[256,256]{1,0:T(8,128)(2,1)S(1)}, u32[]{:S(2)}, u32[]{:S(2)}) collective-permute-start(bf16[256,256]{1,0:T(8,128)(2,1)S(1)} %get-tuple-element.57.refs_1_), channel_id=1, source_target_pairs={{0,16},{4,20},{8,24},{12,28},{16,0},{20,4},{24,8},{28,12},{1,17},{... | collective-permute-start | bytes 393224 | tf_op jit(solution)/shard_map/ppermute | solution.py:457
  56.9 6.1 %collective-permute-start.17 = (bf16[256,256]{1,0:T(8,128)(2,1)S(1)}, bf16[256,256]{1,0:T(8,128)(2,1)S(1)}, u32[]{:S(2)}, u32[]{:S(2)}) collective-permute-start(bf16[256,256]{1,0:T(8,128)(2,1)S(1)} %get-tuple-element.63.refs_0_.refs_8_), channel_id=1, source_target_pairs={{0,4},{4,0},{8,12},{12,8},{16,20},{20,16},{24,28},{28,24},{1,5},{5... | collective-permute-start | bytes 393224 | tf_op jit(solution)/shard_map/ppermute | solution.py:457
  57.8 6.3 %collective-permute-start.19 = (bf16[256,256]{1,0:T(8,128)(2,1)S(1)}, bf16[256,256]{1,0:T(8,128)(2,1)S(1)}, u32[]{:S(2)}, u32[]{:S(2)}) collective-permute-start(bf16[256,256]{1,0:T(8,128)(2,1)S(1)} %get-tuple-element.63.refs_0_.refs_8_), channel_id=1, source_target_pairs={{0,8},{4,12},{8,0},{12,4},{16,24},{20,28},{24,16},{28,20},{1,9},{5... | collective-permute-start | bytes 393224 | tf_op jit(solution)/shard_map/ppermute | solution.py:457
  59.8 6.3 %collective-permute-start.18 = (bf16[256,256]{1,0:T(8,128)(2,1)S(1)}, bf16[256,256]{1,0:T(8,128)(2,1)S(1)}, u32[]{:S(2)}, u32[]{:S(2)}) collective-permute-start(bf16[256,256]{1,0:T(8,128)(2,1)S(1)} %collective-permute-done.16.refs_9_), channel_id=1, source_target_pairs={{0,4},{4,0},{8,12},{12,8},{16,20},{20,16},{24,28},{28,24},{1,5},{5... | collective-permute-start | bytes 393224 | tf_op jit(solution)/shard_map/ppermute | solution.py:457
  60.8 6.2 %collective-permute-start.29 = (bf16[256,256]{1,0:T(8,128)(2,1)S(1)}, bf16[256,256]{1,0:T(8,128)(2,1)S(1)}, u32[]{:S(2)}, u32[]{:S(2)}) collective-permute-start(bf16[256,256]{1,0:T(8,128)(2,1)S(1)} %collective-permute-done.9.refs_4_.refs_8_), channel_id=1, source_target_pairs={{0,8},{4,12},{8,0},{12,4},{16,24},{20,28},{24,16},{28,20},{1,9},{5... | collective-permute-start | bytes 393224 | tf_op jit(solution)/shard_map/ppermute | solution.py:457
  65.0 6.3 %collective-permute-start.26 = (bf16[256,256]{1,0:T(8,128)(2,1)S(1)}, bf16[256,256]{1,0:T(8,128)(2,1)S(1)}, u32[]{:S(2)}, u32[]{:S(2)}) collective-permute-start(bf16[256,256]{1,0:T(8,128)(2,1)S(1)} %collective-permute-done.16.refs_9_), channel_id=1, source_target_pairs={{0,2},{1,3},{2,0},{3,1},{4,6},{5,7},{6,4},{7,5},{8,10},{9,11},{10,... | collective-permute-start | bytes 393224 | tf_op jit(solution)/shard_map/ppermute | solution.py:457
  66.1 6.5 %collective-permute-start.28 = (bf16[256,256]{1,0:T(8,128)(2,1)S(1)}, bf16[256,256]{1,0:T(8,128)(2,1)S(1)}, u32[]{:S(2)}, u32[]{:S(2)}) collective-permute-start(bf16[256,256]{1,0:T(8,128)(2,1)S(1)} %collective-permute-done.18.refs_11_), channel_id=1, source_target_pairs={{0,2},{1,3},{2,0},{3,1},{4,6},{5,7},{6,4},{7,5},{8,10},{9,11},{10,... | collective-permute-start | bytes 393224 | tf_op jit(solution)/shard_map/ppermute | solution.py:457
  67.0 6.3 %collective-permute-start.21 = (bf16[256,256]{1,0:T(8,128)(2,1)S(1)}, bf16[256,256]{1,0:T(8,128)(2,1)S(1)}, u32[]{:S(2)}, u32[]{:S(2)}) collective-permute-start(bf16[256,256]{1,0:T(8,128)(2,1)S(1)} %collective-permute-done.19.refs_12_), channel_id=1, source_target_pairs={{0,4},{4,0},{8,12},{12,8},{16,20},{20,16},{24,28},{28,24},{1,5},{5... | collective-permute-start | bytes 393224 | tf_op jit(solution)/shard_map/ppermute | solution.py:457
  68.2 6.1 %collective-permute-start.22 = (bf16[256,256]{1,0:T(8,128)(2,1)S(1)}, bf16[256,256]{1,0:T(8,128)(2,1)S(1)}, u32[]{:S(2)}, u32[]{:S(2)}) collective-permute-start(bf16[256,256]{1,0:T(8,128)(2,1)S(1)} %collective-permute-done.20.refs_13_), channel_id=1, source_target_pairs={{0,4},{4,0},{8,12},{12,8},{16,20},{20,16},{24,28},{28,24},{1,5},{5... | collective-permute-start | bytes 393224 | tf_op jit(solution)/shard_map/ppermute | solution.py:457
  69.8 8.1 %collective-permute-start.31 = (bf16[256,256]{1,0:T(8,128)(2,1)S(1)}, bf16[256,256]{1,0:T(8,128)(2,1)S(1)}, u32[]{:S(2)}, u32[]{:S(2)}) collective-permute-start(bf16[256,256]{1,0:T(8,128)(2,1)S(1)} %collective-permute-done.29.refs_12_), channel_id=1, source_target_pairs={{0,4},{4,0},{8,12},{12,8},{16,20},{20,16},{24,28},{28,24},{1,5},{5... | collective-permute-start | bytes 393224 | tf_op jit(solution)/shard_map/ppermute | solution.py:457
  71.3 7.3 %collective-permute-start.30 = (bf16[256,256]{1,0:T(8,128)(2,1)S(1)}, bf16[256,256]{1,0:T(8,128)(2,1)S(1)}, u32[]{:S(2)}, u32[]{:S(2)}) collective-permute-start(bf16[256,256]{1,0:T(8,128)(2,1)S(1)} %collective-permute-done.26.refs_9_), channel_id=1, source_target_pairs={{0,8},{4,12},{8,0},{12,4},{16,24},{20,28},{24,16},{28,20},{1,9},{5... | collective-permute-start | bytes 393224 | tf_op jit(solution)/shard_map/ppermute | solution.py:457
  72.7 5.9 %collective-permute-start.32 = (bf16[256,256]{1,0:T(8,128)(2,1)S(1)}, bf16[256,256]{1,0:T(8,128)(2,1)S(1)}, u32[]{:S(2)}, u32[]{:S(2)}) collective-permute-start(bf16[256,256]{1,0:T(8,128)(2,1)S(1)} %collective-permute-done.28.refs_11_), channel_id=1, source_target_pairs={{0,8},{4,12},{8,0},{12,4},{16,24},{20,28},{24,16},{28,20},{1,9},{5... | collective-permute-start | bytes 393224 | tf_op jit(solution)/shard_map/ppermute | solution.py:457
  73.4 9.6 %collective-permute-start.7 = (bf16[256,256]{1,0:T(8,128)(2,1)S(1)}, bf16[256,256]{1,0:T(8,128)(2,1)S(1)}, u32[]{:S(2)}, u32[]{:S(2)}) collective-permute-start(bf16[256,256]{1,0:T(8,128)(2,1)S(1)} %get-tuple-element.63.refs_0_.refs_8_), channel_id=1, source_target_pairs={{0,1},{1,0},{2,3},{3,2},{4,5},{5,4},{6,7},{7,6},{8,9},{9,8},{10,11... | collective-permute-start | bytes 393224 | tf_op jit(solution)/shard_map/ppermute | solution.py:457
  74.3 8.9 %collective-permute-start.8 = (bf16[256,256]{1,0:T(8,128)(2,1)S(1)}, bf16[256,256]{1,0:T(8,128)(2,1)S(1)}, u32[]{:S(2)}, u32[]{:S(2)}) collective-permute-start(bf16[256,256]{1,0:T(8,128)(2,1)S(1)} %get-tuple-element.57.refs_1_), channel_id=1, source_target_pairs={{0,1},{1,0},{2,3},{3,2},{4,5},{5,4},{6,7},{7,6},{8,9},{9,8},{10,11... | collective-permute-start | bytes 393224 | tf_op jit(solution)/shard_map/ppermute | solution.py:457
  77.9 7.6 %collective-permute-start.11 = (bf16[256,256]{1,0:T(8,128)(2,1)S(1)}, bf16[256,256]{1,0:T(8,128)(2,1)S(1)}, u32[]{:S(2)}, u32[]{:S(2)}) collective-permute-start(bf16[256,256]{1,0:T(8,128)(2,1)S(1)} %collective-permute-done.9.refs_4_.refs_8_), channel_id=1, source_target_pairs={{0,1},{1,0},{2,3},{3,2},{4,5},{5,4},{6,7},{7,6},{8,9},{9,8},{10,11... | collective-permute-start | bytes 393224 | tf_op jit(solution)/shard_map/ppermute | solution.py:457
  78.5 7.2 %collective-permute-start.12 = (bf16[256,256]{1,0:T(8,128)(2,1)S(1)}, bf16[256,256]{1,0:T(8,128)(2,1)S(1)}, u32[]{:S(2)}, u32[]{:S(2)}) collective-permute-start(bf16[256,256]{1,0:T(8,128)(2,1)S(1)} %collective-permute-done.10.refs_5_), channel_id=1, source_target_pairs={{0,1},{1,0},{2,3},{3,2},{4,5},{5,4},{6,7},{7,6},{8,9},{9,8},{10,11... | collective-permute-start | bytes 393224 | tf_op jit(solution)/shard_map/ppermute | solution.py:457
  78.6 9.7 %collective-permute-start.23 = (bf16[256,256]{1,0:T(8,128)(2,1)S(1)}, bf16[256,256]{1,0:T(8,128)(2,1)S(1)}, u32[]{:S(2)}, u32[]{:S(2)}) collective-permute-start(bf16[256,256]{1,0:T(8,128)(2,1)S(1)} %get-tuple-element.65), channel_id=1, source_target_pairs={{0,16},{4,20},{8,24},{12,28},{16,0},{20,4},{24,8},{28,12},{1,17},{... | collective-permute-start | bytes 393224 | tf_op jit(solution)/shard_map/ppermute | solution.py:457
  83.0 14.6 %collective-permute-start.24 = (f32[256,256]{1,0:T(8,128)S(1)}, f32[256,256]{1,0:T(8,128)S(1)}, u32[]{:S(2)}, u32[]{:S(2)}) collective-permute-start(f32[256,256]{1,0:T(8,128)S(1)} %get-tuple-element.66), channel_id=1, source_target_pairs={{0,1},{1,0},{2,3},{3,2},{4,5},{5,4},{6,7},{7,6},{8,9},{9,8},{10,11... | collective-permute-start | bytes 786440 | tf_op jit(solution)/shard_map/ppermute | solution.py:457
  83.2 22.8 %collective-permute-start.34 = (f32[256,256]{1,0:T(8,128)S(1)}, f32[256,256]{1,0:T(8,128)S(1)}, u32[]{:S(2)}, u32[]{:S(2)}) collective-permute-start(f32[256,256]{1,0:T(8,128)S(1)} %get-tuple-element.70), channel_id=1, source_target_pairs={{0,1},{1,0},{2,3},{3,2},{4,5},{5,4},{6,7},{7,6},{8,9},{9,8},{10,11... | collective-permute-start | bytes 786440 | tf_op jit(solution)/shard_map/ppermute | solution.py:457
  85.6 12.0 %collective-permute-start.25 = (bf16[256,256]{1,0:T(8,128)(2,1)S(1)}, bf16[256,256]{1,0:T(8,128)(2,1)S(1)}, u32[]{:S(2)}, u32[]{:S(2)}) collective-permute-start(bf16[256,256]{1,0:T(8,128)(2,1)S(1)} %get-tuple-element.67), channel_id=1, source_target_pairs={{0,17},{1,16},{2,19},{3,18},{4,21},{5,20},{6,23},{7,22},{8,25},{9,... | collective-permute-start | bytes 393224 | tf_op jit(solution)/shard_map/ppermute | solution.py:457
  85.7 15.4 %collective-permute-start.33 = (bf16[256,256]{1,0:T(8,128)(2,1)S(1)}, bf16[256,256]{1,0:T(8,128)(2,1)S(1)}, u32[]{:S(2)}, u32[]{:S(2)}) collective-permute-start(bf16[256,256]{1,0:T(8,128)(2,1)S(1)} %get-tuple-element.69), channel_id=1, source_target_pairs={{0,16},{4,20},{8,24},{12,28},{16,0},{20,4},{24,8},{28,12},{1,17},{... | collective-permute-start | bytes 393224 | tf_op jit(solution)/shard_map/ppermute | solution.py:457
  88.3 17.7 %collective-permute-start.35 = (bf16[256,256]{1,0:T(8,128)(2,1)S(1)}, bf16[256,256]{1,0:T(8,128)(2,1)S(1)}, u32[]{:S(2)}, u32[]{:S(2)}) collective-permute-start(bf16[256,256]{1,0:T(8,128)(2,1)S(1)} %get-tuple-element.71), channel_id=1, source_target_pairs={{0,17},{1,16},{2,19},{3,18},{4,21},{5,20},{6,23},{7,22},{8,25},{9,... | collective-permute-start | bytes 393224 | tf_op jit(solution)/shard_map/ppermute | solution.py:457
  (15 other events, 60.9 us)

commit v6 on v5

--- a/solution.py
+++ b/solution.py
@@ -223,7 +223,7 @@
         functools.partial(slots_kernel, per),
         out_shape=tuple(jax.ShapeDtypeStruct(o, BF16) for o in outs),
         grid_spec=spec,
-        compiler_params=params(),
+        compiler_params=params(26),
         cost_estimate=cost(2 * rows * rows * feats, 5 << 20),
         name="slots",
     )(me, dest.reshape(1, samp), lengths.reshape(1, samp), offsets.reshape(1, samp), x)
@@ -256,7 +256,7 @@
         pack_kernel,
         out_shape=tuple(jax.ShapeDtypeStruct(o, BF16) for o in outs),
         grid_spec=spec,
-        compiler_params=params(),
+        compiler_params=params(16),
         cost_estimate=cost(2 * rows * rows * cols, 3 << 20),
         name="pack",
     )(me, mine, core, across, pick, meta)
@@ -321,7 +321,7 @@
         functools.partial(attention_kernel, lmax, learners, half),
         out_shape=tuple(jax.ShapeDtypeStruct(o, BF16) for o in outs),
         grid_spec=spec,
-        compiler_params=params(),
+        compiler_params=params(30),
         cost_estimate=cost(4 * rows * rows * cols, 4 << 20),
         name="attention",
     )(me, kv, queries, out_grad)
@@ -341,7 +341,7 @@
         grid=(1,),
         in_specs=[whole((half, rows))] * 2 + [whole((half, cols))] * 2,
         out_specs=whole((rows, cols)),
-        compiler_params=params(),
+        compiler_params=params(16),
         cost_estimate=cost(4 * half * rows * cols, 3 << 20),
         name="packed_rows",
     )(*place, *outs)
@@ -382,7 +382,7 @@
         rows_kernel,
         out_shape=jax.ShapeDtypeStruct((rows, feats), BF16),
         grid_spec=spec,
-        compiler_params=params(),
+        compiler_params=params(26),
         cost_estimate=cost(4 * rows * feats * cols, 8 << 20),
         name="row_grads",
     )(me, *place, *parts, w_key, w_value)
@@ -418,7 +418,7 @@
         in_specs=[pl.BlockSpec((1, rows, part), lambda i: (half, 0, 0))] * len(xs)
         + [whole(g.shape) for g in pieces],
         out_specs=(whole(out),) * 2,
-        compiler_params=params(),
+        compiler_params=params(20),
         cost_estimate=cost(4 * len(xs) * rows * part * HEAD_DIM, 6 << 20),
         name="weight_grads",
     )(*xs, *pieces)
@@ -446,7 +446,7 @@
         functools.partial(finish_kernel, float(learners)),
         out_shape=(jax.ShapeDtypeStruct(out, F32),) * 2,
         grid_spec=spec,
-        compiler_params=params(),
+        compiler_params=params(12),
         cost_estimate=cost(part * cols, 2 << 20),
         name="finish",
     )(me, *sums)

time: 108 us -> 108 us (level)
  no operation moved by 1% of the time
where the time goes in v6:
time: 108 us; the launch traced here: 107 us
  starting transfers between devices  36.2 us (34%)
  waiting for transfers between devices  33 us (31%)
  Pallas kernels  32.5 us (30%)
  local copies, waits for them, and re-layouts  3.52 us (3%)
  other arithmetic  1.11 us (1%)
    ppermute x36, starting transfers between devices, swap(): return lax.ppermute(x, axis, [(i, i ^ code) for i in range(size)])  31.3 us
    ppermute x36, waiting for transfers between devices, swap(): return lax.ppermute(x, axis, [(i, i ^ code) for i in range(size)])  28.7 us
    pallas_call x2, Pallas kernels, project(): pl.pallas_call(project_kernel, out_shape=(jax.ShapeDtypeStruct(out, F32),...  8.37 us
    pallas_call x4, Pallas kernels, weight_grads(): pl.pallas_call(kernel, out_shape=(jax.ShapeDtypeStruct(out, dtype),) * 2,...  7.31 us
    pallas_call x2, Pallas kernels, attention(): pl.pallas_call(functools.partial(attention_kernel, lmax, learners, half),...  5.78 us
    all_to_all x1, starting transfers between devices, local(): kv = lax.all_to_all(kv[0], 'dp', split_axis=0, concat_axis=0, tiled=True)  4.88 us
    pallas_call x1, Pallas kernels, row_grads(): pl.pallas_call(rows_kernel, out_shape=jax.ShapeDtypeStruct((rows, feats),...  4.78 us
    all_to_all x1, waiting for transfers between devices, local(): kv = lax.all_to_all(kv[0], 'dp', split_axis=0, concat_axis=0, tiled=True)  4.27 us
  transfers between devices with their start and end apart: 37, of which 13 were waited for; matrix products, arithmetic and copies ran while one was open for 0% of the time, Pallas kernels for 25%

profile of v6, /device:TPU:0, one launch (start us, length us, event | category | flops | bytes accessed | tf_op | source)
XLA Modules:
  0.0 107.1 jit_solution(12085417365792053044)
XLA Ops:
  0.7 4.3 %project.2 = (f32[512,256]{1,0:T(8,128)}, f32[512,256]{1,0:T(8,128)}) custom-call(s32[1]{0:T(128)} %bitcast.1.me_ref, bf16[512,2048]{1,0:T(8,128)(2,1)} %bitcast.6, bf16[2048,512]{1,0:T(8,128)(2,1)} %refs_8_.1, bf16[2048,512]{1,0:T(8,128)(2,1)} %refs_9_.1), custom_call_target="tpu_custom_call" | custom-call | tf_op jit(solution)/shard_map/project/pallas_call | solution.py:167
  5.4 2.4 %slots.1 = (bf16[2,512,256]{2,1,0:T(8,128)(2,1)S(1)}, bf16[2,512,256]{2,1,0:T(8,128)(2,1)S(1)}, bf16[2,512,256]{2,1,0:T(8,128)(2,1)S(1)}, bf16[2,512,256]{2,1,0:...) custom-call(s32[1]{0:T(128)} %bitcast.me_ref, s32[1,32]{1,0:T(1,128)S(1)} %bitcast.9, ...), custom_call_target="tpu_custom_call" | custom-call | tf_op jit(solution)/shard_map/slots/pallas_call | solution.py:222
  9.0 3.0 %collective-permute-start.5 = (bf16[2,512,256]{2,1,0:T(8,128)(2,1)S(1)}, bf16[2,512,256]{2,1,0:T(8,128)(2,1)S(1)}, u32[]{:S(2)}, u32[]{:S(2)}) collective-permute-start(bf16[2,512,256]{2,1,0:T(8,128)(2,1)S(1)} %get-tuple-element.54), channel_id=1, source_target_pairs={{0,8},{4,12},{8,0},{12,4},{16,24},{20,28},{24,16},{28,20},{1,9},{5... | collective-permute-start | bytes 1572872 | tf_op jit(solution)/shard_map/ppermute | solution.py:457
  12.0 1.5 %collective-permute-start.4 = (bf16[2,512,256]{2,1,0:T(8,128)(2,1)S(1)}, bf16[2,512,256]{2,1,0:T(8,128)(2,1)S(1)}, u32[]{:S(2)}, u32[]{:S(2)}) collective-permute-start(bf16[2,512,256]{2,1,0:T(8,128)(2,1)S(1)} %get-tuple-element.52), channel_id=1, source_target_pairs={{0,4},{4,0},{8,12},{12,8},{16,20},{20,16},{24,28},{28,24},{1,5},{5... | collective-permute-start | bytes 1572872 | tf_op jit(solution)/shard_map/ppermute | solution.py:457
  13.6 1.5 %collective-permute-start.3 = (f32[512,256]{1,0:T(8,128)S(1)}, f32[512,256]{1,0:T(8,128)S(1)}, u32[]{:S(2)}, u32[]{:S(2)}) collective-permute-start(f32[512,256]{1,0:T(8,128)S(1)} %add.3), channel_id=1, source_target_pairs={{0,2},{1,3},{2,0},{3,1},{4,6},{5,7},{6,4},{7,5},{8,10},{9,11},{10,... | collective-permute-start | bytes 1572872 | tf_op jit(solution)/shard_map/ppermute | solution.py:457
  15.1 4.1 %project.3 = (f32[512,256]{1,0:T(8,128)}, f32[512,256]{1,0:T(8,128)}) custom-call(s32[1]{0:T(128)} %bitcast.1.me_ref, bf16[512,2048]{1,0:T(8,128)(2,1)} %bitcast.7, bf16[2048,512]{1,0:T(8,128)(2,1)} %refs_8_.1, bf16[2048,512]{1,0:T(8,128)(2,1)} %refs_9_.1), custom_call_target="tpu_custom_call" | custom-call | tf_op jit(solution)/shard_map/project/pallas_call | solution.py:167
  19.2 5.0 %collective-permute-done.5.refs_2_ = bf16[2,512,256]{2,1,0:T(8,128)(2,1)S(1)} collective-permute-done((bf16[2,512,256]{2,1,0:T(8,128)(2,1)S(1)}, bf16[2,512,256]{2,1,0:T(8,128)(2,1)S(1)}, u32[]{:S(2)}, u32[]{:S(2)}) %collective-permute-start.5) | collective-permute-done | bytes 524320 | tf_op jit(solution)/shard_map/ppermute | solution.py:457
  24.2 1.5 %collective-permute-done.4.refs_1_ = bf16[2,512,256]{2,1,0:T(8,128)(2,1)S(1)} collective-permute-done((bf16[2,512,256]{2,1,0:T(8,128)(2,1)S(1)}, bf16[2,512,256]{2,1,0:T(8,128)(2,1)S(1)}, u32[]{:S(2)}, u32[]{:S(2)}) %collective-permute-start.4) | collective-permute-done | bytes 524320 | tf_op jit(solution)/shard_map/ppermute | solution.py:457
  25.7 1.4 %collective-permute-start.6 = (bf16[2,512,256]{2,1,0:T(8,128)(2,1)}, bf16[2,512,256]{2,1,0:T(8,128)(2,1)S(1)}, u32[]{:S(2)}, u32[]{:S(2)}) collective-permute-start(bf16[2,512,256]{2,1,0:T(8,128)(2,1)} %get-tuple-element.55), channel_id=1, source_target_pairs={{0,12},{4,8},{8,4},{12,0},{16,28},{20,24},{24,20},{28,16},{1,13},{... | collective-permute-start | bytes 1572872 | tf_op jit(solution)/shard_map/ppermute | solution.py:457
  29.2 4.9 %all-to-all-start = ((bf16[8,80,256]{2,1,0:T(8,128)(2,1)}), bf16[8,80,256]{2,1,0:T(8,128)(2,1)S(1)}, u32[]{:S(2)}, u32[]{:S(2)}) async-start(bf16[8,80,256]{2,1,0:T(8,128)(2,1)} %pack.1), calls=%async_computation | async-start | bytes 655360 | tf_op jit(solution)/shard_map/all_to_all | solution.py:483
  34.6 8.0 %collective-permute-done.6.refs_3_ = bf16[2,512,256]{2,1,0:T(8,128)(2,1)S(1)} collective-permute-done((bf16[2,512,256]{2,1,0:T(8,128)(2,1)}, bf16[2,512,256]{2,1,0:T(8,128)(2,1)S(1)}, u32[]{:S(2)}, u32[]{:S(2)}) %collective-permute-start.6) | collective-permute-done | bytes 524320 | tf_op jit(solution)/shard_map/ppermute | solution.py:457
  42.6 4.3 %all-to-all-done.kv_ref = bf16[8,80,256]{2,1,0:T(8,128)(2,1)S(1)} async-done(((bf16[8,80,256]{2,1,0:T(8,128)(2,1)}), bf16[8,80,256]{2,1,0:T(8,128)(2,1)S(1)}, u32[]{:S(2)}, u32[]{:S(2)}) %all-to-all-start) | async-done | bytes 327712 | tf_op jit(solution)/shard_map/all_to_all | solution.py:483
  46.9 1.2 %copy-done.3 = bf16[512,1024]{1,0:T(8,128)(2,1)S(1)} copy-done((bf16[512,1024]{1,0:T(8,128)(2,1)S(1)}, bf16[512,1024]{1,0:T(8,128)(2,1)}, u32[]{:S(2)}) %copy-start.3) | copy-done | bytes 1048600
  48.1 1.2 %copy-done.4 = bf16[512,1024]{1,0:T(8,128)(2,1)S(1)} copy-done((bf16[512,1024]{1,0:T(8,128)(2,1)S(1)}, bf16[512,1024]{1,0:T(8,128)(2,1)}, u32[]{:S(2)}) %copy-start.4) | copy-done | bytes 1048600
  49.4 2.9 %attention.2 = (bf16[256,256]{1,0:T(8,128)(2,1)S(1)}, bf16[256,1024]{1,0:T(8,128)(2,1)S(1)}, bf16[256,512]{1,0:T(8,128)(2,1)S(1)}) custom-call(s32[1]{0:T(128)} %bitcast.me_ref, bf16[8,80,256]{2,1,0:T(8,128)(2,1)S(1)} %all-to-all-done.kv_ref, bf16[512,1024]{1,0:T(8,128)(2,1)S(1)} %copy-done.3, bf16[512,1024]{1,0:T(8,128)(2,1)S(1)} %copy-done.4), custom_call_target="tpu_custom_call" | custom-call | tf_op jit(solution)/shard_map/attention/pallas_call | solution.py:320
  52.4 2.9 %attention.3 = (bf16[256,256]{1,0:T(8,128)(2,1)S(1)}, bf16[256,1024]{1,0:T(8,128)(2,1)S(1)}, bf16[256,512]{1,0:T(8,128)(2,1)S(1)}) custom-call(s32[1]{0:T(128)} %bitcast.me_ref, bf16[8,80,256]{2,1,0:T(8,128)(2,1)S(1)} %all-to-all-done.kv_ref, bf16[512,1024]{1,0:T(8,128)(2,1)S(1)} %copy-done.3, bf16[512,1024]{1,0:T(8,128)(2,1)S(1)} %copy-done.4), custom_call_target="tpu_custom_call" | custom-call | tf_op jit(solution)/shard_map/attention/pallas_call | solution.py:320
  55.3 1.6 %collective-permute-start.9 = (bf16[256,256]{1,0:T(8,128)(2,1)S(1)}, bf16[256,256]{1,0:T(8,128)(2,1)S(1)}, u32[]{:S(2)}, u32[]{:S(2)}) collective-permute-start(bf16[256,256]{1,0:T(8,128)(2,1)S(1)} %get-tuple-element.63.refs_0_.refs_8_), channel_id=1, source_target_pairs={{0,2},{1,3},{2,0},{3,1},{4,6},{5,7},{6,4},{7,5},{8,10},{9,11},{10,... | collective-permute-start | bytes 393224 | tf_op jit(solution)/shard_map/ppermute | solution.py:457
  57.8 1.5 %collective-permute-start.19 = (bf16[256,256]{1,0:T(8,128)(2,1)S(1)}, bf16[256,256]{1,0:T(8,128)(2,1)S(1)}, u32[]{:S(2)}, u32[]{:S(2)}) collective-permute-start(bf16[256,256]{1,0:T(8,128)(2,1)S(1)} %get-tuple-element.63.refs_0_.refs_8_), channel_id=1, source_target_pairs={{0,8},{4,12},{8,0},{12,4},{16,24},{20,28},{24,16},{28,20},{1,9},{5... | collective-permute-start | bytes 393224 | tf_op jit(solution)/shard_map/ppermute | solution.py:457
  60.8 1.9 %collective-permute-start.29 = (bf16[256,256]{1,0:T(8,128)(2,1)S(1)}, bf16[256,256]{1,0:T(8,128)(2,1)S(1)}, u32[]{:S(2)}, u32[]{:S(2)}) collective-permute-start(bf16[256,256]{1,0:T(8,128)(2,1)S(1)} %collective-permute-done.9.refs_4_.refs_8_), channel_id=1, source_target_pairs={{0,8},{4,12},{8,0},{12,4},{16,24},{20,28},{24,16},{28,20},{1,9},{5... | collective-permute-start | bytes 393224 | tf_op jit(solution)/shard_map/ppermute | solution.py:457
  67.0 1.2 %collective-permute-start.21 = (bf16[256,256]{1,0:T(8,128)(2,1)S(1)}, bf16[256,256]{1,0:T(8,128)(2,1)S(1)}, u32[]{:S(2)}, u32[]{:S(2)}) collective-permute-start(bf16[256,256]{1,0:T(8,128)(2,1)S(1)} %collective-permute-done.19.refs_12_), channel_id=1, source_target_pairs={{0,4},{4,0},{8,12},{12,8},{16,20},{20,16},{24,28},{28,24},{1,5},{5... | collective-permute-start | bytes 393224 | tf_op jit(solution)/shard_map/ppermute | solution.py:457
  68.2 1.3 %collective-permute-start.22 = (bf16[256,256]{1,0:T(8,128)(2,1)S(1)}, bf16[256,256]{1,0:T(8,128)(2,1)S(1)}, u32[]{:S(2)}, u32[]{:S(2)}) collective-permute-start(bf16[256,256]{1,0:T(8,128)(2,1)S(1)} %collective-permute-done.20.refs_13_), channel_id=1, source_target_pairs={{0,4},{4,0},{8,12},{12,8},{16,20},{20,16},{24,28},{28,24},{1,5},{5... | collective-permute-start | bytes 393224 | tf_op jit(solution)/shard_map/ppermute | solution.py:457
  74.3 1.8 %weight_grads.5 = (bf16[256,256]{1,0:T(8,128)(2,1)S(1)}, bf16[256,256]{1,0:T(8,128)(2,1)S(1)}) custom-call(bf16[2,512,256]{2,1,0:T(8,128)(2,1)S(1)} %get-tuple-element.45.refs_0_, bf16[2,512,256]{2,1,0:T(8,128)(2,1)S(1)} %collective-permute-done.4.refs_1_, bf16[2,512,256]{2,1,0:T(8,128)(2,1)S(1)} %collective-permute-done.5.refs_2_, ...), custom_call_target="tpu_custom_call" | custom-call | tf_op jit(solution)/shard_map/weight_grads/pallas_call | solution.py:414
  76.1 1.8 %weight_grads.4 = (f32[256,256]{1,0:T(8,128)S(1)}, f32[256,256]{1,0:T(8,128)S(1)}) custom-call(bf16[2,512,256]{2,1,0:T(8,128)(2,1)S(1)} %get-tuple-element.45.refs_0_, bf16[2,512,256]{2,1,0:T(8,128)(2,1)S(1)} %collective-permute-done.4.refs_1_, bf16[2,512,256]{2,1,0:T(8,128)(2,1)S(1)} %collective-permute-done.5.refs_2_, ...), custom_call_target="tpu_custom_call" | custom-call | tf_op jit(solution)/shard_map/weight_grads/pallas_call | solution.py:414
  78.6 2.6 %collective-permute-start.23 = (bf16[256,256]{1,0:T(8,128)(2,1)S(1)}, bf16[256,256]{1,0:T(8,128)(2,1)S(1)}, u32[]{:S(2)}, u32[]{:S(2)}) collective-permute-start(bf16[256,256]{1,0:T(8,128)(2,1)S(1)} %get-tuple-element.65), channel_id=1, source_target_pairs={{0,16},{4,20},{8,24},{12,28},{16,0},{20,4},{24,8},{28,12},{1,17},{... | collective-permute-start | bytes 393224 | tf_op jit(solution)/shard_map/ppermute | solution.py:457
  81.2 1.8 %weight_grads.6 = (f32[256,256]{1,0:T(8,128)S(1)}, f32[256,256]{1,0:T(8,128)S(1)}) custom-call(bf16[2,512,256]{2,1,0:T(8,128)(2,1)S(1)} %get-tuple-element.45.refs_0_, bf16[2,512,256]{2,1,0:T(8,128)(2,1)S(1)} %collective-permute-done.4.refs_1_, bf16[2,512,256]{2,1,0:T(8,128)(2,1)S(1)} %collective-permute-done.5.refs_2_, ...), custom_call_target="tpu_custom_call" | custom-call | tf_op jit(solution)/shard_map/weight_grads/pallas_call | solution.py:414
  83.6 1.9 %weight_grads.7 = (bf16[256,256]{1,0:T(8,128)(2,1)S(1)}, bf16[256,256]{1,0:T(8,128)(2,1)S(1)}) custom-call(bf16[2,512,256]{2,1,0:T(8,128)(2,1)S(1)} %get-tuple-element.45.refs_0_, bf16[2,512,256]{2,1,0:T(8,128)(2,1)S(1)} %collective-permute-done.4.refs_1_, bf16[2,512,256]{2,1,0:T(8,128)(2,1)S(1)} %collective-permute-done.5.refs_2_, ...), custom_call_target="tpu_custom_call" | custom-call | tf_op jit(solution)/shard_map/weight_grads/pallas_call | solution.py:414
  85.7 2.6 %collective-permute-start.33 = (bf16[256,256]{1,0:T(8,128)(2,1)S(1)}, bf16[256,256]{1,0:T(8,128)(2,1)S(1)}, u32[]{:S(2)}, u32[]{:S(2)}) collective-permute-start(bf16[256,256]{1,0:T(8,128)(2,1)S(1)} %get-tuple-element.69), channel_id=1, source_target_pairs={{0,16},{4,20},{8,24},{12,28},{16,0},{20,4},{24,8},{28,12},{1,17},{... | collective-permute-start | bytes 393224 | tf_op jit(solution)/shard_map/ppermute | solution.py:457
  88.4 1.7 %packed_rows.1 = bf16[512,1024]{1,0:T(8,128)(2,1)} custom-call(bf16[256,512]{1,0:T(8,128)(2,1)S(1)} %get-tuple-element.59.place0, bf16[256,512]{1,0:T(8,128)(2,1)S(1)} %get-tuple-element.60.place1, bf16[256,1024]{1,0:T(8,128)(2,1)S(1)} %get-tuple-element.61.out0, bf16[256,1024]{1,0:T(8,128)(2,1)S(1)} %get-tuple-element.62.out1), custom_call_target="tpu_custom_call" | custom-call | tf_op jit(solution)/shard_map/packed_rows/pallas_call | solution.py:338
  90.1 4.8 %row_grads.1 = bf16[512,2048]{1,0:T(8,128)(2,1)} custom-call(s32[1]{0:T(128)} %bitcast.1.me_ref, bf16[256,512]{1,0:T(8,128)(2,1)S(1)} %get-tuple-element.59.place0, bf16[256,512]{1,0:T(8,128)(2,1)S(1)} %get-tuple-element.60.place1, bf16[256,256]{1,0:T(8,128)(2,1)S(1)} %get-tuple-element.63.refs_0_.refs_8_, bf16[256,256]{1,0:T(8,128)(2,1)S(1)} %get-tuple-element.57.refs_1_, ...), custom_call_target="tpu_custom_call" | custom-call | tf_op jit(solution)/shard_map/row_grads/pallas_call | solution.py:381
  94.8 2.7 %collective-permute-done.25.refs_3_ = bf16[256,256]{1,0:T(8,128)(2,1)S(1)} collective-permute-done((bf16[256,256]{1,0:T(8,128)(2,1)S(1)}, bf16[256,256]{1,0:T(8,128)(2,1)S(1)}, u32[]{:S(2)}, u32[]{:S(2)}) %collective-permute-start.25) | collective-permute-done | bytes 131104 | tf_op jit(solution)/shard_map/ppermute | solution.py:457
  97.6 3.5 %collective-permute-done.33.refs_5_ = bf16[256,256]{1,0:T(8,128)(2,1)S(1)} collective-permute-done((bf16[256,256]{1,0:T(8,128)(2,1)S(1)}, bf16[256,256]{1,0:T(8,128)(2,1)S(1)}, u32[]{:S(2)}, u32[]{:S(2)}) %collective-permute-start.33) | collective-permute-done | bytes 131104 | tf_op jit(solution)/shard_map/ppermute | solution.py:457
  101.1 4.9 %collective-permute-done.35.refs_7_ = bf16[256,256]{1,0:T(8,128)(2,1)S(1)} collective-permute-done((bf16[256,256]{1,0:T(8,128)(2,1)S(1)}, bf16[256,256]{1,0:T(8,128)(2,1)S(1)}, u32[]{:S(2)}, u32[]{:S(2)}) %collective-permute-start.35) | collective-permute-done | bytes 131104 | tf_op jit(solution)/shard_map/ppermute | solution.py:457
  (76 shorter events, 18.7 us)
Async XLA Ops:
  8.9 6.2 %collective-permute-start.1 = (bf16[2,512,256]{2,1,0:T(8,128)(2,1)S(1)}, bf16[2,512,256]{2,1,0:T(8,128)(2,1)S(1)}, u32[]{:S(2)}, u32[]{:S(2)}) collective-permute-start(bf16[2,512,256]{2,1,0:T(8,128)(2,1)S(1)} %get-tuple-element.45.refs_0_), channel_id=1, source_target_pairs={{0,1},{1,0},{2,3},{3,2},{4,5},{5,4},{6,7},{7,6},{8,9},{9,8},{10,11... | collective-permute-start | bytes 1572872 | tf_op jit(solution)/shard_map/ppermute | solution.py:457
  9.0 15.2 %collective-permute-start.5 = (bf16[2,512,256]{2,1,0:T(8,128)(2,1)S(1)}, bf16[2,512,256]{2,1,0:T(8,128)(2,1)S(1)}, u32[]{:S(2)}, u32[]{:S(2)}) collective-permute-start(bf16[2,512,256]{2,1,0:T(8,128)(2,1)S(1)} %get-tuple-element.54), channel_id=1, source_target_pairs={{0,8},{4,12},{8,0},{12,4},{16,24},{20,28},{24,16},{28,20},{1,9},{5... | collective-permute-start | bytes 1572872 | tf_op jit(solution)/shard_map/ppermute | solution.py:457
  12.0 13.6 %collective-permute-start.4 = (bf16[2,512,256]{2,1,0:T(8,128)(2,1)S(1)}, bf16[2,512,256]{2,1,0:T(8,128)(2,1)S(1)}, u32[]{:S(2)}, u32[]{:S(2)}) collective-permute-start(bf16[2,512,256]{2,1,0:T(8,128)(2,1)S(1)} %get-tuple-element.52), channel_id=1, source_target_pairs={{0,4},{4,0},{8,12},{12,8},{16,20},{20,16},{24,28},{28,24},{1,5},{5... | collective-permute-start | bytes 1572872 | tf_op jit(solution)/shard_map/ppermute | solution.py:457
  13.6 13.5 %collective-permute-start.3 = (f32[512,256]{1,0:T(8,128)S(1)}, f32[512,256]{1,0:T(8,128)S(1)}, u32[]{:S(2)}, u32[]{:S(2)}) collective-permute-start(f32[512,256]{1,0:T(8,128)S(1)} %add.3), channel_id=1, source_target_pairs={{0,2},{1,3},{2,0},{3,1},{4,6},{5,7},{6,4},{7,5},{8,10},{9,11},{10,... | collective-permute-start | bytes 1572872 | tf_op jit(solution)/shard_map/ppermute | solution.py:457
  19.2 7.9 %collective-permute-start.2 = (f32[512,256]{1,0:T(8,128)}, f32[512,256]{1,0:T(8,128)S(1)}, u32[]{:S(2)}, u32[]{:S(2)}) collective-permute-start(f32[512,256]{1,0:T(8,128)} %get-tuple-element.48), channel_id=1, source_target_pairs={{0,1},{1,0},{2,3},{3,2},{4,5},{5,4},{6,7},{7,6},{8,9},{9,8},{10,11... | collective-permute-start | bytes 1572872 | tf_op jit(solution)/shard_map/ppermute | solution.py:457
  25.7 17.0 %collective-permute-start.6 = (bf16[2,512,256]{2,1,0:T(8,128)(2,1)}, bf16[2,512,256]{2,1,0:T(8,128)(2,1)S(1)}, u32[]{:S(2)}, u32[]{:S(2)}) collective-permute-start(bf16[2,512,256]{2,1,0:T(8,128)(2,1)} %get-tuple-element.55), channel_id=1, source_target_pairs={{0,12},{4,8},{8,4},{12,0},{16,28},{20,24},{24,20},{28,16},{1,13},{... | collective-permute-start | bytes 1572872 | tf_op jit(solution)/shard_map/ppermute | solution.py:457
  29.2 17.7 %all-to-all-start = ((bf16[8,80,256]{2,1,0:T(8,128)(2,1)}), bf16[8,80,256]{2,1,0:T(8,128)(2,1)S(1)}, u32[]{:S(2)}, u32[]{:S(2)}) async-start(bf16[8,80,256]{2,1,0:T(8,128)(2,1)} %pack.1), calls=%async_computation | async-start | bytes 655360 | tf_op jit(solution)/shard_map/all_to_all | solution.py:483
  34.1 22.8 %collective-permute-start.14 = (bf16[2,512,256]{2,1,0:T(8,128)(2,1)S(1)}, bf16[2,512,256]{2,1,0:T(8,128)(2,1)S(1)}, u32[]{:S(2)}, u32[]{:S(2)}) collective-permute-start(bf16[2,512,256]{2,1,0:T(8,128)(2,1)S(1)} %collective-permute-done.5.refs_2_), channel_id=1, source_target_pairs={{0,1},{1,0},{2,3},{3,2},{4,5},{5,4},{6,7},{7,6},{8,9},{9,8},{10,11... | collective-permute-start | bytes 1572872 | tf_op jit(solution)/shard_map/ppermute | solution.py:457
  34.1 23.7 %collective-permute-start.13 = (bf16[2,512,256]{2,1,0:T(8,128)(2,1)S(1)}, bf16[2,512,256]{2,1,0:T(8,128)(2,1)}, u32[]{:S(2)}, u32[]{:S(2)}) collective-permute-start(bf16[2,512,256]{2,1,0:T(8,128)(2,1)S(1)} %collective-permute-done.4.refs_1_), channel_id=1, source_target_pairs={{0,1},{1,0},{2,3},{3,2},{4,5},{5,4},{6,7},{7,6},{8,9},{9,8},{10,11... | collective-permute-start | bytes 1572872 | tf_op jit(solution)/shard_map/ppermute | solution.py:457
  42.6 16.6 %collective-permute-start.15 = (bf16[2,512,256]{2,1,0:T(8,128)(2,1)S(1)}, bf16[2,512,256]{2,1,0:T(8,128)(2,1)}, u32[]{:S(2)}, u32[]{:S(2)}) collective-permute-start(bf16[2,512,256]{2,1,0:T(8,128)(2,1)S(1)} %collective-permute-done.6.refs_3_), channel_id=1, source_target_pairs={{0,1},{1,0},{2,3},{3,2},{4,5},{5,4},{6,7},{7,6},{8,9},{9,8},{10,11... | collective-permute-start | bytes 1572872 | tf_op jit(solution)/shard_map/ppermute | solution.py:457
  52.2 7.5 %collective-permute-start.16 = (bf16[256,256]{1,0:T(8,128)(2,1)S(1)}, bf16[256,256]{1,0:T(8,128)(2,1)S(1)}, u32[]{:S(2)}, u32[]{:S(2)}) collective-permute-start(bf16[256,256]{1,0:T(8,128)(2,1)S(1)} %get-tuple-element.57.refs_1_), channel_id=1, source_target_pairs={{0,16},{4,20},{8,24},{12,28},{16,0},{20,4},{24,8},{28,12},{1,17},{... | collective-permute-start | bytes 393224 | tf_op jit(solution)/shard_map/ppermute | solution.py:457
  56.9 6.1 %collective-permute-start.17 = (bf16[256,256]{1,0:T(8,128)(2,1)S(1)}, bf16[256,256]{1,0:T(8,128)(2,1)S(1)}, u32[]{:S(2)}, u32[]{:S(2)}) collective-permute-start(bf16[256,256]{1,0:T(8,128)(2,1)S(1)} %get-tuple-element.63.refs_0_.refs_8_), channel_id=1, source_target_pairs={{0,4},{4,0},{8,12},{12,8},{16,20},{20,16},{24,28},{28,24},{1,5},{5... | collective-permute-start | bytes 393224 | tf_op jit(solution)/shard_map/ppermute | solution.py:457
  57.8 6.3 %collective-permute-start.19 = (bf16[256,256]{1,0:T(8,128)(2,1)S(1)}, bf16[256,256]{1,0:T(8,128)(2,1)S(1)}, u32[]{:S(2)}, u32[]{:S(2)}) collective-permute-start(bf16[256,256]{1,0:T(8,128)(2,1)S(1)} %get-tuple-element.63.refs_0_.refs_8_), channel_id=1, source_target_pairs={{0,8},{4,12},{8,0},{12,4},{16,24},{20,28},{24,16},{28,20},{1,9},{5... | collective-permute-start | bytes 393224 | tf_op jit(solution)/shard_map/ppermute | solution.py:457
  59.8 6.3 %collective-permute-start.18 = (bf16[256,256]{1,0:T(8,128)(2,1)S(1)}, bf16[256,256]{1,0:T(8,128)(2,1)S(1)}, u32[]{:S(2)}, u32[]{:S(2)}) collective-permute-start(bf16[256,256]{1,0:T(8,128)(2,1)S(1)} %collective-permute-done.16.refs_9_), channel_id=1, source_target_pairs={{0,4},{4,0},{8,12},{12,8},{16,20},{20,16},{24,28},{28,24},{1,5},{5... | collective-permute-start | bytes 393224 | tf_op jit(solution)/shard_map/ppermute | solution.py:457
  60.8 6.2 %collective-permute-start.29 = (bf16[256,256]{1,0:T(8,128)(2,1)S(1)}, bf16[256,256]{1,0:T(8,128)(2,1)S(1)}, u32[]{:S(2)}, u32[]{:S(2)}) collective-permute-start(bf16[256,256]{1,0:T(8,128)(2,1)S(1)} %collective-permute-done.9.refs_4_.refs_8_), channel_id=1, source_target_pairs={{0,8},{4,12},{8,0},{12,4},{16,24},{20,28},{24,16},{28,20},{1,9},{5... | collective-permute-start | bytes 393224 | tf_op jit(solution)/shard_map/ppermute | solution.py:457
  65.0 6.3 %collective-permute-start.26 = (bf16[256,256]{1,0:T(8,128)(2,1)S(1)}, bf16[256,256]{1,0:T(8,128)(2,1)S(1)}, u32[]{:S(2)}, u32[]{:S(2)}) collective-permute-start(bf16[256,256]{1,0:T(8,128)(2,1)S(1)} %collective-permute-done.16.refs_9_), channel_id=1, source_target_pairs={{0,2},{1,3},{2,0},{3,1},{4,6},{5,7},{6,4},{7,5},{8,10},{9,11},{10,... | collective-permute-start | bytes 393224 | tf_op jit(solution)/shard_map/ppermute | solution.py:457
  66.1 6.5 %collective-permute-start.28 = (bf16[256,256]{1,0:T(8,128)(2,1)S(1)}, bf16[256,256]{1,0:T(8,128)(2,1)S(1)}, u32[]{:S(2)}, u32[]{:S(2)}) collective-permute-start(bf16[256,256]{1,0:T(8,128)(2,1)S(1)} %collective-permute-done.18.refs_11_), channel_id=1, source_target_pairs={{0,2},{1,3},{2,0},{3,1},{4,6},{5,7},{6,4},{7,5},{8,10},{9,11},{10,... | collective-permute-start | bytes 393224 | tf_op jit(solution)/shard_map/ppermute | solution.py:457
  67.0 6.3 %collective-permute-start.21 = (bf16[256,256]{1,0:T(8,128)(2,1)S(1)}, bf16[256,256]{1,0:T(8,128)(2,1)S(1)}, u32[]{:S(2)}, u32[]{:S(2)}) collective-permute-start(bf16[256,256]{1,0:T(8,128)(2,1)S(1)} %collective-permute-done.19.refs_12_), channel_id=1, source_target_pairs={{0,4},{4,0},{8,12},{12,8},{16,20},{20,16},{24,28},{28,24},{1,5},{5... | collective-permute-start | bytes 393224 | tf_op jit(solution)/shard_map/ppermute | solution.py:457
  68.2 6.1 %collective-permute-start.22 = (bf16[256,256]{1,0:T(8,128)(2,1)S(1)}, bf16[256,256]{1,0:T(8,128)(2,1)S(1)}, u32[]{:S(2)}, u32[]{:S(2)}) collective-permute-start(bf16[256,256]{1,0:T(8,128)(2,1)S(1)} %collective-permute-done.20.refs_13_), channel_id=1, source_target_pairs={{0,4},{4,0},{8,12},{12,8},{16,20},{20,16},{24,28},{28,24},{1,5},{5... | collective-permute-start | bytes 393224 | tf_op jit(solution)/shard_map/ppermute | solution.py:457
  69.8 8.1 %collective-permute-start.31 = (bf16[256,256]{1,0:T(8,128)(2,1)S(1)}, bf16[256,256]{1,0:T(8,128)(2,1)S(1)}, u32[]{:S(2)}, u32[]{:S(2)}) collective-permute-start(bf16[256,256]{1,0:T(8,128)(2,1)S(1)} %collective-permute-done.29.refs_12_), channel_id=1, source_target_pairs={{0,4},{4,0},{8,12},{12,8},{16,20},{20,16},{24,28},{28,24},{1,5},{5... | collective-permute-start | bytes 393224 | tf_op jit(solution)/shard_map/ppermute | solution.py:457
  71.3 7.3 %collective-permute-start.30 = (bf16[256,256]{1,0:T(8,128)(2,1)S(1)}, bf16[256,256]{1,0:T(8,128)(2,1)S(1)}, u32[]{:S(2)}, u32[]{:S(2)}) collective-permute-start(bf16[256,256]{1,0:T(8,128)(2,1)S(1)} %collective-permute-done.26.refs_9_), channel_id=1, source_target_pairs={{0,8},{4,12},{8,0},{12,4},{16,24},{20,28},{24,16},{28,20},{1,9},{5... | collective-permute-start | bytes 393224 | tf_op jit(solution)/shard_map/ppermute | solution.py:457
  72.7 5.9 %collective-permute-start.32 = (bf16[256,256]{1,0:T(8,128)(2,1)S(1)}, bf16[256,256]{1,0:T(8,128)(2,1)S(1)}, u32[]{:S(2)}, u32[]{:S(2)}) collective-permute-start(bf16[256,256]{1,0:T(8,128)(2,1)S(1)} %collective-permute-done.28.refs_11_), channel_id=1, source_target_pairs={{0,8},{4,12},{8,0},{12,4},{16,24},{20,28},{24,16},{28,20},{1,9},{5... | collective-permute-start | bytes 393224 | tf_op jit(solution)/shard_map/ppermute | solution.py:457
  73.4 9.6 %collective-permute-start.7 = (bf16[256,256]{1,0:T(8,128)(2,1)S(1)}, bf16[256,256]{1,0:T(8,128)(2,1)S(1)}, u32[]{:S(2)}, u32[]{:S(2)}) collective-permute-start(bf16[256,256]{1,0:T(8,128)(2,1)S(1)} %get-tuple-element.63.refs_0_.refs_8_), channel_id=1, source_target_pairs={{0,1},{1,0},{2,3},{3,2},{4,5},{5,4},{6,7},{7,6},{8,9},{9,8},{10,11... | collective-permute-start | bytes 393224 | tf_op jit(solution)/shard_map/ppermute | solution.py:457
  74.3 8.9 %collective-permute-start.8 = (bf16[256,256]{1,0:T(8,128)(2,1)S(1)}, bf16[256,256]{1,0:T(8,128)(2,1)S(1)}, u32[]{:S(2)}, u32[]{:S(2)}) collective-permute-start(bf16[256,256]{1,0:T(8,128)(2,1)S(1)} %get-tuple-element.57.refs_1_), channel_id=1, source_target_pairs={{0,1},{1,0},{2,3},{3,2},{4,5},{5,4},{6,7},{7,6},{8,9},{9,8},{10,11... | collective-permute-start | bytes 393224 | tf_op jit(solution)/shard_map/ppermute | solution.py:457
  77.9 7.6 %collective-permute-start.11 = (bf16[256,256]{1,0:T(8,128)(2,1)S(1)}, bf16[256,256]{1,0:T(8,128)(2,1)S(1)}, u32[]{:S(2)}, u32[]{:S(2)}) collective-permute-start(bf16[256,256]{1,0:T(8,128)(2,1)S(1)} %collective-permute-done.9.refs_4_.refs_8_), channel_id=1, source_target_pairs={{0,1},{1,0},{2,3},{3,2},{4,5},{5,4},{6,7},{7,6},{8,9},{9,8},{10,11... | collective-permute-start | bytes 393224 | tf_op jit(solution)/shard_map/ppermute | solution.py:457
  78.5 7.2 %collective-permute-start.12 = (bf16[256,256]{1,0:T(8,128)(2,1)S(1)}, bf16[256,256]{1,0:T(8,128)(2,1)S(1)}, u32[]{:S(2)}, u32[]{:S(2)}) collective-permute-start(bf16[256,256]{1,0:T(8,128)(2,1)S(1)} %collective-permute-done.10.refs_5_), channel_id=1, source_target_pairs={{0,1},{1,0},{2,3},{3,2},{4,5},{5,4},{6,7},{7,6},{8,9},{9,8},{10,11... | collective-permute-start | bytes 393224 | tf_op jit(solution)/shard_map/ppermute | solution.py:457
  78.6 9.7 %collective-permute-start.23 = (bf16[256,256]{1,0:T(8,128)(2,1)S(1)}, bf16[256,256]{1,0:T(8,128)(2,1)S(1)}, u32[]{:S(2)}, u32[]{:S(2)}) collective-permute-start(bf16[256,256]{1,0:T(8,128)(2,1)S(1)} %get-tuple-element.65), channel_id=1, source_target_pairs={{0,16},{4,20},{8,24},{12,28},{16,0},{20,4},{24,8},{28,12},{1,17},{... | collective-permute-start | bytes 393224 | tf_op jit(solution)/shard_map/ppermute | solution.py:457
  83.0 14.6 %collective-permute-start.24 = (f32[256,256]{1,0:T(8,128)S(1)}, f32[256,256]{1,0:T(8,128)S(1)}, u32[]{:S(2)}, u32[]{:S(2)}) collective-permute-start(f32[256,256]{1,0:T(8,128)S(1)} %get-tuple-element.66), channel_id=1, source_target_pairs={{0,1},{1,0},{2,3},{3,2},{4,5},{5,4},{6,7},{7,6},{8,9},{9,8},{10,11... | collective-permute-start | bytes 786440 | tf_op jit(solution)/shard_map/ppermute | solution.py:457
  83.2 22.8 %collective-permute-start.34 = (f32[256,256]{1,0:T(8,128)S(1)}, f32[256,256]{1,0:T(8,128)S(1)}, u32[]{:S(2)}, u32[]{:S(2)}) collective-permute-start(f32[256,256]{1,0:T(8,128)S(1)} %get-tuple-element.70), channel_id=1, source_target_pairs={{0,1},{1,0},{2,3},{3,2},{4,5},{5,4},{6,7},{7,6},{8,9},{9,8},{10,11... | collective-permute-start | bytes 786440 | tf_op jit(solution)/shard_map/ppermute | solution.py:457
  85.5 12.0 %collective-permute-start.25 = (bf16[256,256]{1,0:T(8,128)(2,1)S(1)}, bf16[256,256]{1,0:T(8,128)(2,1)S(1)}, u32[]{:S(2)}, u32[]{:S(2)}) collective-permute-start(bf16[256,256]{1,0:T(8,128)(2,1)S(1)} %get-tuple-element.67), channel_id=1, source_target_pairs={{0,17},{1,16},{2,19},{3,18},{4,21},{5,20},{6,23},{7,22},{8,25},{9,... | collective-permute-start | bytes 393224 | tf_op jit(solution)/shard_map/ppermute | solution.py:457
  85.7 15.4 %collective-permute-start.33 = (bf16[256,256]{1,0:T(8,128)(2,1)S(1)}, bf16[256,256]{1,0:T(8,128)(2,1)S(1)}, u32[]{:S(2)}, u32[]{:S(2)}) collective-permute-start(bf16[256,256]{1,0:T(8,128)(2,1)S(1)} %get-tuple-element.69), channel_id=1, source_target_pairs={{0,16},{4,20},{8,24},{12,28},{16,0},{20,4},{24,8},{28,12},{1,17},{... | collective-permute-start | bytes 393224 | tf_op jit(solution)/shard_map/ppermute | solution.py:457
  88.3 17.7 %collective-permute-start.35 = (bf16[256,256]{1,0:T(8,128)(2,1)S(1)}, bf16[256,256]{1,0:T(8,128)(2,1)S(1)}, u32[]{:S(2)}, u32[]{:S(2)}) collective-permute-start(bf16[256,256]{1,0:T(8,128)(2,1)S(1)} %get-tuple-element.71), channel_id=1, source_target_pairs={{0,17},{1,16},{2,19},{3,18},{4,21},{5,20},{6,23},{7,22},{8,25},{9,... | collective-permute-start | bytes 393224 | tf_op jit(solution)/shard_map/ppermute | solution.py:457
  (15 other events, 60.9 us)
